TPU v7x, 256 devices: a whole 4x4x8 slice. The times are simulated.
256 devices in a mesh: row: 32 (over z, x), col: 8 (over y, core).
Axes of the slice: x: 4, y: 4, z: 8, core: 2. Of those that a mesh axis runs over, the one named last changes fastest.
Arguments:
- node_features: bfloat16 [65536, 768], P(('row', 'col')), may hold values from -6 to 6
- neighbour_count: int32 [65536], P(('row', 'col')), may hold values from 1 to 64
- tile_rows: int32 [32, 8, 128], P('row', 'col'), may hold values from 0 to 15
- tile_cols: int32 [32, 8, 128], P('row', 'col'), may hold values from 0 to 63
- tile_count: int32 [32, 8], P('row', 'col'), may hold values from 32 to 128, as said below
- patterns: int32 [32, 8, 128, 128, 128], P('row', 'col'), may hold values 0 or 1
- w_self: float32 [768, 256], replicated, may hold values from -0.21875 to 0.21875
- w_neigh: float32 [768, 256], replicated, may hold values from -0.21875 to 0.21875
- bias: float32 [256], replicated, may hold values from -3 to 3
Outputs:
- out: float32 [65536, 256], P(('row', 'col'))
Inputs may be any that keep to these rules, and one draw needn't show every extreme that they name: `tile_count`: number of slots of a cell that are used; slots at or beyond it are ignored.
All inputs are finite; a program needn't handle non-finite values. No bound on the sum of `patterns` on one device may be relied on, other than what follows from the above.
Results may differ from a plain program's by a relative error of at most 0.0003.
Values may be sent and summed in bfloat16 or wider, within the bound.
No kernel may reach another device: no remote copies, remote signals or barrier semaphores. Data moves between devices by JAX's collectives and lax.ppermute only.
A program may use at most 128 MiB of HBM per device.

v0:
```python
import jax
import jax.numpy as jnp
from jax import lax
from jax.sharding import PartitionSpec as P


def tile_products(pattern_block, picked):
    zero_one = pattern_block.astype(picked.dtype)
    return jnp.einsum("sij,sjw->siw", zero_one, picked, preferred_element_type=jnp.float32)


def aggregate(columns, rows_slots, cols_slots, filled, pattern, row_tiles):
    tile_size = pattern.shape[-1]
    feature_width = columns.shape[1]
    col_tiles = columns.reshape(-1, tile_size, feature_width)
    slot_total = rows_slots.shape[0]
    group_size = min(16, slot_total)

    def add_group(group_index, running):
        first_slot = group_index * group_size
        picked_rows = lax.dynamic_slice_in_dim(rows_slots, first_slot, group_size)
        picked_cols = lax.dynamic_slice_in_dim(cols_slots, first_slot, group_size)
        pattern_block = lax.dynamic_slice_in_dim(pattern, first_slot, group_size, 0)
        live_slot = first_slot + jnp.arange(group_size, dtype=jnp.int32) < filled
        pattern_block = jnp.where(live_slot[:, None, None], pattern_block, 0)
        picked = jnp.take(col_tiles, picked_cols, axis=0)
        product = tile_products(pattern_block, picked)
        for slot in range(group_size):
            target = picked_rows[slot]
            current = lax.dynamic_slice_in_dim(running, target, 1, 0)
            running = lax.dynamic_update_slice_in_dim(
                running, current + product[slot][None], target, 0
            )
        return running

    groups = (filled + group_size - 1) // group_size
    running = lax.fori_loop(
        0, groups, add_group, jnp.zeros((row_tiles, tile_size, feature_width), jnp.float32)
    )
    return running.reshape(row_tiles * tile_size, feature_width)


def body(
    node_features,
    neighbour_count,
    tile_rows,
    tile_cols,
    tile_count,
    patterns,
    w_self,
    w_neigh,
    bias,
):
    precise = lax.Precision.HIGHEST
    span_rows = node_features.shape[0]
    tile_size = patterns.shape[-1]
    row_tiles = lax.axis_size("col") * span_rows // tile_size
    features = node_features.astype(jnp.float32)
    columns = lax.all_gather(node_features, "row", axis=0, tiled=True)
    partial_terms = aggregate(
        columns, tile_rows[0, 0], tile_cols[0, 0], tile_count[0, 0], patterns[0, 0], row_tiles
    )
    summed = lax.psum_scatter(partial_terms, "col", scatter_dimension=0, tiled=True)
    divisor = neighbour_count.astype(jnp.float32)[:, None]
    neighbour_part = jnp.dot(summed / divisor, w_neigh, precision=precise)
    own_part = jnp.dot(features, w_self, precision=precise)
    return jax.nn.relu(own_part + neighbour_part + bias)


def solution(mesh):
    return jax.shard_map(
        body,
        mesh=mesh,
        in_specs=(
            P(("row", "col"), None),
            P(("row", "col")),
            P("row", "col", None),
            P("row", "col", None),
            P("row", "col"),
            P("row", "col", None, None, None),
            P(),
            P(),
            P(),
        ),
        out_specs=P(("row", "col"), None),
        check_vma=False,
    )
```

profile of v0, /device:TPU:32, one launch (start us, length us, event | category | flops | bytes accessed | tf_op | source)
XLA Modules:
  0.0 784.4 jit_solution(15723813677374994002)
XLA Ops:
  8.0 122.5 %all-gather.2.cloned.1.call-done = bf16[8192,768]{1,0:T(8,128)(2,1)} async-done(((bf16[256,768]{1,0:T(8,128)(2,1)}), bf16[8192,768]{1,0:T(8,128)(2,1)}) %all-gather.2.cloned.1.call-update) | async-done | bytes 12582928 | tf_op jit(solution)/shard_map/all_gather | solution.py:59
  130.5 3.3 broadcast_in_dim.30
  133.7 223.9 %while.10 = (s32[]{:T(128)}, f32[16,128,768]{2,1,0:T(8,128)}, s32[]{:T(128)}, s32[128]{0:T(128)S(1)}, s32[]{:T(128)}, /*index=5*/s32[128,128,128]{2,1,0:T(8,128)...) while((s32[]{:T(128)}, f32[16,128,768]{2,1,0:T(8,128)}, ...), condition=%wide.region_1.2_spmd, body=%wide.region_0.1_spmd.sunk | while | flops 406324352 | bytes 35657016 | solution.py:37
  133.7 0.7 compare_and_fusion.2
  134.5 7.0 gather_fusion
  141.5 5.8 fusion.54
  147.4 0.7 fusion.53
  150.0 1.9 fusion.55
  153.8 1.9 fusion.56
  157.6 1.9 fusion.57
  161.6 1.9 fusion.58
  165.3 1.9 fusion.59
  168.9 1.9 fusion.60
  172.9 2.0 fusion.61
  176.6 1.9 fusion.62
  180.4 1.9 fusion.63
  184.1 1.9 fusion.64
  187.9 1.9 fusion.65
  191.5 2.0 fusion.66
  195.4 1.9 fusion.67
  199.0 1.9 fusion.68
  202.8 1.9 fusion.69
  206.4 1.9 fusion.70
  208.4 0.7 compare_and_fusion.2
  209.1 7.0 gather_fusion
  216.1 5.8 fusion.54
  222.0 0.7 fusion.53
  224.6 1.9 fusion.55
  228.4 1.9 fusion.56
  232.2 1.9 fusion.57
  236.2 1.9 fusion.58
  240.0 1.9 fusion.59
  243.6 1.9 fusion.60
  247.5 1.9 fusion.61
  251.2 1.9 fusion.62
  255.0 1.9 fusion.63
  258.8 2.0 fusion.64
  262.6 1.9 fusion.65
  266.2 1.9 fusion.66
  270.0 1.9 fusion.67
  273.7 1.9 fusion.68
  277.4 1.9 fusion.69
  281.0 2.0 fusion.70
  283.0 0.7 compare_and_fusion.2
  283.7 7.0 gather_fusion
  290.8 5.8 fusion.54
  299.2 1.9 fusion.55
  303.1 1.9 fusion.56
  306.9 1.9 fusion.57
  310.9 1.9 fusion.58
  314.7 1.9 fusion.59
  318.3 1.9 fusion.60
  322.2 1.9 fusion.61
  325.8 1.9 fusion.62
  329.6 1.9 fusion.63
  333.4 1.9 fusion.64
  337.2 1.9 fusion.65
  340.8 1.9 fusion.66
  344.6 1.9 fusion.67
  348.3 1.9 fusion.68
  352.0 1.9 fusion.69
  355.7 1.9 fusion.70
  359.2 415.7 %reduce-scatter.2.cloned.1.call-done = f32[256,768]{1,0:T(8,128)} async-done(((f32[2048,768]{1,0:T(8,128)}), f32[256,768]{1,0:T(8,128)}) %reduce-scatter.2.cloned.1.call-update) | async-done | bytes 786448 | tf_op jit(solution)/shard_map/reduce_scatter | solution.py:63
  774.8 2.7 fusion.25
  (27 shorter events, 3.3 us)
Async XLA Ops:
  6.5 351.7 %copy-start = (f32[768,256]{1,0:T(8,128)S(1)}, f32[768,256]{1,0:T(8,128)}, u32[]{:S(2)}) copy-start(f32[768,256]{1,0:T(8,128)} %param.17) | copy-start | bytes 2359300
  6.5 127.2 %copy-start.6 = (s32[1,1,128]{2,1,0:T(1,128)S(1)}, s32[1,1,128]{2,1,0:T(1,128)}, u32[]{:S(2)}) copy-start(s32[1,1,128]{2,1,0:T(1,128)} %param.13) | copy-start | bytes 1540
  6.5 127.2 %copy-start.2 = (s32[1,1,128]{2,1,0:T(1,128)S(1)}, s32[1,1,128]{2,1,0:T(1,128)}, u32[]{:S(2)}) copy-start(s32[1,1,128]{2,1,0:T(1,128)} %param.14) | copy-start | bytes 1540
  6.5 123.9 %all-gather.2.cloned.1.call-start = ((), (), s32[]{:S(2)}) async-start(), calls=%async_computation.1 | async-start | bytes 12976128 | tf_op jit(solution)/shard_map/all_gather | solution.py:59
  7.3 767.6 %reduce-scatter.2.cloned.1.call-start = ((), (), s32[]{:S(2)}) async-start(), calls=%async_computation.2 | async-start | bytes 7077888 | tf_op jit(solution)/shard_map/reduce_scatter | solution.py:63
  357.6 0.7 copy-start.3
  357.6 1.0 copy-start.1
  357.6 417.2 %copy-start.4 = (f32[768,256]{1,0:T(8,128)S(1)}, f32[768,256]{1,0:T(8,128)}, u32[]{:S(2)}) copy-start(f32[768,256]{1,0:T(8,128)} %param.18) | copy-start | bytes 2359300
  357.6 417.2 %copy-start.5 = (f32[256]{0:T(256)S(1)}, f32[256]{0:T(256)}, u32[]{:S(2)}) copy-start(f32[256]{0:T(256)} %param.19) | copy-start | bytes 3076
Sparse Core Ops, SparseCore 0:
  9.9 120.4 all-gather.1
  357.8 417.0 reduce-scatter.1
where the time goes:
time: 792 us; the launch traced here: 784 us
  waiting for transfers between devices  539 us (68%)
  other arithmetic  94.1 us (12%)
  loops' own time  88.8 us (11%)
  local copies, waits for them, and re-layouts  27.7 us (3%)
  matrix products  20.8 us (3%)
  between operations  14.1 us (2%)
    reduce_scatter x1, waiting for transfers between devices, body(): lax.psum_scatter(partial_terms, 'col', scatter_dimension=0, tiled=True)  416 us
    all_gather x1, waiting for transfers between devices, body(): columns = lax.all_gather(node_features, 'row', axis=0, tiled=True)  122 us
    dynamic_update_slice x48, other arithmetic, add_group(): lax.dynamic_update_slice_in_dim(running, current + product[slot][None], t...  91.9 us
    another operation x1, loops' own time, aggregate(): lax.fori_loop(0, groups, add_group, jnp.zeros((row_tiles, tile_size, feat...  88.8 us
    gather x3, local copies, waits for them, and re-layouts, add_group(): picked = jnp.take(col_tiles, picked_cols, axis=0)  21.1 us
    dot_general x3, matrix products, tile_products(): jnp.einsum('sij,sjw->siw', zero_one, picked, preferred_element_type=jnp.f...  17.5 us
  transfers between devices with their start and end apart: 2, of which 2 were waited for; matrix products, arithmetic and copies ran while one was open for 0% of the time, Pallas kernels for 0%

commit v1 on v0

v1 whole, which is shorter than its diff:
```python
import functools

import jax
import jax.numpy as jnp
from jax import lax
from jax.experimental import pallas as pl
from jax.experimental.pallas import tpu as pltpu
from jax.sharding import PartitionSpec as P

Z, X, Y, CORES = 8, 4, 4, 2
SPAN = 256
TILE = 128
H = 256
LANES = 128
WORDS = H // 2
SHARD = SPAN + 8
Z_ORDER = (0, 1, 4, 7, 2, 5, 6, 3)
Z_PLACE = tuple(Z_ORDER.index(d) for d in range(Z))
VMEM_LIMIT = 56 * 1024 * 1024
BF, F32, I32 = jnp.bfloat16, jnp.float32, jnp.int32


def encode(values, out_ref):
    size = jnp.maximum(jnp.max(jnp.abs(values), axis=1, keepdims=True), 2.0**-100)
    exponent = jnp.zeros(size.shape, I32)
    factor = jnp.full(size.shape, 2.0**14, F32)
    for k in (32, 16, 8, 4, 2, 1):
        big = size >= 2.0**k
        size = jnp.where(big, size * 2.0**-k, size)
        factor = jnp.where(big, factor * 2.0**-k, factor)
        exponent = jnp.where(big, exponent + k, exponent)
    for k in (64, 32, 16, 8, 4, 2, 1):
        small = size < 2.0 ** (1 - k)
        size = jnp.where(small, size * 2.0**k, size)
        factor = jnp.where(small, factor * 2.0**k, factor)
        exponent = jnp.where(small, exponent - k, exponent)
    codes = jnp.clip(jnp.floor(values * factor + 0.5), -32767.0, 32767.0).astype(I32)
    out_ref[:SPAN, :] = (codes[:, :WORDS] << 16) | (codes[:, WORDS:] & 0xFFFF)
    along = jnp.transpose(jnp.broadcast_to(exponent, (SPAN, LANES)))
    out_ref[SPAN : SPAN + 8, :] = jnp.zeros((8, LANES), I32)
    for half in range(SPAN // LANES):
        out_ref[SPAN + half : SPAN + half + 1, :] = along[:1, half * LANES : (half + 1) * LANES]


def power_of_two(exponent):
    left = exponent + (120 - 14)
    result = jnp.full(exponent.shape, 2.0**-120, F32)
    for bit in range(7):
        result = jnp.where((left >> bit) & 1 == 1, result * 2.0 ** (1 << bit), result)
    return jnp.where((left >> 7) & 1 == 1, result * 2.0**64 * 2.0**64, result)


def two_codes(words):
    return (words >> 16).astype(F32), ((words << 16) >> 16).astype(F32)


def project_kernel(x_ref, w_ref, out_ref):
    w = w_ref[...]
    high = w.astype(BF)
    low = (w - high.astype(F32)).astype(BF)
    x = x_ref[...]
    z = jnp.dot(x, high, preferred_element_type=F32) + jnp.dot(x, low, preferred_element_type=F32)
    encode(z, out_ref)


def project(x, w):
    return pl.pallas_call(
        project_kernel,
        out_shape=jax.ShapeDtypeStruct((SHARD, WORDS), I32),
        compiler_params=pltpu.CompilerParams(vmem_limit_bytes=VMEM_LIMIT),
        name="project",
    )(x, w)


def aggregate_kernel(layout, slots_ref, pat_hbm, *refs):
    pieces = refs[: len(layout)]
    keep_ref, send_ref, raw, parts, scales, pat, acc, piece_sem, pat_sem = refs[len(layout) :]
    slot_total = pat_hbm.shape[0]
    copies = []
    for n, (first, count) in enumerate(layout):
        copy = pltpu.make_async_copy(
            pieces[n], raw.at[pl.ds(first * SHARD, count * SHARD)], piece_sem.at[n]
        )
        copy.start()
        copies.append(copy)
    pat_copy = pltpu.make_async_copy(pat_hbm, pat, pat_sem)
    pat_copy.start()
    acc[...] = jnp.zeros_like(acc)

    def decode(shard, carry):
        base = pl.multiple_of(shard * SHARD, 8)
        exponents = raw[pl.ds(base + SPAN, 8), :]
        scale = power_of_two(exponents)
        for half in range(2):
            words = raw[pl.ds(base + half * TILE, TILE), :]
            tile = shard * 2 + half
            scales[tile] = jnp.broadcast_to(scale[half : half + 1], (8, LANES))
            for side, code in enumerate(two_codes(words)):
                high = code.astype(BF)
                low = (code - high.astype(F32)).astype(BF)
                at = pl.ds(side * WORDS, WORDS)
                parts[tile, :TILE, at] = high
                parts[tile, TILE:, at] = low
        return carry

    for n, (first, count) in enumerate(layout):
        copies[n].wait()
        lax.fori_loop(first, first + count, decode, 0)
    pat_copy.wait()
    live = slots_ref[2, 0]
    group = 4

    def add_group(g, carry):
        for k in range(group):
            s = g * group + k
            row, col = slots_ref[0, s], slots_ref[1, s]
            scale = jnp.where(s < live, scales[col], 0.0)[:1].astype(BF)
            p = pat[s] * scale
            acc[row] += jnp.dot(
                jnp.concatenate([p, p], axis=1), parts[col], preferred_element_type=F32
            )
        return carry

    lax.fori_loop(0, (live + group - 1) // group, add_group, 0)
    half = acc.shape[0] // 2
    keep_ref[...] = acc[:half].reshape(keep_ref.shape)
    send_ref[...] = acc[half:].reshape(send_ref.shape)


def aggregate(slots, pat, pieces, layout, row_tiles):
    half_rows = row_tiles * TILE // 2
    shards = sum(count for _, count in layout)
    return pl.pallas_call(
        functools.partial(aggregate_kernel, layout),
        out_shape=[jax.ShapeDtypeStruct((half_rows, H), F32)] * 2,
        in_specs=[pl.BlockSpec(memory_space=pltpu.SMEM)]
        + [pl.BlockSpec(memory_space=pl.ANY)] * (1 + len(pieces)),
        out_specs=[pl.BlockSpec(memory_space=pltpu.VMEM)] * 2,
        scratch_shapes=[
            pltpu.VMEM((shards * SHARD, WORDS), I32),
            pltpu.VMEM((shards * 2, 2 * TILE, H), BF),
            pltpu.VMEM((shards * 2, 8, LANES), F32),
            pltpu.VMEM(pat.shape, BF),
            pltpu.VMEM((row_tiles, TILE, H), F32),
            pltpu.SemaphoreType.DMA((len(pieces),)),
            pltpu.SemaphoreType.DMA,
        ],
        compiler_params=pltpu.CompilerParams(vmem_limit_bytes=VMEM_LIMIT),
        name="aggregate",
    )(slots, pat, *pieces)


def pair_kernel(keep_ref, other_ref, own_ref, *pay_refs):
    own_ref[...] = keep_ref[:SPAN] + other_ref[:SPAN]
    for j, pay_ref in enumerate(pay_refs, 1):
        at = pl.ds(j * SPAN, SPAN)
        encode(keep_ref[at] + other_ref[at], pay_ref)


def add_pair(keep, other):
    return pl.pallas_call(
        pair_kernel,
        out_shape=[jax.ShapeDtypeStruct((SPAN, H), F32)]
        + [jax.ShapeDtypeStruct((SHARD, WORDS), I32)] * (Y - 1),
        compiler_params=pltpu.CompilerParams(vmem_limit_bytes=VMEM_LIMIT),
        name="add_pair",
    )(keep, other)


def self_kernel(x_ref, w_ref, bias_ref, out_ref):
    w = w_ref[...]
    high = w.astype(BF)
    low = (w - high.astype(F32)).astype(BF)
    x = x_ref[...]
    z = jnp.dot(x, high, preferred_element_type=F32) + jnp.dot(x, low, preferred_element_type=F32)
    out_ref[...] = z + bias_ref[...]


def self_part(x, w, bias):
    return pl.pallas_call(
        self_kernel,
        out_shape=jax.ShapeDtypeStruct((SPAN, H), F32),
        compiler_params=pltpu.CompilerParams(vmem_limit_bytes=VMEM_LIMIT),
        name="self_part",
    )(x, w, bias)


def finish_kernel(own_ref, self_ref, count_ref, *refs):
    out_ref = refs[-1]
    divisor = count_ref[...].astype(F32)
    for half in range(SPAN // TILE):
        at = pl.ds(half * TILE, TILE)
        left, right = own_ref[at, :WORDS], own_ref[at, WORDS:]
        for pay_ref in refs[:-1]:
            row = pay_ref[SPAN + half : SPAN + half + 1, :]
            scale = jnp.transpose(jnp.broadcast_to(power_of_two(row), (TILE, LANES)))
            a, b = two_codes(pay_ref[at, :])
            left, right = left + a * scale, right + b * scale
        d = divisor[half * TILE : (half + 1) * TILE]
        out_ref[at, :WORDS] = jnp.maximum(left / d + self_ref[at, :WORDS], 0.0)
        out_ref[at, WORDS:] = jnp.maximum(right / d + self_ref[at, WORDS:], 0.0)


def finish(own, self_rows, count, pays):
    return pl.pallas_call(
        finish_kernel,
        out_shape=jax.ShapeDtypeStruct((SPAN, H), F32),
        compiler_params=pltpu.CompilerParams(vmem_limit_bytes=VMEM_LIMIT),
        name="finish",
    )(own, self_rows, count, *pays)


def from_z(x, d):
    return lax.ppermute(x, "row", [(((z + d) % Z) * X + k, z * X + k) for z in range(Z) for k in range(X)])


def from_x(x, d):
    return lax.ppermute(x, "row", [(z * X + (k + d) % X, z * X + k) for z in range(Z) for k in range(X)])


def from_y(x, d):
    return lax.ppermute(
        x, "col", [(((y + d) % Y) * CORES + k, y * CORES + k) for y in range(Y) for k in range(CORES)]
    )


def from_core(x):
    return lax.ppermute(x, "col", [(c ^ 1, c) for c in range(Y * CORES)])


def z_near(block):
    near, far, last = from_z(block, 1), from_z(block, 4), from_z(block, -1)
    return jnp.concatenate([near, far, last])


def z_rest(near):
    up = from_z(near[: 2 * SHARD], 1)
    down = from_z(jnp.concatenate([near[2 * SHARD :], near[SHARD : 2 * SHARD]]), -1)
    return up, down


def body(
    node_features, neighbour_count, tile_rows, tile_cols, tile_count, patterns, w_self, w_neigh, bias
):
    row_tiles = Y * CORES * SPAN // TILE
    mine = project(node_features, w_neigh)

    across = from_x(mine, 2)
    side_0 = [from_x(mine, 1), from_x(mine, -1)]
    near = z_near(mine)
    across_near = z_near(across)
    side_1 = [from_x(near, 1), from_x(near, -1)]
    up, down = z_rest(near)
    across_up, across_down = z_rest(across_near)
    rest = jnp.concatenate([up, down])
    side_2 = [from_x(rest, 1), from_x(rest, -1)]

    row_at, col_at = lax.axis_index("row"), lax.axis_index("col")
    z_at, x_at = row_at // X, row_at % X
    y_at, core_at = col_at // CORES, col_at % CORES
    cols = tile_cols[0, 0]
    source = cols // 2
    dz = (source // X - z_at) % Z
    dx = (source % X - x_at) % X
    place = jnp.take(jnp.asarray(Z_PLACE, I32), dz)
    col_index = (dx * Z + place) * 2 + cols % 2
    rows = tile_rows[0, 0]
    span = rows // 2
    other = (span % CORES != core_at).astype(I32)
    row_index = other * (row_tiles // 2) + ((span // CORES - y_at) % Y) * 2 + rows % 2
    slots = jnp.stack([row_index, col_index, jnp.broadcast_to(tile_count[0, 0], rows.shape)])

    pieces = [mine, near, rest, side_0[0], side_1[0], side_2[0], across, across_near, across_up, across_down,
              side_0[1], side_1[1], side_2[1]]
    layout = [(0, 1), (1, 3), (4, 4), (8, 1), (9, 3), (12, 4), (16, 1), (17, 3), (20, 2), (22, 2),
              (24, 1), (25, 3), (28, 4)]
    keep, send = aggregate(slots, patterns[0, 0].astype(BF), pieces, layout, row_tiles)

    own, *pays = add_pair(keep, from_core(send))
    pays = [from_y(pay, -j) for j, pay in enumerate(pays, 1)]
    self_rows = self_part(node_features, w_self, bias[None, :])
    return finish(own, self_rows, neighbour_count[:, None], pays)


def solution(mesh):
    return jax.shard_map(
        body,
        mesh=mesh,
        in_specs=(
            P(("row", "col"), None),
            P(("row", "col")),
            P("row", "col", None),
            P("row", "col", None),
            P("row", "col"),
            P("row", "col", None, None, None),
            P(),
            P(),
            P(),
        ),
        out_specs=P(("row", "col"), None),
        check_vma=False,
    )
```

time: 792 us -> 99.7 us (0.13)
  waiting for transfers between devices: 539 us -> 28.3 us
  loops' own time: 88.8 us -> 0 us
  other arithmetic: 94.1 us -> 8.05 us
  starting transfers between devices: 0.04 us -> 37.6 us
  local copies, waits for them, and re-layouts: 27.7 us -> 4.24 us
  matrix products: 20.8 us -> 0 us
  Pallas kernels: 0 us -> 19.9 us
  between operations: 14.1 us -> 0.9 us
    reduce_scatter x1 -> x0, waiting for transfers between devices: 416 us -> none  [body(): lax.psum_scatter(partial_terms, 'col', scatter_dimension=0, tiled=True)]
    all_gather x1 -> x0, waiting for transfers between devices: 122 us -> none  [body(): columns = lax.all_gather(node_features, 'row', axis=0, tiled=True)]
    dynamic_update_slice x48 -> x0, other arithmetic: 91.9 us -> none  [add_group(): lax.dynamic_update_slice_in_dim(running, current + product[slot][None], t...]
    another operation x1 -> x0, loops' own time: 88.8 us -> none  [aggregate(): lax.fori_loop(0, groups, add_group, jnp.zeros((row_tiles, tile_size, feat...]
    ppermute x0 -> x21, starting transfers between devices: none -> 37.6 us  [the longest x10 17.1 us: from_z(): lax.ppermute(x, 'row', [((z + d) % Z * X + k, z * X + k) for z in range(Z...]
    ppermute x0 -> x21, waiting for transfers between devices: none -> 28.3 us  [the longest x10 16.2 us: from_z(): lax.ppermute(x, 'row', [((z + d) % Z * X + k, z * X + k) for z in range(Z...]
    gather x3 -> x0, local copies, waits for them, and re-layouts: 21.1 us -> none  [add_group(): picked = jnp.take(col_tiles, picked_cols, axis=0)]
    dot_general x5 -> x0, matrix products: 20.8 us -> none  [the longest x3 17.5 us: tile_products(): jnp.einsum('sij,sjw->siw', zero_one, picked, preferred_element_type=jnp.f...]
  transfers between devices with their start and end apart: 2 -> 21, of which waited for: 2 -> 6; matrix products, arithmetic and copies ran while one was open for 0% -> 9% of each run, Pallas kernels for 0% -> 2%
where the time goes in v1:
time: 99.7 us; the launch traced here: 99.1 us
  starting transfers between devices  37.6 us (38%)
  waiting for transfers between devices  28.3 us (28%)
  Pallas kernels  19.9 us (20%)
  other arithmetic  8.05 us (8%)
  local copies, waits for them, and re-layouts  4.24 us (4%)
    ppermute x10, starting transfers between devices, from_z(): lax.ppermute(x, 'row', [((z + d) % Z * X + k, z * X + k) for z in range(Z...  17.1 us
    ppermute x10, waiting for transfers between devices, from_z(): lax.ppermute(x, 'row', [((z + d) % Z * X + k, z * X + k) for z in range(Z...  16.2 us
    ppermute x7, starting transfers between devices, from_x(): lax.ppermute(x, 'row', [(z * X + (k + d) % X, z * X + k) for z in range(Z...  13 us
    pallas_call x1, Pallas kernels, aggregate(): pl.pallas_call(functools.partial(aggregate_kernel, layout), out_shape=[ja...  9 us
    ppermute x3, starting transfers between devices, from_y(): lax.ppermute(x, 'col', [((y + d) % Y * CORES + k, y * CORES + k) for y in...  7.42 us
    convert_element_type x1, other arithmetic, body(): patterns[0, 0].astype(BF)  6.46 us
    ppermute x7, waiting for transfers between devices, from_x(): lax.ppermute(x, 'row', [(z * X + (k + d) % X, z * X + k) for z in range(Z...  5.68 us
    pallas_call x1, Pallas kernels, add_pair(): pl.pallas_call(pair_kernel, out_shape=[jax.ShapeDtypeStruct((SPAN, H), F3...  3.7 us
  transfers between devices with their start and end apart: 21, of which 6 were waited for; matrix products, arithmetic and copies ran while one was open for 9% of the time, Pallas kernels for 2%

profile of v1, /device:TPU:32, one launch (start us, length us, event | category | flops | bytes accessed | tf_op | source)
XLA Modules:
  0.0 99.1 jit_solution(7626292142794000598)
XLA Ops:
  0.0 2.8 %project.1.refs_0_ = s32[264,128]{1,0:T(8,128)} custom-call(bf16[256,768]{1,0:T(8,128)(2,1)} %x_ref.3, f32[768,256]{1,0:T(8,128)} %w_ref.2), custom_call_target="tpu_custom_call" | custom-call | tf_op jit(solution)/shard_map/project/pallas_call | solution.py:67
  2.8 1.8 %collective-permute-start = (s32[264,128]{1,0:T(8,128)}, s32[264,128]{1,0:T(8,128)S(1)}, u32[]{:S(2)}, u32[]{:S(2)}) collective-permute-start(s32[264,128]{1,0:T(8,128)} %project.1.refs_0_), channel_id=1, source_target_pairs={{32,0},{40,8},{48,16},{56,24},{64,32},{72,40},{80,48},{88,56},{96,... | collective-permute-start | bytes 405512 | tf_op jit(solution)/shard_map/ppermute | solution.py:214
  4.6 5.5 %collective-permute-start.1 = (s32[264,128]{1,0:T(8,128)}, s32[264,128]{1,0:T(8,128)S(1)}, u32[]{:S(2)}, u32[]{:S(2)}) collective-permute-start(s32[264,128]{1,0:T(8,128)} %project.1.refs_0_), channel_id=1, source_target_pairs={{128,0},{136,8},{144,16},{152,24},{160,32},{168,40},{176,48},{184,... | collective-permute-start | bytes 405512 | tf_op jit(solution)/shard_map/ppermute | solution.py:214
  10.1 1.0 %collective-permute-start.2 = (s32[264,128]{1,0:T(8,128)}, s32[264,128]{1,0:T(8,128)S(1)}, u32[]{:S(2)}, u32[]{:S(2)}) collective-permute-start(s32[264,128]{1,0:T(8,128)} %project.1.refs_0_), channel_id=1, source_target_pairs={{224,0},{232,8},{240,16},{248,24},{0,32},{8,40},{16,48},{24,56},{3... | collective-permute-start | bytes 405512 | tf_op jit(solution)/shard_map/ppermute | solution.py:214
  11.1 3.0 %collective-permute-start.8 = (s32[264,128]{1,0:T(8,128)}, s32[264,128]{1,0:T(8,128)S(1)}, u32[]{:S(2)}, u32[]{:S(2)}) collective-permute-start(s32[264,128]{1,0:T(8,128)} %project.1.refs_0_), channel_id=1, source_target_pairs={{16,0},{24,8},{0,16},{8,24},{48,32},{56,40},{32,48},{40,56},{80,64... | collective-permute-start | bytes 405512 | tf_op jit(solution)/shard_map/ppermute | solution.py:218
  14.1 6.5 %convert_bitcast_fusion.pat_hbm = bf16[128,128,128]{2,1,0:T(8,128)(2,1)} fusion(s32[1,1,128,128,128]{4,3,2,1,0:T(8,128)} %param.15), kind=kLoop, calls=%fused_computation | loop fusion | flops 2097152 | bytes 12582912 | tf_op jit(solution)/shard_map/convert_element_type | solution.py:277
  20.6 0.0 collective-permute-done
  20.6 0.0 collective-permute-done.1
  20.6 0.0 collective-permute-done.2
  20.6 1.1 %collective-permute-start.3 = (s32[528,128]{1,0:T(8,128)S(1)}, s32[528,128]{1,0:T(8,128)S(1)}, u32[]{:S(2)}, u32[]{:S(2)}) collective-permute-start(s32[528,128]{1,0:T(8,128)S(1)} %get-tuple-element.20), channel_id=1, source_target_pairs={{32,0},{40,8},{48,16},{56,24},{64,32},{72,40},{80,48},{88,56},{96,... | collective-permute-start | bytes 811016 | tf_op jit(solution)/shard_map/ppermute | solution.py:214
  21.7 1.0 %collective-permute-start.4 = (s32[528,128]{1,0:T(8,128)S(1)}, s32[528,128]{1,0:T(8,128)S(1)}, u32[]{:S(2)}, u32[]{:S(2)}) collective-permute-start(s32[528,128]{1,0:T(8,128)S(1)} %get-tuple-element.19), channel_id=1, source_target_pairs={{224,0},{232,8},{240,16},{248,24},{0,32},{8,40},{16,48},{24,56},{3... | collective-permute-start | bytes 811016 | tf_op jit(solution)/shard_map/ppermute | solution.py:214
  22.7 0.0 collective-permute-done.8.refs_6_
  22.7 3.1 %collective-permute-start.10 = (s32[264,128]{1,0:T(8,128)S(1)}, s32[264,128]{1,0:T(8,128)S(1)}, u32[]{:S(2)}, u32[]{:S(2)}) collective-permute-start(s32[264,128]{1,0:T(8,128)S(1)} %collective-permute-done.8.refs_6_), channel_id=1, source_target_pairs={{128,0},{136,8},{144,16},{152,24},{160,32},{168,40},{176,48},{184,... | collective-permute-start | bytes 405512 | tf_op jit(solution)/shard_map/ppermute | solution.py:214
  25.9 0.8 collective-permute-start.11
  26.7 1.2 %collective-permute-start.9 = (s32[264,128]{1,0:T(8,128)S(1)}, s32[264,128]{1,0:T(8,128)S(1)}, u32[]{:S(2)}, u32[]{:S(2)}) collective-permute-start(s32[264,128]{1,0:T(8,128)S(1)} %collective-permute-done.8.refs_6_), channel_id=1, source_target_pairs={{32,0},{40,8},{48,16},{56,24},{64,32},{72,40},{80,48},{88,56},{96,... | collective-permute-start | bytes 405512 | tf_op jit(solution)/shard_map/ppermute | solution.py:214
  27.9 0.0 copy-start.2
  27.9 10.5 %collective-permute-done.10 = s32[264,128]{1,0:T(8,128)S(1)} collective-permute-done((s32[264,128]{1,0:T(8,128)S(1)}, s32[264,128]{1,0:T(8,128)S(1)}, u32[]{:S(2)}, u32[]{:S(2)}) %collective-permute-start.10) | collective-permute-done | bytes 135200 | tf_op jit(solution)/shard_map/ppermute | solution.py:214
  38.4 0.0 copy-done.5
  38.4 1.5 %collective-permute-start.14 = (s32[264,128]{1,0:T(8,128)S(1)}, s32[264,128]{1,0:T(8,128)S(1)}, u32[]{:S(2)}, u32[]{:S(2)}) collective-permute-start(s32[264,128]{1,0:T(8,128)S(1)} %copy-done.5), channel_id=1, source_target_pairs={{24,0},{0,8},{8,16},{16,24},{56,32},{32,40},{40,48},{48,56},{88,64... | collective-permute-start | bytes 405512 | tf_op jit(solution)/shard_map/ppermute | solution.py:218
  39.9 0.0 collective-permute-done.11
  39.9 1.7 %collective-permute-start.5 = (s32[264,128]{1,0:T(8,128)S(1)}, s32[264,128]{1,0:T(8,128)S(1)}, u32[]{:S(2)}, u32[]{:S(2)}) collective-permute-start(s32[264,128]{1,0:T(8,128)S(1)} %copy-done.5), channel_id=1, source_target_pairs={{8,0},{16,8},{24,16},{0,24},{40,32},{48,40},{56,48},{32,56},{72,64... | collective-permute-start | bytes 405512 | tf_op jit(solution)/shard_map/ppermute | solution.py:218
  41.7 0.0 collective-permute-done.9
  41.7 0.3 collective-permute-start.15
  42.0 0.1 pad_add_fusion.3
  42.0 0.0 collective-permute-done.3
  42.0 3.0 %collective-permute-start.6 = (s32[792,128]{1,0:T(8,128)S(1)}, s32[792,128]{1,0:T(8,128)S(1)}, u32[]{:S(2)}, u32[]{:S(2)}) collective-permute-start(s32[792,128]{1,0:T(8,128)S(1)} %constant_dynamic-update-slice_fusion.refs_1_), channel_id=1, source_target_pairs={{8,0},{16,8},{24,16},{0,24},{40,32},{48,40},{56,48},{32,56},{72,64... | collective-permute-start | bytes 1216520 | tf_op jit(solution)/shard_map/ppermute | solution.py:218
  45.1 0.0 collective-permute-done.4
  45.1 1.5 %collective-permute-start.12 = (s32[528,128]{1,0:T(8,128)S(1)}, s32[528,128]{1,0:T(8,128)S(1)}, u32[]{:S(2)}, u32[]{:S(2)}) collective-permute-start(s32[528,128]{1,0:T(8,128)S(1)} %get-tuple-element.18), channel_id=1, source_target_pairs={{32,0},{40,8},{48,16},{56,24},{64,32},{72,40},{80,48},{88,56},{96,... | collective-permute-start | bytes 811016 | tf_op jit(solution)/shard_map/ppermute | solution.py:214
  46.6 0.0 copy-start
  46.6 0.0 collective-permute-done.14.refs_10_
  46.7 0.0 copy-start.14
  46.7 0.3 collective-permute-start.16
  46.9 0.0 collective-permute-done.5.refs_3_
  46.9 0.0 copy-start.15
  47.0 3.2 %collective-permute-start.7 = (s32[1056,128]{1,0:T(8,128)S(1)}, s32[1056,128]{1,0:T(8,128)S(1)}, u32[]{:S(2)}, u32[]{:S(2)}) collective-permute-start(s32[1056,128]{1,0:T(8,128)S(1)} %constant_dynamic-update-slice_fusion.3.refs_2_), channel_id=1, source_target_pairs={{8,0},{16,8},{24,16},{0,24},{40,32},{48,40},{56,48},{32,56},{72,64... | collective-permute-start | bytes 1622024 | tf_op jit(solution)/shard_map/ppermute | solution.py:218
  50.2 0.0 copy-done.17
  50.9 0.1 pad.13.clone
  50.9 0.7 collective-permute-done.12.refs_8_
  51.6 0.0 collective-permute-start.13
  51.6 0.7 add_add_fusion.slots_ref
  52.3 0.8 pad_add_fusion.refs_7_
  53.1 5.0 %collective-permute-done.13.refs_9_ = s32[528,128]{1,0:T(8,128)S(1)} collective-permute-done((s32[528,128]{1,0:T(8,128)S(1)}, s32[528,128]{1,0:T(8,128)S(1)}, u32[]{:S(2)}, u32[]{:S(2)}) %collective-permute-start.13) | collective-permute-done | bytes 270368 | tf_op jit(solution)/shard_map/ppermute | solution.py:214
  58.1 0.0 collective-permute-done.15.refs_11_
  58.1 0.0 collective-permute-done.6.refs_4_
  58.1 5.7 %collective-permute-done.16.refs_12_ = s32[1056,128]{1,0:T(8,128)S(1)} collective-permute-done((s32[1056,128]{1,0:T(8,128)S(1)}, s32[1056,128]{1,0:T(8,128)S(1)}, u32[]{:S(2)}, u32[]{:S(2)}) %collective-permute-start.16) | collective-permute-done | bytes 540704 | tf_op jit(solution)/shard_map/ppermute | solution.py:218
  63.8 0.0 collective-permute-done.7.refs_5_
  63.9 0.8 copy-done.3
  64.6 0.8 copy-done.4
  65.4 9.0 %aggregate.1 = (f32[1024,256]{1,0:T(8,128)}, f32[1024,256]{1,0:T(8,128)}) custom-call(s32[3,128]{1,0:T(4,128)} %add_add_fusion.slots_ref, bf16[128,128,128]{2,1,0:T(8,128)(2,1)} %convert_bitcast_fusion.pat_hbm, s32[264,128]{1,0:T(8,128)} %project.1.refs_0_, s32[792,128]{1,0:T(8,128)} %copy-done.2, s32[1056,128]{1,0:T(8,128)} %copy-done, ...), custom_call_target="tpu_custom_call" | custom-call | tf_op jit(solution)/shard_map/aggregate/pallas_call | solution.py:133
  74.4 0.1 collective-permute-start.17
  74.5 2.9 %collective-permute-done.17.other_ref = f32[1024,256]{1,0:T(8,128)S(1)} collective-permute-done((f32[1024,256]{1,0:T(8,128)}, f32[1024,256]{1,0:T(8,128)S(1)}, u32[]{:S(2)}, u32[]{:S(2)}) %collective-permute-start.17) | collective-permute-done | bytes 1048608 | tf_op jit(solution)/shard_map/ppermute | solution.py:228
  77.4 1.0 copy-done.1
  78.4 3.7 %add_pair.1 = (f32[256,256]{1,0:T(8,128)}, s32[264,128]{1,0:T(8,128)}, s32[264,128]{1,0:T(8,128)}, s32[264,128]{1,0:T(8,128)}) custom-call(f32[1024,256]{1,0:T(8,128)} %get-tuple-element.11.keep_ref, f32[1024,256]{1,0:T(8,128)} %copy-done.1), custom_call_target="tpu_custom_call" | custom-call | tf_op jit(solution)/shard_map/add_pair/pallas_call | solution.py:161
  82.1 2.1 %collective-permute-start.18 = (s32[264,128]{1,0:T(8,128)}, s32[264,128]{1,0:T(8,128)S(1)}, u32[]{:S(2)}, u32[]{:S(2)}) collective-permute-start(s32[264,128]{1,0:T(8,128)} %get-tuple-element.14), channel_id=1, source_target_pairs={{6,0},{7,1},{0,2},{1,3},{2,4},{3,5},{4,6},{5,7},{14,8},{15,9},{8,1... | collective-permute-start | bytes 405512 | tf_op jit(solution)/shard_map/ppermute | solution.py:222
  84.2 5.4 %collective-permute-start.19 = (s32[264,128]{1,0:T(8,128)}, s32[264,128]{1,0:T(8,128)S(1)}, u32[]{:S(2)}, u32[]{:S(2)}) collective-permute-start(s32[264,128]{1,0:T(8,128)} %get-tuple-element.15), channel_id=1, source_target_pairs={{4,0},{5,1},{6,2},{7,3},{0,4},{1,5},{2,6},{3,7},{12,8},{13,9},{14,... | collective-permute-start | bytes 405512 | tf_op jit(solution)/shard_map/ppermute | solution.py:222
  89.5 0.0 collective-permute-start.20
  89.5 0.8 copy.11.count_ref
  90.3 2.3 %self_part.1.self_ref = f32[256,256]{1,0:T(8,128)} custom-call(bf16[256,768]{1,0:T(8,128)(2,1)} %x_ref.3, f32[768,256]{1,0:T(8,128)} %w_ref.3, f32[1,256]{1,0:T(1,128)} %bitcast.73), custom_call_target="tpu_custom_call" | custom-call | tf_op jit(solution)/shard_map/self_part/pallas_call | solution.py:180
  92.6 0.0 collective-permute-done.18.refs_0_
  92.6 3.6 %collective-permute-done.19.refs_1_ = s32[264,128]{1,0:T(8,128)S(1)} collective-permute-done((s32[264,128]{1,0:T(8,128)}, s32[264,128]{1,0:T(8,128)S(1)}, u32[]{:S(2)}, u32[]{:S(2)}) %collective-permute-start.19) | collective-permute-done | bytes 135200 | tf_op jit(solution)/shard_map/ppermute | solution.py:222
  96.2 0.0 collective-permute-done.20.refs_2_
  96.2 0.6 copy-done.11
  96.9 0.1 copy-done.12
  96.9 2.2 %finish.1 = f32[256,256]{1,0:T(8,128)} custom-call(f32[256,256]{1,0:T(8,128)} %get-tuple-element.13.own_ref, f32[256,256]{1,0:T(8,128)} %self_part.1.self_ref, s32[256,1]{1,0:T(8,128)} %copy.11.count_ref, s32[264,128]{1,0:T(8,128)} %copy-done.10, s32[264,128]{1,0:T(8,128)} %copy-done.11, s32[264,128]{1,0:T(8,128)} %copy-done.12), custom_call_target="tpu_custom_call" | custom-call | tf_op jit(solution)/shard_map/finish/pallas_call | solution.py:205
  (34 shorter events, 0.2 us)
Async XLA Ops:
  2.8 35.7 %copy-start.5 = (s32[264,128]{1,0:T(8,128)S(1)}, s32[264,128]{1,0:T(8,128)}, u32[]{:S(2)}) copy-start(s32[264,128]{1,0:T(8,128)} %project.1.refs_0_) | copy-start | bytes 405508
  2.8 47.4 %copy-start.17 = (s32[1,1,128]{2,1,0:T(1,128)S(1)}, s32[1,1,128]{2,1,0:T(1,128)}, u32[]{:S(2)}) copy-start(s32[1,1,128]{2,1,0:T(1,128)} %param.12) | copy-start | bytes 1540
  2.8 47.4 %copy-start.18 = (s32[1,1,128]{2,1,0:T(1,128)S(1)}, s32[1,1,128]{2,1,0:T(1,128)}, u32[]{:S(2)}) copy-start(s32[1,1,128]{2,1,0:T(1,128)} %param.13) | copy-start | bytes 1540
  2.8 17.8 %collective-permute-start = (s32[264,128]{1,0:T(8,128)}, s32[264,128]{1,0:T(8,128)S(1)}, u32[]{:S(2)}, u32[]{:S(2)}) collective-permute-start(s32[264,128]{1,0:T(8,128)} %project.1.refs_0_), channel_id=1, source_target_pairs={{32,0},{40,8},{48,16},{56,24},{64,32},{72,40},{80,48},{88,56},{96,... | collective-permute-start | bytes 405512 | tf_op jit(solution)/shard_map/ppermute | solution.py:214
  4.6 16.0 %collective-permute-start.1 = (s32[264,128]{1,0:T(8,128)}, s32[264,128]{1,0:T(8,128)S(1)}, u32[]{:S(2)}, u32[]{:S(2)}) collective-permute-start(s32[264,128]{1,0:T(8,128)} %project.1.refs_0_), channel_id=1, source_target_pairs={{128,0},{136,8},{144,16},{152,24},{160,32},{168,40},{176,48},{184,... | collective-permute-start | bytes 405512 | tf_op jit(solution)/shard_map/ppermute | solution.py:214
  10.1 10.5 %collective-permute-start.2 = (s32[264,128]{1,0:T(8,128)}, s32[264,128]{1,0:T(8,128)S(1)}, u32[]{:S(2)}, u32[]{:S(2)}) collective-permute-start(s32[264,128]{1,0:T(8,128)} %project.1.refs_0_), channel_id=1, source_target_pairs={{224,0},{232,8},{240,16},{248,24},{0,32},{8,40},{16,48},{24,56},{3... | collective-permute-start | bytes 405512 | tf_op jit(solution)/shard_map/ppermute | solution.py:214
  11.1 11.6 %collective-permute-start.8 = (s32[264,128]{1,0:T(8,128)}, s32[264,128]{1,0:T(8,128)S(1)}, u32[]{:S(2)}, u32[]{:S(2)}) collective-permute-start(s32[264,128]{1,0:T(8,128)} %project.1.refs_0_), channel_id=1, source_target_pairs={{16,0},{24,8},{0,16},{8,24},{48,32},{56,40},{32,48},{40,56},{80,64... | collective-permute-start | bytes 405512 | tf_op jit(solution)/shard_map/ppermute | solution.py:218
  20.6 68.9 %copy-start.16 = (s32[256]{0:T(256)S(1)}, s32[256]{0:T(256)}, u32[]{:S(2)}) copy-start(s32[256]{0:T(256)} %param.11) | copy-start | bytes 3076
  20.6 21.4 %collective-permute-start.3 = (s32[528,128]{1,0:T(8,128)S(1)}, s32[528,128]{1,0:T(8,128)S(1)}, u32[]{:S(2)}, u32[]{:S(2)}) collective-permute-start(s32[528,128]{1,0:T(8,128)S(1)} %get-tuple-element.20), channel_id=1, source_target_pairs={{32,0},{40,8},{48,16},{56,24},{64,32},{72,40},{80,48},{88,56},{96,... | collective-permute-start | bytes 811016 | tf_op jit(solution)/shard_map/ppermute | solution.py:214
  21.7 23.4 %collective-permute-start.4 = (s32[528,128]{1,0:T(8,128)S(1)}, s32[528,128]{1,0:T(8,128)S(1)}, u32[]{:S(2)}, u32[]{:S(2)}) collective-permute-start(s32[528,128]{1,0:T(8,128)S(1)} %get-tuple-element.19), channel_id=1, source_target_pairs={{224,0},{232,8},{240,16},{248,24},{0,32},{8,40},{16,48},{24,56},{3... | collective-permute-start | bytes 811016 | tf_op jit(solution)/shard_map/ppermute | solution.py:214
  22.7 41.0 %copy-start.13 = (s32[264,128]{1,0:T(8,128)}, s32[264,128]{1,0:T(8,128)S(1)}, u32[]{:S(2)}) copy-start(s32[264,128]{1,0:T(8,128)S(1)} %collective-permute-done.8.refs_6_) | copy-start | bytes 405508
  22.7 15.7 %collective-permute-start.10 = (s32[264,128]{1,0:T(8,128)S(1)}, s32[264,128]{1,0:T(8,128)S(1)}, u32[]{:S(2)}, u32[]{:S(2)}) collective-permute-start(s32[264,128]{1,0:T(8,128)S(1)} %collective-permute-done.8.refs_6_), channel_id=1, source_target_pairs={{128,0},{136,8},{144,16},{152,24},{160,32},{168,40},{176,48},{184,... | collective-permute-start | bytes 405512 | tf_op jit(solution)/shard_map/ppermute | solution.py:214
  25.9 14.1 %collective-permute-start.11 = (s32[264,128]{1,0:T(8,128)S(1)}, s32[264,128]{1,0:T(8,128)S(1)}, u32[]{:S(2)}, u32[]{:S(2)}) collective-permute-start(s32[264,128]{1,0:T(8,128)S(1)} %collective-permute-done.8.refs_6_), channel_id=1, source_target_pairs={{224,0},{232,8},{240,16},{248,24},{0,32},{8,40},{16,48},{24,56},{3... | collective-permute-start | bytes 405512 | tf_op jit(solution)/shard_map/ppermute | solution.py:214
  26.7 15.0 %collective-permute-start.9 = (s32[264,128]{1,0:T(8,128)S(1)}, s32[264,128]{1,0:T(8,128)S(1)}, u32[]{:S(2)}, u32[]{:S(2)}) collective-permute-start(s32[264,128]{1,0:T(8,128)S(1)} %collective-permute-done.8.refs_6_), channel_id=1, source_target_pairs={{32,0},{40,8},{48,16},{56,24},{64,32},{72,40},{80,48},{88,56},{96,... | collective-permute-start | bytes 405512 | tf_op jit(solution)/shard_map/ppermute | solution.py:214
  27.9 35.9 %copy-start.2 = (s32[792,128]{1,0:T(8,128)}, s32[792,128]{1,0:T(8,128)S(1)}, u32[]{:S(2)}) copy-start(s32[792,128]{1,0:T(8,128)S(1)} %constant_dynamic-update-slice_fusion.refs_1_) | copy-start | bytes 1216516
  38.4 8.2 %collective-permute-start.14 = (s32[264,128]{1,0:T(8,128)S(1)}, s32[264,128]{1,0:T(8,128)S(1)}, u32[]{:S(2)}, u32[]{:S(2)}) collective-permute-start(s32[264,128]{1,0:T(8,128)S(1)} %copy-done.5), channel_id=1, source_target_pairs={{24,0},{0,8},{8,16},{16,24},{56,32},{32,40},{40,48},{48,56},{88,64... | collective-permute-start | bytes 405512 | tf_op jit(solution)/shard_map/ppermute | solution.py:218
  39.9 7.0 %collective-permute-start.5 = (s32[264,128]{1,0:T(8,128)S(1)}, s32[264,128]{1,0:T(8,128)S(1)}, u32[]{:S(2)}, u32[]{:S(2)}) collective-permute-start(s32[264,128]{1,0:T(8,128)S(1)} %copy-done.5), channel_id=1, source_target_pairs={{8,0},{16,8},{24,16},{0,24},{40,32},{48,40},{56,48},{32,56},{72,64... | collective-permute-start | bytes 405512 | tf_op jit(solution)/shard_map/ppermute | solution.py:218
  41.7 16.4 %collective-permute-start.15 = (s32[792,128]{1,0:T(8,128)S(1)}, s32[792,128]{1,0:T(8,128)S(1)}, u32[]{:S(2)}, u32[]{:S(2)}) collective-permute-start(s32[792,128]{1,0:T(8,128)S(1)} %constant_dynamic-update-slice_fusion.refs_1_), channel_id=1, source_target_pairs={{24,0},{0,8},{8,16},{16,24},{56,32},{32,40},{40,48},{48,56},{88,64... | collective-permute-start | bytes 1216520 | tf_op jit(solution)/shard_map/ppermute | solution.py:218
  42.0 16.1 %collective-permute-start.6 = (s32[792,128]{1,0:T(8,128)S(1)}, s32[792,128]{1,0:T(8,128)S(1)}, u32[]{:S(2)}, u32[]{:S(2)}) collective-permute-start(s32[792,128]{1,0:T(8,128)S(1)} %constant_dynamic-update-slice_fusion.refs_1_), channel_id=1, source_target_pairs={{8,0},{16,8},{24,16},{0,24},{40,32},{48,40},{56,48},{32,56},{72,64... | collective-permute-start | bytes 1216520 | tf_op jit(solution)/shard_map/ppermute | solution.py:218
  45.1 6.5 %collective-permute-start.12 = (s32[528,128]{1,0:T(8,128)S(1)}, s32[528,128]{1,0:T(8,128)S(1)}, u32[]{:S(2)}, u32[]{:S(2)}) collective-permute-start(s32[528,128]{1,0:T(8,128)S(1)} %get-tuple-element.18), channel_id=1, source_target_pairs={{32,0},{40,8},{48,16},{56,24},{64,32},{72,40},{80,48},{88,56},{96,... | collective-permute-start | bytes 811016 | tf_op jit(solution)/shard_map/ppermute | solution.py:214
  46.6 17.2 %copy-start = (s32[1056,128]{1,0:T(8,128)}, s32[1056,128]{1,0:T(8,128)S(1)}, u32[]{:S(2)}) copy-start(s32[1056,128]{1,0:T(8,128)S(1)} %constant_dynamic-update-slice_fusion.3.refs_2_) | copy-start | bytes 1622020
  46.7 17.2 %copy-start.14 = (s32[264,128]{1,0:T(8,128)}, s32[264,128]{1,0:T(8,128)S(1)}, u32[]{:S(2)}) copy-start(s32[264,128]{1,0:T(8,128)S(1)} %collective-permute-done.14.refs_10_) | copy-start | bytes 405508
  46.7 17.1 %collective-permute-start.16 = (s32[1056,128]{1,0:T(8,128)S(1)}, s32[1056,128]{1,0:T(8,128)S(1)}, u32[]{:S(2)}, u32[]{:S(2)}) collective-permute-start(s32[1056,128]{1,0:T(8,128)S(1)} %constant_dynamic-update-slice_fusion.3.refs_2_), channel_id=1, source_target_pairs={{24,0},{0,8},{8,16},{16,24},{56,32},{32,40},{40,48},{48,56},{88,64... | collective-permute-start | bytes 1622024 | tf_op jit(solution)/shard_map/ppermute | solution.py:218
  46.9 16.9 %copy-start.15 = (s32[264,128]{1,0:T(8,128)}, s32[264,128]{1,0:T(8,128)S(1)}, u32[]{:S(2)}) copy-start(s32[264,128]{1,0:T(8,128)S(1)} %collective-permute-done.5.refs_3_) | copy-start | bytes 405508
  47.0 16.8 %collective-permute-start.7 = (s32[1056,128]{1,0:T(8,128)S(1)}, s32[1056,128]{1,0:T(8,128)S(1)}, u32[]{:S(2)}, u32[]{:S(2)}) collective-permute-start(s32[1056,128]{1,0:T(8,128)S(1)} %constant_dynamic-update-slice_fusion.3.refs_2_), channel_id=1, source_target_pairs={{8,0},{16,8},{24,16},{0,24},{40,32},{48,40},{56,48},{32,56},{72,64... | collective-permute-start | bytes 1622024 | tf_op jit(solution)/shard_map/ppermute | solution.py:218
  51.6 12.2 %copy-start.8 = (s32[528,128]{1,0:T(8,128)}, s32[528,128]{1,0:T(8,128)S(1)}, u32[]{:S(2)}) copy-start(s32[528,128]{1,0:T(8,128)S(1)} %collective-permute-done.12.refs_8_) | copy-start | bytes 811012
  51.6 6.5 %collective-permute-start.13 = (s32[528,128]{1,0:T(8,128)S(1)}, s32[528,128]{1,0:T(8,128)S(1)}, u32[]{:S(2)}, u32[]{:S(2)}) collective-permute-start(s32[528,128]{1,0:T(8,128)S(1)} %get-tuple-element.17), channel_id=1, source_target_pairs={{224,0},{232,8},{240,16},{248,24},{0,32},{8,40},{16,48},{24,56},{3... | collective-permute-start | bytes 811016 | tf_op jit(solution)/shard_map/ppermute | solution.py:214
  58.1 5.8 %copy-start.9 = (s32[528,128]{1,0:T(8,128)}, s32[528,128]{1,0:T(8,128)S(1)}, u32[]{:S(2)}) copy-start(s32[528,128]{1,0:T(8,128)S(1)} %collective-permute-done.13.refs_9_) | copy-start | bytes 811012
  58.1 5.8 %copy-start.6 = (s32[792,128]{1,0:T(8,128)}, s32[792,128]{1,0:T(8,128)S(1)}, u32[]{:S(2)}) copy-start(s32[792,128]{1,0:T(8,128)S(1)} %collective-permute-done.15.refs_11_) | copy-start | bytes 1216516
  58.1 5.8 %copy-start.7 = (s32[792,128]{1,0:T(8,128)}, s32[792,128]{1,0:T(8,128)S(1)}, u32[]{:S(2)}) copy-start(s32[792,128]{1,0:T(8,128)S(1)} %collective-permute-done.6.refs_4_) | copy-start | bytes 1216516
  63.8 0.8 copy-start.3
  64.6 0.8 copy-start.4
  74.4 3.0 %collective-permute-start.17 = (f32[1024,256]{1,0:T(8,128)}, f32[1024,256]{1,0:T(8,128)S(1)}, u32[]{:S(2)}, u32[]{:S(2)}) collective-permute-start(f32[1024,256]{1,0:T(8,128)} %get-tuple-element.12), channel_id=1, source_target_pairs={{1,0},{0,1},{3,2},{2,3},{5,4},{4,5},{7,6},{6,7},{9,8},{8,9},{11,10... | collective-permute-start | bytes 3145736 | tf_op jit(solution)/shard_map/ppermute | solution.py:228
  77.4 1.0 copy-start.1
  82.1 10.5 %collective-permute-start.18 = (s32[264,128]{1,0:T(8,128)}, s32[264,128]{1,0:T(8,128)S(1)}, u32[]{:S(2)}, u32[]{:S(2)}) collective-permute-start(s32[264,128]{1,0:T(8,128)} %get-tuple-element.14), channel_id=1, source_target_pairs={{6,0},{7,1},{0,2},{1,3},{2,4},{3,5},{4,6},{5,7},{14,8},{15,9},{8,1... | collective-permute-start | bytes 405512 | tf_op jit(solution)/shard_map/ppermute | solution.py:222
  84.2 12.1 %collective-permute-start.19 = (s32[264,128]{1,0:T(8,128)}, s32[264,128]{1,0:T(8,128)S(1)}, u32[]{:S(2)}, u32[]{:S(2)}) collective-permute-start(s32[264,128]{1,0:T(8,128)} %get-tuple-element.15), channel_id=1, source_target_pairs={{4,0},{5,1},{6,2},{7,3},{0,4},{1,5},{2,6},{3,7},{12,8},{13,9},{14,... | collective-permute-start | bytes 405512 | tf_op jit(solution)/shard_map/ppermute | solution.py:222
  89.5 6.7 %collective-permute-start.20 = (s32[264,128]{1,0:T(8,128)}, s32[264,128]{1,0:T(8,128)S(1)}, u32[]{:S(2)}, u32[]{:S(2)}) collective-permute-start(s32[264,128]{1,0:T(8,128)} %get-tuple-element.16), channel_id=1, source_target_pairs={{2,0},{3,1},{4,2},{5,3},{6,4},{7,5},{0,6},{1,7},{10,8},{11,9},{12,... | collective-permute-start | bytes 405512 | tf_op jit(solution)/shard_map/ppermute | solution.py:222
  92.6 3.6 %copy-start.10 = (s32[264,128]{1,0:T(8,128)}, s32[264,128]{1,0:T(8,128)S(1)}, u32[]{:S(2)}) copy-start(s32[264,128]{1,0:T(8,128)S(1)} %collective-permute-done.18.refs_0_) | copy-start | bytes 405508
  96.2 0.7 copy-start.11
  96.2 0.7 copy-start.12

commit v2 on v1

v2 whole, which is shorter than its diff:
```python
import functools

import jax
import jax.numpy as jnp
from jax import lax
from jax.experimental import pallas as pl
from jax.experimental.pallas import tpu as pltpu
from jax.sharding import PartitionSpec as P

Z, X, Y, CORES = 8, 4, 4, 2
SPAN = 256
TILE = 128
H = 256
LANES = 128
WORDS = H // 2
SHARD = SPAN + 8
GROUP = 16
EARLY = 20
STEPS = (0, 1, -1, 2)
VMEM_LIMIT = 20 * 1024 * 1024
BF, F32, I32 = jnp.bfloat16, jnp.float32, jnp.int32


def encode(values, out_ref):
    size = jnp.maximum(jnp.max(jnp.abs(values), axis=1, keepdims=True), 2.0**-100)
    exponent = jnp.floor(jnp.log2(size) + 0.001)
    codes = jnp.floor(values * jnp.exp2(14.0 - exponent) + 0.5).astype(I32)
    out_ref[:SPAN, :] = (codes[:, :WORDS] << 16) | (codes[:, WORDS:] & 0xFFFF)
    along = jnp.transpose(jnp.broadcast_to(exponent, (SPAN, LANES))).astype(I32)
    out_ref[SPAN : SPAN + 8, :] = jnp.zeros((8, LANES), I32)
    for half in range(SPAN // LANES):
        out_ref[SPAN + half : SPAN + half + 1, :] = along[:1, half * LANES : (half + 1) * LANES]


def power_of_two(exponent):
    left = exponent + (120 - 14)
    result = jnp.full(exponent.shape, 2.0**-120, F32)
    for bit in range(7):
        result = jnp.where((left >> bit) & 1 == 1, result * 2.0 ** (1 << bit), result)
    return jnp.where((left >> 7) & 1 == 1, result * 2.0**64 * 2.0**64, result)


def two_codes(words):
    return (words >> 16).astype(F32), ((words << 16) >> 16).astype(F32)


def vmem(*arrays):
    return [pltpu.with_memory_space_constraint(array, pltpu.VMEM) for array in arrays]


IN_VMEM = pl.BlockSpec(memory_space=pltpu.VMEM)


def project_kernel(x_ref, w_ref, out_ref):
    w = w_ref[...]
    high = w.astype(BF)
    low = (w - high.astype(F32)).astype(BF)
    x = x_ref[...]
    z = jnp.dot(x, high, preferred_element_type=F32) + jnp.dot(x, low, preferred_element_type=F32)
    encode(z, out_ref)


def project(x, w):
    return pl.pallas_call(
        project_kernel,
        out_shape=pltpu.VMEM((SHARD, WORDS), I32),
        compiler_params=pltpu.CompilerParams(vmem_limit_bytes=VMEM_LIMIT),
        name="project",
    )(x, w)


def load_kernel(pat_hbm, after_ref, out_ref, zero_ref, landing, sem):
    chunk, depth = landing.shape[1], landing.shape[0]
    steps = pat_hbm.shape[0] // chunk

    def fetch(step):
        slot = step % depth
        return pltpu.make_async_copy(pat_hbm.at[pl.ds(step * chunk, chunk)], landing.at[slot], sem.at[slot])

    for step in range(depth):
        fetch(step).start()
    for step in range(steps):
        fetch(step).wait()
        out_ref[step * chunk : (step + 1) * chunk] = landing[step % depth].astype(BF)
        if step + depth < steps:
            fetch(step + depth).start()
    zero_ref[...] = after_ref[SPAN + 2 : SPAN + 3, :1]


def load_patterns(patterns, after):
    return pl.pallas_call(
        load_kernel,
        out_shape=[pltpu.VMEM(patterns.shape, BF), jax.ShapeDtypeStruct((1, 1), I32)],
        in_specs=[pl.BlockSpec(memory_space=pltpu.HBM), IN_VMEM],
        out_specs=[IN_VMEM, IN_VMEM],
        scratch_shapes=[pltpu.VMEM((4, 8, TILE, TILE), I32), pltpu.SemaphoreType.DMA((4,))],
        compiler_params=pltpu.CompilerParams(vmem_limit_bytes=VMEM_LIMIT),
        name="load_patterns",
    )(pltpu.with_memory_space_constraint(patterns, pltpu.HBM), *vmem(after))


def aggregate_kernel(late, counts, slots_ref, pat, *refs):
    pieces, refs = refs[: len(counts)], refs[len(counts) :]
    if late:
        first_ref, keep_ref, send_ref, parts, scales, acc = refs
    else:
        acc, parts, scales = refs
    start = slots_ref[3, 0] if late else 0
    stop = slots_ref[4, 0] if late else slots_ref[3, 0]
    groups = (stop - start + GROUP - 1) // GROUP

    acc[...] = first_ref[...] if late else jnp.zeros_like(acc)

    at = 0
    for piece, count in zip(pieces, counts):

        def decode(n, carry, piece=piece, at=at):
            base = pl.multiple_of(n * SHARD, 8)
            scale = power_of_two(piece[pl.ds(base + SPAN, 8), :])
            for half in range(2):
                words = piece[pl.ds(base + half * TILE, TILE), :]
                tile = (at + n) * 2 + half
                scales[tile] = jnp.broadcast_to(scale[half : half + 1], (8, LANES))
                for side, code in enumerate(two_codes(words)):
                    high = code.astype(BF)
                    low = (code - high.astype(F32)).astype(BF)
                    where = pl.ds(side * WORDS, WORDS)
                    parts[tile, :TILE, where] = high
                    parts[tile, TILE:, where] = low
            return carry

        lax.fori_loop(0, count, decode, 0)
        at += count

    def add_group(g, carry):
        for k in range(GROUP):
            n = start + g * GROUP + k
            at = jnp.minimum(n, pat.shape[0] - 1)
            row, col = slots_ref[0, at], jnp.where(n < stop, slots_ref[1, at], 0)
            p = pat[slots_ref[2, at]] * jnp.where(n < stop, scales[col], 0.0)[:1].astype(BF)
            acc[row] += jnp.dot(
                jnp.concatenate([p, p], axis=1), parts[col], preferred_element_type=F32
            )
        return carry

    lax.fori_loop(0, groups, add_group, 0)
    if late:
        keep_ref[...] = acc[: acc.shape[0] // 2]
        send_ref[...] = acc[acc.shape[0] // 2 :]


def aggregate(slots, pat, pieces, row_tiles, first=None):
    late = first is not None
    counts = tuple(piece.shape[0] // SHARD for piece in pieces)
    shards = sum(counts)
    sums = pltpu.VMEM((row_tiles, TILE, H), F32)
    half = pltpu.VMEM((row_tiles // 2, TILE, H), F32)
    operands = vmem(pat, *pieces, first) if late else vmem(pat, *pieces)
    return pl.pallas_call(
        functools.partial(aggregate_kernel, late, counts),
        out_shape=[half, half] if late else sums,
        in_specs=[pl.BlockSpec(memory_space=pltpu.SMEM)] + [IN_VMEM] * len(operands),
        out_specs=[IN_VMEM, IN_VMEM] if late else IN_VMEM,
        scratch_shapes=[
            pltpu.VMEM((shards * 2, 2 * TILE, H), BF),
            pltpu.VMEM((shards * 2, 8, LANES), F32),
        ]
        + [sums] * late,
        compiler_params=pltpu.CompilerParams(vmem_limit_bytes=VMEM_LIMIT),
        name="aggregate_late" if late else "aggregate_early",
    )(slots, *operands)


def pair_kernel(keep_ref, other_ref, own_ref, *pay_refs):
    tiles = SPAN // TILE
    for j in range(Y):
        at = pl.ds(j * tiles, tiles)
        both = (keep_ref[at] + other_ref[at]).reshape(SPAN, H)
        if j == 0:
            own_ref[...] = both
        else:
            encode(both, pay_refs[j - 1])


def add_pair(keep, other):
    return pl.pallas_call(
        pair_kernel,
        out_shape=[pltpu.VMEM((SPAN, H), F32)] + [pltpu.VMEM((SHARD, WORDS), I32)] * (Y - 1),
        in_specs=[IN_VMEM] * 2,
        out_specs=[IN_VMEM] * Y,
        compiler_params=pltpu.CompilerParams(vmem_limit_bytes=VMEM_LIMIT),
        name="add_pair",
    )(*vmem(keep, other))


def self_kernel(x_ref, w_ref, bias_ref, out_ref):
    w = w_ref[...]
    high = w.astype(BF)
    low = (w - high.astype(F32)).astype(BF)
    x = x_ref[...]
    z = jnp.dot(x, high, preferred_element_type=F32) + jnp.dot(x, low, preferred_element_type=F32)
    out_ref[...] = z + bias_ref[...]


def self_part(x, w, bias):
    return pl.pallas_call(
        self_kernel,
        out_shape=pltpu.VMEM((SPAN, H), F32),
        out_specs=IN_VMEM,
        compiler_params=pltpu.CompilerParams(vmem_limit_bytes=VMEM_LIMIT),
        name="self_part",
    )(x, w, bias)


def finish_kernel(own_ref, self_ref, count_ref, *refs):
    out_ref = refs[-1]
    for half in range(SPAN // TILE):
        at = pl.ds(half * TILE, TILE)
        left, right = own_ref[at, :WORDS], own_ref[at, WORDS:]
        for pay_ref in refs[:-1]:
            row = pay_ref[SPAN + half : SPAN + half + 1, :]
            scale = jnp.transpose(jnp.broadcast_to(power_of_two(row), (TILE, LANES)))
            a, b = two_codes(pay_ref[at, :])
            left, right = left + a * scale, right + b * scale
        d = jnp.transpose(jnp.broadcast_to(count_ref[half : half + 1].astype(F32), (TILE, LANES)))
        out_ref[at, :WORDS] = jnp.maximum(left / d + self_ref[at, :WORDS], 0.0)
        out_ref[at, WORDS:] = jnp.maximum(right / d + self_ref[at, WORDS:], 0.0)


def finish(own, self_rows, count, pays):
    return pl.pallas_call(
        finish_kernel,
        out_shape=jax.ShapeDtypeStruct((SPAN, H), F32),
        compiler_params=pltpu.CompilerParams(vmem_limit_bytes=VMEM_LIMIT),
        in_specs=[IN_VMEM] * (3 + len(pays)),
        name="finish",
    )(*vmem(own, self_rows), count, *vmem(*pays))


def from_far_z(x):
    return lax.ppermute(x, "row", [(((z + Z // 2) % Z) * X + k, z * X + k) for z in range(Z) for k in range(X)])


def from_step(x, step, x_core):
    pairs = []
    for z in range(Z):
        for k in range(X):
            for c in range(Y * CORES):
                if c % CORES == x_core:
                    source = z * X + (k + step) % X
                else:
                    source = ((z + (-step if step == 2 and z % 2 else step)) % Z) * X + k
                pairs.append((source * Y * CORES + c, (z * X + k) * Y * CORES + c))
    return lax.ppermute(x, ("row", "col"), pairs)


def from_y(x, d):
    return lax.ppermute(
        x, "col", [(((y + d) % Y) * CORES + k, y * CORES + k) for y in range(Y) for k in range(CORES)]
    )


def from_core(x):
    return lax.ppermute(x, "col", [(c ^ 1, c) for c in range(Y * CORES)])


def sort_slots(row, shard, half, live):
    index = jnp.arange(row.shape[0], dtype=I32)
    late = shard >= EARLY
    kind = jnp.where(index < live, late.astype(I32), 2)
    key = kind * row.shape[0] + index
    rank = jnp.sum(key[None, :] < key[:, None], axis=1)
    tile = jnp.where(late, shard - EARLY, shard) * 2 + half
    lists = jnp.stack([row, tile, index])
    spread = jnp.sum(jnp.where(rank[None, :] == index[:, None], lists[:, None, :], 0), axis=2)
    ends = jnp.stack([jnp.sum(kind == 0), live])
    return jnp.concatenate([spread, jnp.broadcast_to(ends[:, None], (2, row.shape[0]))])


def body(
    node_features, neighbour_count, tile_rows, tile_cols, tile_count, patterns, w_self, w_neigh, bias
):
    row_tiles = Y * CORES * SPAN // TILE
    mine = project(node_features, w_neigh)

    far = from_far_z(mine)
    line = jnp.concatenate([mine] + [from_step(mine, step, 0) for step in STEPS[1:]])
    across = [from_step(line, step, 1) for step in STEPS[1:]]
    zero_one, zero = load_patterns(patterns[0, 0], line)
    far_line = jnp.concatenate([far] + [from_step(far, step, 0) for step in STEPS[1:]]) + zero[0, 0]
    far_across = [from_step(far_line, step, 1) for step in STEPS[1:]]

    row_at, col_at = lax.axis_index("row"), lax.axis_index("col")
    z_at, x_at = row_at // X, row_at % X
    y_at, core_at = col_at // CORES, col_at % CORES
    cols = tile_cols[0, 0]
    source = cols // 2
    dz = (source // X - z_at) % Z
    dx = (source % X - x_at) % X
    x_place = jnp.where(dx == 3, 2, jnp.where(dx == 2, 3, dx))
    z_step = dz % 4
    z_place = jnp.where(z_step == 3, 2, jnp.where(z_step == 2, 3, z_step))
    first = jnp.where(z_place == 2, 7, jnp.where((z_place == 3) & (z_at % 2 == 1), 6, z_step))
    second = dz != first
    z_first = core_at == 1
    line_place, across_place = jnp.where(z_first, z_place, x_place), jnp.where(z_first, x_place, z_place)
    piece = jnp.where(across_place == 0, second.astype(I32), across_place + jnp.where(second, 4, 1))
    shard = piece * 4 + line_place
    rows = tile_rows[0, 0]
    span = rows // 2
    other = (span % CORES != core_at).astype(I32)
    row_index = other * (row_tiles // 2) + ((span // CORES - y_at) % Y) * 2 + rows % 2
    slots = sort_slots(row_index, shard, cols % 2, tile_count[0, 0])

    early = aggregate(slots, zero_one, [line, far_line, *across], row_tiles)
    keep, send = aggregate(slots, zero_one, far_across, row_tiles, early)

    own, *pays = add_pair(keep, from_core(send))
    pays = [from_y(pay, -j) for j, pay in enumerate(pays, 1)]
    self_rows = self_part(node_features, w_self, bias[None, :])
    return finish(own, self_rows, neighbour_count.reshape(SPAN // LANES, LANES), pays)


def solution(mesh):
    return jax.shard_map(
        body,
        mesh=mesh,
        in_specs=(
            P(("row", "col"), None),
            P(("row", "col")),
            P("row", "col", None),
            P("row", "col", None),
            P("row", "col"),
            P("row", "col", None, None, None),
            P(),
            P(),
            P(),
        ),
        out_specs=P(("row", "col"), None),
        check_vma=False,
    )
```

time: 99.7 us -> 75.2 us (0.75)
  waiting for transfers between devices: 28.3 us -> 21.3 us
  Pallas kernels: 19.9 us -> 14.3 us
  starting transfers between devices: 37.6 us -> 32.2 us
  other arithmetic: 8.05 us -> 4.04 us
  local copies, waits for them, and re-layouts: 4.24 us -> 2.23 us
    ppermute x17 -> x13, waiting for transfers between devices: 21.9 us -> 14.4 us  [the longest x12 11.6 us: from_step(): return lax.ppermute(x, ('row', 'col'), pairs)]
    convert_element_type x1 -> x0, other arithmetic: 6.46 us -> none  [body(): patterns[0, 0].astype(BF)]
    pallas_call x4 -> x6, Pallas kernels: 17.8 us -> 13.3 us  [the longest x2 6.51 us: aggregate(): pl.pallas_call(functools.partial(aggregate_kernel, late, counts), out_sha...]
    ppermute x17 -> x13, starting transfers between devices: 30.1 us -> 25.8 us  [the longest x12 19.5 us: from_step(): return lax.ppermute(x, ('row', 'col'), pairs)]
    reduce_sum x0 -> x3, other arithmetic: none -> 1.73 us  [the longest x1 1.41 us: sort_slots(): ends = jnp.stack([jnp.sum(kind == 0), live])]
    pallas_call x1, Pallas kernels: 2.17 us -> 0.95 us  [finish(): pl.pallas_call(finish_kernel, out_shape=jax.ShapeDtypeStruct((SPAN, H), F...]
    unnamed x41 -> x12, local copies, waits for them, and re-layouts: 3.34 us -> 2.15 us
    ppermute x3, starting transfers between devices: 7.42 us -> 6.39 us  [from_y(): lax.ppermute(x, 'col', [((y + d) % Y * CORES + k, y * CORES + k) for y in...]
  transfers between devices with their start and end apart: 21 -> 17, of which waited for: 6 -> 7; matrix products, arithmetic and copies ran while one was open for 9% -> 5% of each run, Pallas kernels for 2% -> 13%
where the time goes in v2:
time: 75.2 us; the launch traced here: 74.9 us
  starting transfers between devices  32.2 us (43%)
  waiting for transfers between devices  21.3 us (28%)
  Pallas kernels  14.3 us (19%)
  other arithmetic  4.04 us (5%)
  local copies, waits for them, and re-layouts  2.23 us (3%)
  between operations  0.83 us (1%)
    ppermute x12, starting transfers between devices, from_step(): return lax.ppermute(x, ('row', 'col'), pairs)  19.5 us
    ppermute x12, waiting for transfers between devices, from_step(): return lax.ppermute(x, ('row', 'col'), pairs)  11.6 us
    pallas_call x2, Pallas kernels, aggregate(): pl.pallas_call(functools.partial(aggregate_kernel, late, counts), out_sha...  6.51 us
    ppermute x3, starting transfers between devices, from_y(): lax.ppermute(x, 'col', [((y + d) % Y * CORES + k, y * CORES + k) for y in...  6.39 us
    ppermute x1, starting transfers between devices, from_far_z(): lax.ppermute(x, 'row', [((z + Z // 2) % Z * X + k, z * X + k) for z in ra...  6.3 us
    pallas_call x1, Pallas kernels, load_patterns(): pl.pallas_call(load_kernel, out_shape=[pltpu.VMEM(patterns.shape, BF), ja...  5.56 us
    ppermute x3, waiting for transfers between devices, from_y(): lax.ppermute(x, 'col', [((y + d) % Y * CORES + k, y * CORES + k) for y in...  4.27 us
    ppermute x1, waiting for transfers between devices, from_far_z(): lax.ppermute(x, 'row', [((z + Z // 2) % Z * X + k, z * X + k) for z in ra...  2.76 us
  transfers between devices with their start and end apart: 17, of which 7 were waited for; matrix products, arithmetic and copies ran while one was open for 5% of the time, Pallas kernels for 13%

profile of v2, /device:TPU:32, one launch (start us, length us, event | category | flops | bytes accessed | tf_op | source)
XLA Modules:
  0.0 74.9 jit_solution(15746941600717210983)
XLA Ops:
  0.0 0.0 copy-start
  0.0 1.0 %copy-done = bf16[256,768]{1,0:T(8,128)(2,1)S(1)} copy-done((bf16[256,768]{1,0:T(8,128)(2,1)S(1)}, bf16[256,768]{1,0:T(8,128)(2,1)}, u32[]{:S(2)}) %copy-start) | copy-done | bytes 393240
  1.0 0.0 copy-start.2
  1.0 1.1 %copy-done.2 = f32[768,256]{1,0:T(8,128)S(1)} copy-done((f32[768,256]{1,0:T(8,128)S(1)}, f32[768,256]{1,0:T(8,128)}, u32[]{:S(2)}) %copy-start.2) | copy-done | bytes 786456
  2.1 0.5 project.1
  2.6 2.8 %collective-permute-start = (s32[264,128]{1,0:T(8,128)S(1)}, s32[264,128]{1,0:T(8,128)S(1)}, u32[]{:S(2)}, u32[]{:S(2)}) collective-permute-start(s32[264,128]{1,0:T(8,128)S(1)} %project.1), channel_id=1, source_target_pairs={{8,0},{33,1},{10,2},{35,3},{12,4},{37,5},{14,6},{39,7},{16,8},{41,... | collective-permute-start | bytes 405512 | tf_op jit(solution)/shard_map/ppermute | solution.py:254
  5.5 0.0 collective-permute-start.1
  5.5 2.3 %collective-permute-start.2 = (s32[264,128]{1,0:T(8,128)S(1)}, s32[264,128]{1,0:T(8,128)S(1)}, u32[]{:S(2)}, u32[]{:S(2)}) collective-permute-start(s32[264,128]{1,0:T(8,128)S(1)} %project.1), channel_id=1, source_target_pairs={{16,0},{65,1},{18,2},{67,3},{20,4},{69,5},{22,6},{71,7},{24,8},{73... | collective-permute-start | bytes 405512 | tf_op jit(solution)/shard_map/ppermute | solution.py:254
  7.7 6.3 %collective-permute-start.3 = (s32[264,128]{1,0:T(8,128)S(1)}, s32[264,128]{1,0:T(8,128)S(1)}, u32[]{:S(2)}, u32[]{:S(2)}) collective-permute-start(s32[264,128]{1,0:T(8,128)S(1)} %project.1), channel_id=1, source_target_pairs={{128,0},{136,8},{144,16},{152,24},{160,32},{168,40},{176,48},{184,... | collective-permute-start | bytes 405512 | tf_op jit(solution)/shard_map/ppermute | solution.py:241
  14.7 1.4 %fusion.10 = (s32[]{:T(128)}, s32[128]{0:T(128)S(1)}) fusion(pred[]{:T(512)S(6)} %eq.176, s32[]{:T(128)S(6)} %select_n.443, s32[]{:T(128)S(6)} %select_n.438, s32[1,1,128]{2,1,0:T(1,128)} %param.12, pred[]{:T(512)S(6)} %eq.168, s32[]{:T(128)} %bitcast.48), kind=kLoop, calls=%fused_computation.90 | loop fusion | flops 12671 | bytes 1042 | tf_op jit(solution)/shard_map/reduce_sum | solution.py:276
  16.1 0.7 fusion
  16.8 0.0 collective-permute-done
  16.9 0.0 collective-permute-done.1
  16.9 0.0 collective-permute-done.2
  16.9 1.1 %collective-permute-start.10 = (s32[1056,128]{1,0:T(8,128)S(1)}, s32[1056,128]{1,0:T(8,128)S(1)}, u32[]{:S(2)}, u32[]{:S(2)}) collective-permute-start(s32[1056,128]{1,0:T(8,128)S(1)} %pad_add_fusion.after_ref.refs_0_), channel_id=1, source_target_pairs={{32,0},{9,1},{34,2},{11,3},{36,4},{13,5},{38,6},{15,7},{40,8},{17,... | collective-permute-start | bytes 1622024 | tf_op jit(solution)/shard_map/ppermute | solution.py:254
  18.0 2.8 %collective-permute-done.3 = s32[264,128]{1,0:T(8,128)S(1)} collective-permute-done((s32[264,128]{1,0:T(8,128)S(1)}, s32[264,128]{1,0:T(8,128)S(1)}, u32[]{:S(2)}, u32[]{:S(2)}) %collective-permute-start.3) | collective-permute-done | bytes 135200 | tf_op jit(solution)/shard_map/ppermute | solution.py:241
  20.8 0.3 collective-permute-start.4
  21.1 1.7 %collective-permute-start.5 = (s32[264,128]{1,0:T(8,128)S(1)}, s32[264,128]{1,0:T(8,128)S(1)}, u32[]{:S(2)}, u32[]{:S(2)}) collective-permute-start(s32[264,128]{1,0:T(8,128)S(1)} %collective-permute-done.3), channel_id=1, source_target_pairs={{24,0},{225,1},{26,2},{227,3},{28,4},{229,5},{30,6},{231,7},{0,8},... | collective-permute-start | bytes 405512 | tf_op jit(solution)/shard_map/ppermute | solution.py:254
  22.8 1.5 %collective-permute-start.6 = (s32[264,128]{1,0:T(8,128)S(1)}, s32[264,128]{1,0:T(8,128)S(1)}, u32[]{:S(2)}, u32[]{:S(2)}) collective-permute-start(s32[264,128]{1,0:T(8,128)S(1)} %collective-permute-done.3), channel_id=1, source_target_pairs={{16,0},{65,1},{18,2},{67,3},{20,4},{69,5},{22,6},{71,7},{24,8},{73... | collective-permute-start | bytes 405512 | tf_op jit(solution)/shard_map/ppermute | solution.py:254
  24.3 0.8 %pad_add_fusion.3 = s32[2]{0:T(128)S(1)} fusion(s32[1]{0:T(128)} %bitcast.49, s32[1]{0:T(128)} %bitcast.4), kind=kLoop, calls=%fused_computation.98 | loop fusion | flops 2 | bytes 16 | tf_op jit(solution)/shard_map/stack | solution.py:276
  25.1 0.1 pad.9.clone
  25.2 0.2 convert_reduce_fusion
  25.4 3.0 %collective-permute-start.11 = (s32[1056,128]{1,0:T(8,128)S(1)}, s32[1056,128]{1,0:T(8,128)S(1)}, u32[]{:S(2)}, u32[]{:S(2)}) collective-permute-start(s32[1056,128]{1,0:T(8,128)S(1)} %pad_add_fusion.after_ref.refs_0_), channel_id=1, source_target_pairs={{224,0},{25,1},{226,2},{27,3},{228,4},{29,5},{230,6},{31,7},{232,8... | collective-permute-start | bytes 1622024 | tf_op jit(solution)/shard_map/ppermute | solution.py:254
  28.3 5.6 %load_patterns.1 = (bf16[128,128,128]{2,1,0:T(8,128)(2,1)S(1)}, s32[1,1]{1,0:T(1,128)}) custom-call(s32[128,128,128]{2,1,0:T(8,128)} %bitcast.52, s32[1056,128]{1,0:T(8,128)S(1)} %pad_add_fusion.after_ref.refs_0_), custom_call_target="tpu_custom_call" | custom-call | tf_op jit(solution)/shard_map/load_patterns/pallas_call | solution.py:91
  33.9 0.0 collective-permute-done.4
  33.9 1.3 %collective-permute-start.12 = (s32[1056,128]{1,0:T(8,128)S(1)}, s32[1056,128]{1,0:T(8,128)S(1)}, u32[]{:S(2)}, u32[]{:S(2)}) collective-permute-start(s32[1056,128]{1,0:T(8,128)S(1)} %pad_add_fusion.after_ref.refs_0_), channel_id=1, source_target_pairs={{64,0},{17,1},{66,2},{19,3},{68,4},{21,5},{70,6},{23,7},{72,8},{25... | collective-permute-start | bytes 1622024 | tf_op jit(solution)/shard_map/ppermute | solution.py:254
  35.2 0.0 collective-permute-done.5
  35.2 0.0 collective-permute-done.6
  35.2 0.7 add_add_fusion.refs_1_
  35.9 1.1 %collective-permute-start.7 = (s32[1056,128]{1,0:T(8,128)S(1)}, s32[1056,128]{1,0:T(8,128)S(1)}, u32[]{:S(2)}, u32[]{:S(2)}) collective-permute-start(s32[1056,128]{1,0:T(8,128)S(1)} %add_add_fusion.refs_1_), channel_id=1, source_target_pairs={{32,0},{9,1},{34,2},{11,3},{36,4},{13,5},{38,6},{15,7},{40,8},{17,... | collective-permute-start | bytes 1622024 | tf_op jit(solution)/shard_map/ppermute | solution.py:254
  37.0 1.0 %collective-permute-start.8 = (s32[1056,128]{1,0:T(8,128)S(1)}, s32[1056,128]{1,0:T(8,128)S(1)}, u32[]{:S(2)}, u32[]{:S(2)}) collective-permute-start(s32[1056,128]{1,0:T(8,128)S(1)} %add_add_fusion.refs_1_), channel_id=1, source_target_pairs={{224,0},{25,1},{226,2},{27,3},{228,4},{29,5},{230,6},{31,7},{232,8... | collective-permute-start | bytes 1622024 | tf_op jit(solution)/shard_map/ppermute | solution.py:254
  38.0 0.0 collective-permute-done.10.refs_2_
  38.0 3.3 %collective-permute-start.9 = (s32[1056,128]{1,0:T(8,128)S(1)}, s32[1056,128]{1,0:T(8,128)S(1)}, u32[]{:S(2)}, u32[]{:S(2)}) collective-permute-start(s32[1056,128]{1,0:T(8,128)S(1)} %add_add_fusion.refs_1_), channel_id=1, source_target_pairs={{64,0},{17,1},{66,2},{19,3},{68,4},{21,5},{70,6},{23,7},{72,8},{25... | collective-permute-start | bytes 1622024 | tf_op jit(solution)/shard_map/ppermute | solution.py:254
  41.4 0.1 select_reduce_fusion
  41.5 0.1 pad_add_fusion.1.slots_ref
  41.6 0.0 collective-permute-done.11.refs_3_
  41.6 4.0 %collective-permute-done.12.refs_4_ = s32[1056,128]{1,0:T(8,128)S(1)} collective-permute-done((s32[1056,128]{1,0:T(8,128)S(1)}, s32[1056,128]{1,0:T(8,128)S(1)}, u32[]{:S(2)}, u32[]{:S(2)}) %collective-permute-start.12) | collective-permute-done | bytes 540704 | tf_op jit(solution)/shard_map/ppermute | solution.py:254
  45.6 3.8 %aggregate_early.1.refs_3_ = f32[16,128,256]{2,1,0:T(8,128)S(1)} custom-call(s32[5,128]{1,0:T(8,128)S(1)} %pad_add_fusion.1.slots_ref, bf16[128,128,128]{2,1,0:T(8,128)(2,1)S(1)} %get-tuple-element.13.pat, s32[1056,128]{1,0:T(8,128)S(1)} %pad_add_fusion.after_ref.refs_0_, s32[1056,128]{1,0:T(8,128)S(1)} %add_add_fusion.refs_1_, ...), custom_call_target="tpu_custom_call" | custom-call | tf_op jit(solution)/shard_map/aggregate_early/pallas_call | solution.py:159
  49.4 0.0 copy-start.1
  49.4 0.0 copy-start.3
  49.4 0.0 copy-start.4
  49.4 0.0 copy-start.5
  49.4 0.0 collective-permute-done.7.refs_0_
  49.4 1.8 %collective-permute-done.8.refs_1_ = s32[1056,128]{1,0:T(8,128)S(1)} collective-permute-done((s32[1056,128]{1,0:T(8,128)S(1)}, s32[1056,128]{1,0:T(8,128)S(1)}, u32[]{:S(2)}, u32[]{:S(2)}) %collective-permute-start.8) | collective-permute-done | bytes 540704 | tf_op jit(solution)/shard_map/ppermute | solution.py:254
  51.3 5.8 %collective-permute-done.9.refs_2_ = s32[1056,128]{1,0:T(8,128)S(1)} collective-permute-done((s32[1056,128]{1,0:T(8,128)S(1)}, s32[1056,128]{1,0:T(8,128)S(1)}, u32[]{:S(2)}, u32[]{:S(2)}) %collective-permute-start.9) | collective-permute-done | bytes 540704 | tf_op jit(solution)/shard_map/ppermute | solution.py:254
  57.1 2.7 %aggregate_late.1 = (f32[8,128,256]{2,1,0:T(8,128)S(1)}, f32[8,128,256]{2,1,0:T(8,128)S(1)}) custom-call(s32[5,128]{1,0:T(8,128)S(1)} %pad_add_fusion.1.slots_ref, bf16[128,128,128]{2,1,0:T(8,128)(2,1)S(1)} %get-tuple-element.13.pat, s32[1056,128]{1,0:T(8,128)S(1)} %collective-permute-done.7.refs_0_, s32[1056,128]{1,0:T(8,128)S(1)} %collective-permute-done.8.refs_1_, ...), custom_call_target="tpu_custom_call" | custom-call | tf_op jit(solution)/shard_map/aggregate_late/pallas_call | solution.py:159
  59.8 0.1 collective-permute-start.13
  59.9 2.6 %collective-permute-done.13.other_ref = f32[8,128,256]{2,1,0:T(8,128)S(1)} collective-permute-done((f32[8,128,256]{2,1,0:T(8,128)S(1)}, f32[8,128,256]{2,1,0:T(8,128)S(1)}, u32[]{:S(2)}, u32[]{:S(2)}) %collective-permute-start.13) | collective-permute-done | bytes 1048608 | tf_op jit(solution)/shard_map/ppermute | solution.py:264
  62.5 0.4 add_pair.1
  62.9 2.1 %collective-permute-start.14 = (s32[264,128]{1,0:T(8,128)S(1)}, s32[264,128]{1,0:T(8,128)S(1)}, u32[]{:S(2)}, u32[]{:S(2)}) collective-permute-start(s32[264,128]{1,0:T(8,128)S(1)} %get-tuple-element.18), channel_id=1, source_target_pairs={{6,0},{7,1},{0,2},{1,3},{2,4},{3,5},{4,6},{5,7},{14,8},{15,9},{8,1... | collective-permute-start | bytes 405512 | tf_op jit(solution)/shard_map/ppermute | solution.py:258
  65.1 2.4 %collective-permute-start.15 = (s32[264,128]{1,0:T(8,128)S(1)}, s32[264,128]{1,0:T(8,128)S(1)}, u32[]{:S(2)}, u32[]{:S(2)}) collective-permute-start(s32[264,128]{1,0:T(8,128)S(1)} %get-tuple-element.19), channel_id=1, source_target_pairs={{4,0},{5,1},{6,2},{7,3},{0,4},{1,5},{2,6},{3,7},{12,8},{13,9},{14,... | collective-permute-start | bytes 405512 | tf_op jit(solution)/shard_map/ppermute | solution.py:258
  67.5 1.8 %collective-permute-start.16 = (s32[264,128]{1,0:T(8,128)S(1)}, s32[264,128]{1,0:T(8,128)S(1)}, u32[]{:S(2)}, u32[]{:S(2)}) collective-permute-start(s32[264,128]{1,0:T(8,128)S(1)} %get-tuple-element.20), channel_id=1, source_target_pairs={{2,0},{3,1},{4,2},{5,3},{6,4},{7,5},{0,6},{1,7},{10,8},{11,9},{12,... | collective-permute-start | bytes 405512 | tf_op jit(solution)/shard_map/ppermute | solution.py:258
  69.3 0.0 copy-done.1
  69.3 0.0 copy-done.3
  69.3 0.0 copy-done.4
  69.3 0.4 self_part.1.self_ref
  69.7 0.2 collective-permute-done.14.refs_0_
  69.9 4.1 %collective-permute-done.15.refs_1_ = s32[264,128]{1,0:T(8,128)S(1)} collective-permute-done((s32[264,128]{1,0:T(8,128)S(1)}, s32[264,128]{1,0:T(8,128)S(1)}, u32[]{:S(2)}, u32[]{:S(2)}) %collective-permute-start.15) | collective-permute-done | bytes 135200 | tf_op jit(solution)/shard_map/ppermute | solution.py:258
  74.0 0.0 collective-permute-done.16.refs_2_
  74.0 0.0 copy-done.5
  74.0 0.9 %finish.1 = f32[256,256]{1,0:T(8,128)} custom-call(f32[256,256]{1,0:T(8,128)S(1)} %get-tuple-element.17.own_ref, f32[256,256]{1,0:T(8,128)S(1)} %self_part.1.self_ref, s32[2,128]{1,0:T(2,128)S(1)} %bitcast.51, s32[264,128]{1,0:T(8,128)S(1)} %collective-permute-done.14.refs_0_, s32[264,128]{1,0:T(8,128)S(1)} %collective-permute-done.15.refs_1_, ...), custom_call_target="tpu_custom_call" | custom-call | tf_op jit(solution)/shard_map/finish/pallas_call | solution.py:231
  (5 shorter events, 0.1 us)
Async XLA Ops:
  0.0 1.0 %copy-start = (bf16[256,768]{1,0:T(8,128)(2,1)S(1)}, bf16[256,768]{1,0:T(8,128)(2,1)}, u32[]{:S(2)}) copy-start(bf16[256,768]{1,0:T(8,128)(2,1)} %x_ref.3) | copy-start | bytes 1179652
  1.0 1.1 %copy-start.2 = (f32[768,256]{1,0:T(8,128)S(1)}, f32[768,256]{1,0:T(8,128)}, u32[]{:S(2)}) copy-start(f32[768,256]{1,0:T(8,128)} %w_ref.2) | copy-start | bytes 2359300
  2.6 14.2 %collective-permute-start = (s32[264,128]{1,0:T(8,128)S(1)}, s32[264,128]{1,0:T(8,128)S(1)}, u32[]{:S(2)}, u32[]{:S(2)}) collective-permute-start(s32[264,128]{1,0:T(8,128)S(1)} %project.1), channel_id=1, source_target_pairs={{8,0},{33,1},{10,2},{35,3},{12,4},{37,5},{14,6},{39,7},{16,8},{41,... | collective-permute-start | bytes 405512 | tf_op jit(solution)/shard_map/ppermute | solution.py:254
  5.5 11.4 %collective-permute-start.1 = (s32[264,128]{1,0:T(8,128)S(1)}, s32[264,128]{1,0:T(8,128)S(1)}, u32[]{:S(2)}, u32[]{:S(2)}) collective-permute-start(s32[264,128]{1,0:T(8,128)S(1)} %project.1), channel_id=1, source_target_pairs={{24,0},{225,1},{26,2},{227,3},{28,4},{229,5},{30,6},{231,7},{0,8},... | collective-permute-start | bytes 405512 | tf_op jit(solution)/shard_map/ppermute | solution.py:254
  5.5 11.4 %collective-permute-start.2 = (s32[264,128]{1,0:T(8,128)S(1)}, s32[264,128]{1,0:T(8,128)S(1)}, u32[]{:S(2)}, u32[]{:S(2)}) collective-permute-start(s32[264,128]{1,0:T(8,128)S(1)} %project.1), channel_id=1, source_target_pairs={{16,0},{65,1},{18,2},{67,3},{20,4},{69,5},{22,6},{71,7},{24,8},{73... | collective-permute-start | bytes 405512 | tf_op jit(solution)/shard_map/ppermute | solution.py:254
  7.7 13.0 %collective-permute-start.3 = (s32[264,128]{1,0:T(8,128)S(1)}, s32[264,128]{1,0:T(8,128)S(1)}, u32[]{:S(2)}, u32[]{:S(2)}) collective-permute-start(s32[264,128]{1,0:T(8,128)S(1)} %project.1), channel_id=1, source_target_pairs={{128,0},{136,8},{144,16},{152,24},{160,32},{168,40},{176,48},{184,... | collective-permute-start | bytes 405512 | tf_op jit(solution)/shard_map/ppermute | solution.py:241
  16.9 21.1 %collective-permute-start.10 = (s32[1056,128]{1,0:T(8,128)S(1)}, s32[1056,128]{1,0:T(8,128)S(1)}, u32[]{:S(2)}, u32[]{:S(2)}) collective-permute-start(s32[1056,128]{1,0:T(8,128)S(1)} %pad_add_fusion.after_ref.refs_0_), channel_id=1, source_target_pairs={{32,0},{9,1},{34,2},{11,3},{36,4},{13,5},{38,6},{15,7},{40,8},{17,... | collective-permute-start | bytes 1622024 | tf_op jit(solution)/shard_map/ppermute | solution.py:254
  20.8 13.1 %collective-permute-start.4 = (s32[264,128]{1,0:T(8,128)S(1)}, s32[264,128]{1,0:T(8,128)S(1)}, u32[]{:S(2)}, u32[]{:S(2)}) collective-permute-start(s32[264,128]{1,0:T(8,128)S(1)} %collective-permute-done.3), channel_id=1, source_target_pairs={{8,0},{33,1},{10,2},{35,3},{12,4},{37,5},{14,6},{39,7},{16,8},{41,... | collective-permute-start | bytes 405512 | tf_op jit(solution)/shard_map/ppermute | solution.py:254
  21.1 14.1 %collective-permute-start.5 = (s32[264,128]{1,0:T(8,128)S(1)}, s32[264,128]{1,0:T(8,128)S(1)}, u32[]{:S(2)}, u32[]{:S(2)}) collective-permute-start(s32[264,128]{1,0:T(8,128)S(1)} %collective-permute-done.3), channel_id=1, source_target_pairs={{24,0},{225,1},{26,2},{227,3},{28,4},{229,5},{30,6},{231,7},{0,8},... | collective-permute-start | bytes 405512 | tf_op jit(solution)/shard_map/ppermute | solution.py:254
  22.8 12.4 %collective-permute-start.6 = (s32[264,128]{1,0:T(8,128)S(1)}, s32[264,128]{1,0:T(8,128)S(1)}, u32[]{:S(2)}, u32[]{:S(2)}) collective-permute-start(s32[264,128]{1,0:T(8,128)S(1)} %collective-permute-done.3), channel_id=1, source_target_pairs={{16,0},{65,1},{18,2},{67,3},{20,4},{69,5},{22,6},{71,7},{24,8},{73... | collective-permute-start | bytes 405512 | tf_op jit(solution)/shard_map/ppermute | solution.py:254
  25.4 16.2 %collective-permute-start.11 = (s32[1056,128]{1,0:T(8,128)S(1)}, s32[1056,128]{1,0:T(8,128)S(1)}, u32[]{:S(2)}, u32[]{:S(2)}) collective-permute-start(s32[1056,128]{1,0:T(8,128)S(1)} %pad_add_fusion.after_ref.refs_0_), channel_id=1, source_target_pairs={{224,0},{25,1},{226,2},{27,3},{228,4},{29,5},{230,6},{31,7},{232,8... | collective-permute-start | bytes 1622024 | tf_op jit(solution)/shard_map/ppermute | solution.py:254
  33.9 11.6 %collective-permute-start.12 = (s32[1056,128]{1,0:T(8,128)S(1)}, s32[1056,128]{1,0:T(8,128)S(1)}, u32[]{:S(2)}, u32[]{:S(2)}) collective-permute-start(s32[1056,128]{1,0:T(8,128)S(1)} %pad_add_fusion.after_ref.refs_0_), channel_id=1, source_target_pairs={{64,0},{17,1},{66,2},{19,3},{68,4},{21,5},{70,6},{23,7},{72,8},{25... | collective-permute-start | bytes 1622024 | tf_op jit(solution)/shard_map/ppermute | solution.py:254
  35.9 13.5 %collective-permute-start.7 = (s32[1056,128]{1,0:T(8,128)S(1)}, s32[1056,128]{1,0:T(8,128)S(1)}, u32[]{:S(2)}, u32[]{:S(2)}) collective-permute-start(s32[1056,128]{1,0:T(8,128)S(1)} %add_add_fusion.refs_1_), channel_id=1, source_target_pairs={{32,0},{9,1},{34,2},{11,3},{36,4},{13,5},{38,6},{15,7},{40,8},{17,... | collective-permute-start | bytes 1622024 | tf_op jit(solution)/shard_map/ppermute | solution.py:254
  37.0 14.2 %collective-permute-start.8 = (s32[1056,128]{1,0:T(8,128)S(1)}, s32[1056,128]{1,0:T(8,128)S(1)}, u32[]{:S(2)}, u32[]{:S(2)}) collective-permute-start(s32[1056,128]{1,0:T(8,128)S(1)} %add_add_fusion.refs_1_), channel_id=1, source_target_pairs={{224,0},{25,1},{226,2},{27,3},{228,4},{29,5},{230,6},{31,7},{232,8... | collective-permute-start | bytes 1622024 | tf_op jit(solution)/shard_map/ppermute | solution.py:254
  38.0 19.1 %collective-permute-start.9 = (s32[1056,128]{1,0:T(8,128)S(1)}, s32[1056,128]{1,0:T(8,128)S(1)}, u32[]{:S(2)}, u32[]{:S(2)}) collective-permute-start(s32[1056,128]{1,0:T(8,128)S(1)} %add_add_fusion.refs_1_), channel_id=1, source_target_pairs={{64,0},{17,1},{66,2},{19,3},{68,4},{21,5},{70,6},{23,7},{72,8},{25... | collective-permute-start | bytes 1622024 | tf_op jit(solution)/shard_map/ppermute | solution.py:254
  49.4 19.9 %copy-start.1 = (bf16[256,768]{1,0:T(8,128)(2,1)S(1)}, bf16[256,768]{1,0:T(8,128)(2,1)}, u32[]{:S(2)}) copy-start(bf16[256,768]{1,0:T(8,128)(2,1)} %x_ref.3) | copy-start | bytes 1179652
  49.4 19.9 %copy-start.3 = (f32[768,256]{1,0:T(8,128)S(1)}, f32[768,256]{1,0:T(8,128)}, u32[]{:S(2)}) copy-start(f32[768,256]{1,0:T(8,128)} %w_ref.3) | copy-start | bytes 2359300
  49.4 19.9 %copy-start.4 = (f32[256]{0:T(256)S(1)}, f32[256]{0:T(256)}, u32[]{:S(2)}) copy-start(f32[256]{0:T(256)} %param.17) | copy-start | bytes 3076
  49.4 24.6 %copy-start.5 = (s32[256]{0:T(256)S(1)}, s32[256]{0:T(256)}, u32[]{:S(2)}) copy-start(s32[256]{0:T(256)} %param.10) | copy-start | bytes 3076
  59.8 2.7 %collective-permute-start.13 = (f32[8,128,256]{2,1,0:T(8,128)S(1)}, f32[8,128,256]{2,1,0:T(8,128)S(1)}, u32[]{:S(2)}, u32[]{:S(2)}) collective-permute-start(f32[8,128,256]{2,1,0:T(8,128)S(1)} %get-tuple-element.16), channel_id=1, source_target_pairs={{1,0},{0,1},{3,2},{2,3},{5,4},{4,5},{7,6},{6,7},{9,8},{8,9},{11,10... | collective-permute-start | bytes 3145736 | tf_op jit(solution)/shard_map/ppermute | solution.py:264
  62.9 7.0 %collective-permute-start.14 = (s32[264,128]{1,0:T(8,128)S(1)}, s32[264,128]{1,0:T(8,128)S(1)}, u32[]{:S(2)}, u32[]{:S(2)}) collective-permute-start(s32[264,128]{1,0:T(8,128)S(1)} %get-tuple-element.18), channel_id=1, source_target_pairs={{6,0},{7,1},{0,2},{1,3},{2,4},{3,5},{4,6},{5,7},{14,8},{15,9},{8,1... | collective-permute-start | bytes 405512 | tf_op jit(solution)/shard_map/ppermute | solution.py:258
  65.1 8.9 %collective-permute-start.15 = (s32[264,128]{1,0:T(8,128)S(1)}, s32[264,128]{1,0:T(8,128)S(1)}, u32[]{:S(2)}, u32[]{:S(2)}) collective-permute-start(s32[264,128]{1,0:T(8,128)S(1)} %get-tuple-element.19), channel_id=1, source_target_pairs={{4,0},{5,1},{6,2},{7,3},{0,4},{1,5},{2,6},{3,7},{12,8},{13,9},{14,... | collective-permute-start | bytes 405512 | tf_op jit(solution)/shard_map/ppermute | solution.py:258
  67.5 6.5 %collective-permute-start.16 = (s32[264,128]{1,0:T(8,128)S(1)}, s32[264,128]{1,0:T(8,128)S(1)}, u32[]{:S(2)}, u32[]{:S(2)}) collective-permute-start(s32[264,128]{1,0:T(8,128)S(1)} %get-tuple-element.20), channel_id=1, source_target_pairs={{2,0},{3,1},{4,2},{5,3},{6,4},{7,5},{0,6},{1,7},{10,8},{11,9},{12,... | collective-permute-start | bytes 405512 | tf_op jit(solution)/shard_map/ppermute | solution.py:258

commit v3 on v2

--- a/solution.py
+++ b/solution.py
@@ -15,6 +15,7 @@
 WORDS = H // 2
 SHARD = SPAN + 8
 GROUP = 16
+CHUNKS = 3
 EARLY = 20
 STEPS = (0, 1, -1, 2)
 VMEM_LIMIT = 20 * 1024 * 1024
@@ -51,12 +52,25 @@
 IN_VMEM = pl.BlockSpec(memory_space=pltpu.VMEM)
 
 
-def project_kernel(x_ref, w_ref, out_ref):
-    w = w_ref[...]
-    high = w.astype(BF)
-    low = (w - high.astype(F32)).astype(BF)
-    x = x_ref[...]
-    z = jnp.dot(x, high, preferred_element_type=F32) + jnp.dot(x, low, preferred_element_type=F32)
+def project_kernel(x_hbm, w_hbm, out_ref, x_ref, w_ref, sem):
+    chunk = x_ref.shape[1] // CHUNKS
+    copies = []
+    for n in range(CHUNKS):
+        at = pl.ds(n * chunk, chunk)
+        copies.append(pltpu.make_async_copy(w_hbm.at[at], w_ref.at[at], sem.at[n]))
+        copies.append(pltpu.make_async_copy(x_hbm.at[:, at], x_ref.at[:, at], sem.at[CHUNKS + n]))
+    for copy in copies:
+        copy.start()
+    z = jnp.zeros((SPAN, H), F32)
+    for n in range(CHUNKS):
+        copies[2 * n].wait()
+        copies[2 * n + 1].wait()
+        at = slice(n * chunk, (n + 1) * chunk)
+        w = w_ref[at]
+        high = w.astype(BF)
+        low = (w - high.astype(F32)).astype(BF)
+        x = x_ref[:, at]
+        z += jnp.dot(x, high, preferred_element_type=F32) + jnp.dot(x, low, preferred_element_type=F32)
     encode(z, out_ref)
 
 
@@ -64,12 +78,33 @@
     return pl.pallas_call(
         project_kernel,
         out_shape=pltpu.VMEM((SHARD, WORDS), I32),
+        in_specs=[pl.BlockSpec(memory_space=pltpu.HBM)] * 2,
+        out_specs=IN_VMEM,
+        scratch_shapes=[
+            pltpu.VMEM(x.shape, x.dtype),
+            pltpu.VMEM(w.shape, w.dtype),
+            pltpu.SemaphoreType.DMA((2 * CHUNKS,)),
+        ],
         compiler_params=pltpu.CompilerParams(vmem_limit_bytes=VMEM_LIMIT),
         name="project",
-    )(x, w)
-
-
-def load_kernel(pat_hbm, after_ref, out_ref, zero_ref, landing, sem):
+    )(*[pltpu.with_memory_space_constraint(array, pltpu.HBM) for array in (x, w)])
+
+
+def zero_kernel(after_ref, zero_ref):
+    zero_ref[...] = after_ref[SPAN + 2 : SPAN + 3, :1]
+
+
+def zero_after(blocks):
+    return pl.pallas_call(
+        zero_kernel,
+        out_shape=pltpu.VMEM((1, 1), I32),
+        in_specs=[IN_VMEM],
+        out_specs=IN_VMEM,
+        name="zero_after",
+    )(*vmem(blocks))
+
+
+def load_kernel(pat_hbm, after_ref, out_ref, landing, sem):
     chunk, depth = landing.shape[1], landing.shape[0]
     steps = pat_hbm.shape[0] // chunk
 
@@ -84,16 +119,15 @@
         out_ref[step * chunk : (step + 1) * chunk] = landing[step % depth].astype(BF)
         if step + depth < steps:
             fetch(step + depth).start()
-    zero_ref[...] = after_ref[SPAN + 2 : SPAN + 3, :1]
 
 
 def load_patterns(patterns, after):
     return pl.pallas_call(
         load_kernel,
-        out_shape=[pltpu.VMEM(patterns.shape, BF), jax.ShapeDtypeStruct((1, 1), I32)],
+        out_shape=pltpu.VMEM(patterns.shape, BF),
         in_specs=[pl.BlockSpec(memory_space=pltpu.HBM), IN_VMEM],
-        out_specs=[IN_VMEM, IN_VMEM],
-        scratch_shapes=[pltpu.VMEM((4, 8, TILE, TILE), I32), pltpu.SemaphoreType.DMA((4,))],
+        out_specs=IN_VMEM,
+        scratch_shapes=[pltpu.VMEM((8, 8, TILE, TILE), I32), pltpu.SemaphoreType.DMA((8,))],
         compiler_params=pltpu.CompilerParams(vmem_limit_bytes=VMEM_LIMIT),
         name="load_patterns",
     )(pltpu.with_memory_space_constraint(patterns, pltpu.HBM), *vmem(after))
@@ -283,17 +317,18 @@
     row_tiles = Y * CORES * SPAN // TILE
     mine = project(node_features, w_neigh)
 
+    line = jnp.concatenate([mine] + [from_step(mine, step, 0) for step in STEPS[1:]])
     far = from_far_z(mine)
-    line = jnp.concatenate([mine] + [from_step(mine, step, 0) for step in STEPS[1:]])
     across = [from_step(line, step, 1) for step in STEPS[1:]]
-    zero_one, zero = load_patterns(patterns[0, 0], line)
+    zero = zero_after(line)
     far_line = jnp.concatenate([far] + [from_step(far, step, 0) for step in STEPS[1:]]) + zero[0, 0]
     far_across = [from_step(far_line, step, 1) for step in STEPS[1:]]
+    zero_one = load_patterns(patterns[0, 0], far_line)
 
     row_at, col_at = lax.axis_index("row"), lax.axis_index("col")
     z_at, x_at = row_at // X, row_at % X
     y_at, core_at = col_at // CORES, col_at % CORES
-    cols = tile_cols[0, 0]
+    cols = tile_cols[0, 0] + far_line[-1, -1]
     source = cols // 2
     dz = (source // X - z_at) % Z
     dx = (source % X - x_at) % X
@@ -316,7 +351,7 @@
     keep, send = aggregate(slots, zero_one, far_across, row_tiles, early)
 
     own, *pays = add_pair(keep, from_core(send))
-    pays = [from_y(pay, -j) for j, pay in enumerate(pays, 1)]
+    pays = [from_y(pays[j - 1], -j) for j in (2, 1, 3)]
     self_rows = self_part(node_features, w_self, bias[None, :])
     return finish(own, self_rows, neighbour_count.reshape(SPAN // LANES, LANES), pays)
 

time: 75.2 us -> 69.9 us (0.930)
  waiting for transfers between devices: 21.3 us -> 13 us
  starting transfers between devices: 32.2 us -> 35.9 us
  local copies, waits for them, and re-layouts: 2.23 us -> 0.69 us
  other arithmetic: 4.04 us -> 5.07 us
    ppermute x12, waiting for transfers between devices: 11.6 us -> 5.61 us  [from_step(): return lax.ppermute(x, ('row', 'col'), pairs)]
    ppermute x12, starting transfers between devices: 19.5 us -> 22.4 us  [from_step(): return lax.ppermute(x, ('row', 'col'), pairs)]
    unnamed x12 -> x8, local copies, waits for them, and re-layouts: 2.15 us -> 0.03 us
    ppermute x1, waiting for transfers between devices: 2.76 us -> 1.16 us  [from_far_z(): lax.ppermute(x, 'row', [((z + Z // 2) % Z * X + k, z * X + k) for z in ra...]
    pallas_call x1 -> x2, Pallas kernels: 5.56 us -> 4.2 us  [the longest x1 3.69 us: load_patterns(): pl.pallas_call(load_kernel, out_shape=pltpu.VMEM(patterns.shape, BF), in_...]
    pallas_call x1, Pallas kernels: 0.51 us -> 1.87 us  [project(): pl.pallas_call(project_kernel, out_shape=pltpu.VMEM((SHARD, WORDS), I32),...]
  transfers between devices with their start and end apart: 17 -> 17, of which waited for: 7 -> 6; matrix products, arithmetic and copies ran while one was open for 5% -> 8% of each run, Pallas kernels for 13% -> 12%
where the time goes in v3:
time: 69.9 us; the launch traced here: 69.7 us
  starting transfers between devices  35.9 us (51%)
  Pallas kernels  14.3 us (20%)
  waiting for transfers between devices  13 us (19%)
  other arithmetic  5.07 us (7%)
  between operations  0.83 us (1%)
    ppermute x12, starting transfers between devices, from_step(): return lax.ppermute(x, ('row', 'col'), pairs)  22.4 us
    ppermute x3, starting transfers between devices, from_y(): lax.ppermute(x, 'col', [((y + d) % Y * CORES + k, y * CORES + k) for y in...  6.99 us
    pallas_call x2, Pallas kernels, aggregate(): pl.pallas_call(functools.partial(aggregate_kernel, late, counts), out_sha...  6.53 us
    ppermute x1, starting transfers between devices, from_far_z(): lax.ppermute(x, 'row', [((z + Z // 2) % Z * X + k, z * X + k) for z in ra...  6.38 us
    ppermute x12, waiting for transfers between devices, from_step(): return lax.ppermute(x, ('row', 'col'), pairs)  5.61 us
    pallas_call x1, Pallas kernels, load_patterns(): pl.pallas_call(load_kernel, out_shape=pltpu.VMEM(patterns.shape, BF), in_...  3.69 us
    ppermute x3, waiting for transfers between devices, from_y(): lax.ppermute(x, 'col', [((y + d) % Y * CORES + k, y * CORES + k) for y in...  3.54 us
    ppermute x1, waiting for transfers between devices, from_core(): return lax.ppermute(x, 'col', [(c ^ 1, c) for c in range(Y * CORES)])  2.65 us
  transfers between devices with their start and end apart: 17, of which 6 were waited for; matrix products, arithmetic and copies ran while one was open for 8% of the time, Pallas kernels for 12%

profile of v3, /device:TPU:32, one launch (start us, length us, event | category | flops | bytes accessed | tf_op | source)
XLA Modules:
  0.0 69.7 jit_solution(10053406921306402490)
XLA Ops:
  0.0 1.9 %project.1 = s32[264,128]{1,0:T(8,128)S(1)} custom-call(bf16[256,768]{1,0:T(8,128)(2,1)} %x_ref.1, f32[768,256]{1,0:T(8,128)} %w_hbm.1), custom_call_target="tpu_custom_call" | custom-call | tf_op jit(solution)/shard_map/project/pallas_call | solution.py:78
  1.9 6.4 %collective-permute-start = (s32[264,128]{1,0:T(8,128)S(1)}, s32[264,128]{1,0:T(8,128)S(1)}, u32[]{:S(2)}, u32[]{:S(2)}) collective-permute-start(s32[264,128]{1,0:T(8,128)S(1)} %project.1), channel_id=1, source_target_pairs={{128,0},{136,8},{144,16},{152,24},{160,32},{168,40},{176,48},{184,... | collective-permute-start | bytes 405512 | tf_op jit(solution)/shard_map/ppermute | solution.py:275
  8.3 2.8 %collective-permute-start.4 = (s32[264,128]{1,0:T(8,128)S(1)}, s32[264,128]{1,0:T(8,128)S(1)}, u32[]{:S(2)}, u32[]{:S(2)}) collective-permute-start(s32[264,128]{1,0:T(8,128)S(1)} %project.1), channel_id=1, source_target_pairs={{8,0},{33,1},{10,2},{35,3},{12,4},{37,5},{14,6},{39,7},{16,8},{41,... | collective-permute-start | bytes 405512 | tf_op jit(solution)/shard_map/ppermute | solution.py:288
  11.0 0.0 collective-permute-start.5
  11.0 2.3 %collective-permute-start.6 = (s32[264,128]{1,0:T(8,128)S(1)}, s32[264,128]{1,0:T(8,128)S(1)}, u32[]{:S(2)}, u32[]{:S(2)}) collective-permute-start(s32[264,128]{1,0:T(8,128)S(1)} %project.1), channel_id=1, source_target_pairs={{16,0},{65,1},{18,2},{67,3},{20,4},{69,5},{22,6},{71,7},{24,8},{73... | collective-permute-start | bytes 405512 | tf_op jit(solution)/shard_map/ppermute | solution.py:288
  14.0 1.2 %collective-permute-done = s32[264,128]{1,0:T(8,128)S(1)} collective-permute-done((s32[264,128]{1,0:T(8,128)S(1)}, s32[264,128]{1,0:T(8,128)S(1)}, u32[]{:S(2)}, u32[]{:S(2)}) %collective-permute-start) | collective-permute-done | bytes 135200 | tf_op jit(solution)/shard_map/ppermute | solution.py:275
  15.1 2.8 %collective-permute-start.1 = (s32[264,128]{1,0:T(8,128)S(1)}, s32[264,128]{1,0:T(8,128)S(1)}, u32[]{:S(2)}, u32[]{:S(2)}) collective-permute-start(s32[264,128]{1,0:T(8,128)S(1)} %collective-permute-done), channel_id=1, source_target_pairs={{8,0},{33,1},{10,2},{35,3},{12,4},{37,5},{14,6},{39,7},{16,8},{41,... | collective-permute-start | bytes 405512 | tf_op jit(solution)/shard_map/ppermute | solution.py:288
  17.9 0.0 collective-permute-start.2
  17.9 0.0 collective-permute-done.4
  17.9 2.3 %collective-permute-start.3 = (s32[264,128]{1,0:T(8,128)S(1)}, s32[264,128]{1,0:T(8,128)S(1)}, u32[]{:S(2)}, u32[]{:S(2)}) collective-permute-start(s32[264,128]{1,0:T(8,128)S(1)} %collective-permute-done), channel_id=1, source_target_pairs={{16,0},{65,1},{18,2},{67,3},{20,4},{69,5},{22,6},{71,7},{24,8},{73... | collective-permute-start | bytes 405512 | tf_op jit(solution)/shard_map/ppermute | solution.py:288
  20.2 0.0 collective-permute-done.5
  20.2 0.0 collective-permute-done.6
  20.2 0.5 zero_after.1
  20.7 0.0 collective-permute-start.10
  20.7 3.2 %collective-permute-start.11 = (s32[1056,128]{1,0:T(8,128)S(1)}, s32[1056,128]{1,0:T(8,128)S(1)}, u32[]{:S(2)}, u32[]{:S(2)}) collective-permute-start(s32[1056,128]{1,0:T(8,128)S(1)} %pad_add_fusion.after_ref.refs_0_), channel_id=1, source_target_pairs={{224,0},{25,1},{226,2},{27,3},{228,4},{29,5},{230,6},{31,7},{232,8... | collective-permute-start | bytes 1622024 | tf_op jit(solution)/shard_map/ppermute | solution.py:288
  24.0 0.0 collective-permute-done.1
  24.0 2.4 %collective-permute-start.12 = (s32[1056,128]{1,0:T(8,128)S(1)}, s32[1056,128]{1,0:T(8,128)S(1)}, u32[]{:S(2)}, u32[]{:S(2)}) collective-permute-start(s32[1056,128]{1,0:T(8,128)S(1)} %pad_add_fusion.after_ref.refs_0_), channel_id=1, source_target_pairs={{64,0},{17,1},{66,2},{19,3},{68,4},{21,5},{70,6},{23,7},{72,8},{25... | collective-permute-start | bytes 1622024 | tf_op jit(solution)/shard_map/ppermute | solution.py:288
  26.3 0.0 collective-permute-done.2
  26.3 0.0 collective-permute-done.3
  26.3 0.7 add_add_fusion.after_ref.refs_1_
  27.0 0.6 slice.4
  27.6 2.8 %collective-permute-start.7 = (s32[1056,128]{1,0:T(8,128)S(1)}, s32[1056,128]{1,0:T(8,128)S(1)}, u32[]{:S(2)}, u32[]{:S(2)}) collective-permute-start(s32[1056,128]{1,0:T(8,128)S(1)} %add_add_fusion.after_ref.refs_1_), channel_id=1, source_target_pairs={{32,0},{9,1},{34,2},{11,3},{36,4},{13,5},{38,6},{15,7},{40,8},{17,... | collective-permute-start | bytes 1622024 | tf_op jit(solution)/shard_map/ppermute | solution.py:288
  30.4 0.2 collective-permute-start.8
  30.6 1.9 %fusion.10 = (s32[]{:T(128)}, s32[128]{0:T(128)S(1)}) fusion(pred[]{:T(512)S(6)} %eq.176, s32[]{:T(128)S(6)} %select_n.443, s32[]{:T(128)S(6)} %select_n.438, s32[1,1,128]{2,1,0:T(1,128)} %param.12, s32[]{:T(128)} %bitcast.2, pred[]{:T(512)S(6)} %eq.168, s32[]{:T(128)} %bitcast.49), kind=kLoop, calls=%fused_computation.90 | loop fusion | flops 12799 | bytes 1046 | tf_op jit(solution)/shard_map/reduce_sum | solution.py:310
  32.6 1.4 %fusion = (s32[1,128]{1,0:T(1,128)S(1)}, s32[1,128]{1,0:T(1,128)S(1)}) fusion(s32[1,1,128]{2,1,0:T(1,128)} %param.11, s32[]{:T(128)S(6)} %select_n.459, s32[]{:T(128)S(6)} %select_n.434, pred[]{:T(512)S(6)} %eq.176, s32[]{:T(128)S(6)} %select_n.443, s32[]{:T(128)S(6)} %select_n.438, s32[1,1,128]{2,1,0:T(1,128)} %param.12, s32[]{:T(128)} %bitcast.2, pred[]{:T(512)S(6)} %eq.168), kind=kLoop, calls=%fused_computation.80 | loop fusion | flops 20096 | bytes 2070 | tf_op jit(solution)/shard_map/add | solution.py:347
  34.0 0.6 pad_add_fusion.3
  34.6 0.1 pad.1.clone
  34.6 3.7 %load_patterns.1.pat = bf16[128,128,128]{2,1,0:T(8,128)(2,1)S(1)} custom-call(s32[128,128,128]{2,1,0:T(8,128)} %bitcast.53, s32[1056,128]{1,0:T(8,128)S(1)} %add_add_fusion.after_ref.refs_1_), custom_call_target="tpu_custom_call" | custom-call | tf_op jit(solution)/shard_map/load_patterns/pallas_call | solution.py:125
  38.4 0.2 convert_reduce_fusion
  38.6 0.0 collective-permute-done.10.refs_2_
  38.6 3.7 %collective-permute-start.9 = (s32[1056,128]{1,0:T(8,128)S(1)}, s32[1056,128]{1,0:T(8,128)S(1)}, u32[]{:S(2)}, u32[]{:S(2)}) collective-permute-start(s32[1056,128]{1,0:T(8,128)S(1)} %add_add_fusion.after_ref.refs_1_), channel_id=1, source_target_pairs={{64,0},{17,1},{66,2},{19,3},{68,4},{21,5},{70,6},{23,7},{72,8},{25... | collective-permute-start | bytes 1622024 | tf_op jit(solution)/shard_map/ppermute | solution.py:288
  42.3 0.1 select_reduce_fusion
  42.5 0.1 pad_add_fusion.1.slots_ref
  42.5 0.0 collective-permute-done.11.refs_3_
  42.5 0.0 collective-permute-done.12.refs_4_
  42.5 3.8 %aggregate_early.1.refs_3_ = f32[16,128,256]{2,1,0:T(8,128)S(1)} custom-call(s32[5,128]{1,0:T(8,128)S(1)} %pad_add_fusion.1.slots_ref, bf16[128,128,128]{2,1,0:T(8,128)(2,1)S(1)} %load_patterns.1.pat, s32[1056,128]{1,0:T(8,128)S(1)} %pad_add_fusion.after_ref.refs_0_, s32[1056,128]{1,0:T(8,128)S(1)} %add_add_fusion.after_ref.refs_1_, ...), custom_call_target="tpu_custom_call" | custom-call | tf_op jit(solution)/shard_map/aggregate_early/pallas_call | solution.py:193
  46.4 0.0 copy-start
  46.4 0.0 copy-start.1
  46.4 0.0 copy-start.2
  46.4 0.0 copy-start.3
  46.4 0.0 collective-permute-done.7.refs_0_
  46.4 0.0 collective-permute-done.8.refs_1_
  46.5 5.6 %collective-permute-done.9.refs_2_ = s32[1056,128]{1,0:T(8,128)S(1)} collective-permute-done((s32[1056,128]{1,0:T(8,128)S(1)}, s32[1056,128]{1,0:T(8,128)S(1)}, u32[]{:S(2)}, u32[]{:S(2)}) %collective-permute-start.9) | collective-permute-done | bytes 540704 | tf_op jit(solution)/shard_map/ppermute | solution.py:288
  52.0 2.7 %aggregate_late.1 = (f32[8,128,256]{2,1,0:T(8,128)S(1)}, f32[8,128,256]{2,1,0:T(8,128)S(1)}) custom-call(s32[5,128]{1,0:T(8,128)S(1)} %pad_add_fusion.1.slots_ref, bf16[128,128,128]{2,1,0:T(8,128)(2,1)S(1)} %load_patterns.1.pat, s32[1056,128]{1,0:T(8,128)S(1)} %collective-permute-done.7.refs_0_, s32[1056,128]{1,0:T(8,128)S(1)} %collective-permute-done.8.refs_1_, ...), custom_call_target="tpu_custom_call" | custom-call | tf_op jit(solution)/shard_map/aggregate_late/pallas_call | solution.py:193
  54.7 0.1 collective-permute-start.13
  54.8 2.6 %collective-permute-done.13.other_ref = f32[8,128,256]{2,1,0:T(8,128)S(1)} collective-permute-done((f32[8,128,256]{2,1,0:T(8,128)S(1)}, f32[8,128,256]{2,1,0:T(8,128)S(1)}, u32[]{:S(2)}, u32[]{:S(2)}) %collective-permute-start.13) | collective-permute-done | bytes 1048608 | tf_op jit(solution)/shard_map/ppermute | solution.py:298
  57.5 0.4 add_pair.1
  57.9 3.8 %collective-permute-start.14 = (s32[264,128]{1,0:T(8,128)S(1)}, s32[264,128]{1,0:T(8,128)S(1)}, u32[]{:S(2)}, u32[]{:S(2)}) collective-permute-start(s32[264,128]{1,0:T(8,128)S(1)} %get-tuple-element.14), channel_id=1, source_target_pairs={{4,0},{5,1},{6,2},{7,3},{0,4},{1,5},{2,6},{3,7},{12,8},{13,9},{14,... | collective-permute-start | bytes 405512 | tf_op jit(solution)/shard_map/ppermute | solution.py:292
  61.6 0.7 collective-permute-start.15
  62.3 2.6 %collective-permute-start.16 = (s32[264,128]{1,0:T(8,128)S(1)}, s32[264,128]{1,0:T(8,128)S(1)}, u32[]{:S(2)}, u32[]{:S(2)}) collective-permute-start(s32[264,128]{1,0:T(8,128)S(1)} %get-tuple-element.16), channel_id=1, source_target_pairs={{2,0},{3,1},{4,2},{5,3},{6,4},{7,5},{0,6},{1,7},{10,8},{11,9},{12,... | collective-permute-start | bytes 405512 | tf_op jit(solution)/shard_map/ppermute | solution.py:292
  64.9 0.0 copy-done
  64.9 0.0 copy-done.1
  64.9 0.0 copy-done.2
  64.9 0.4 self_part.1.self_ref
  65.2 0.7 %collective-permute-done.14.refs_0_ = s32[264,128]{1,0:T(8,128)S(1)} collective-permute-done((s32[264,128]{1,0:T(8,128)S(1)}, s32[264,128]{1,0:T(8,128)S(1)}, u32[]{:S(2)}, u32[]{:S(2)}) %collective-permute-start.14) | collective-permute-done | bytes 135200 | tf_op jit(solution)/shard_map/ppermute | solution.py:292
  66.0 2.5 %collective-permute-done.15.refs_1_ = s32[264,128]{1,0:T(8,128)S(1)} collective-permute-done((s32[264,128]{1,0:T(8,128)S(1)}, s32[264,128]{1,0:T(8,128)S(1)}, u32[]{:S(2)}, u32[]{:S(2)}) %collective-permute-start.15) | collective-permute-done | bytes 135200 | tf_op jit(solution)/shard_map/ppermute | solution.py:292
  68.5 0.3 collective-permute-done.16.refs_2_
  68.8 0.0 copy-done.3
  68.8 0.9 %finish.1 = f32[256,256]{1,0:T(8,128)} custom-call(f32[256,256]{1,0:T(8,128)S(1)} %get-tuple-element.13.own_ref, f32[256,256]{1,0:T(8,128)S(1)} %self_part.1.self_ref, s32[2,128]{1,0:T(2,128)S(1)} %bitcast.52, s32[264,128]{1,0:T(8,128)S(1)} %collective-permute-done.14.refs_0_, s32[264,128]{1,0:T(8,128)S(1)} %collective-permute-done.15.refs_1_, ...), custom_call_target="tpu_custom_call" | custom-call | tf_op jit(solution)/shard_map/finish/pallas_call | solution.py:265
  (5 shorter events, 0.1 us)
Async XLA Ops:
  1.9 13.3 %collective-permute-start = (s32[264,128]{1,0:T(8,128)S(1)}, s32[264,128]{1,0:T(8,128)S(1)}, u32[]{:S(2)}, u32[]{:S(2)}) collective-permute-start(s32[264,128]{1,0:T(8,128)S(1)} %project.1), channel_id=1, source_target_pairs={{128,0},{136,8},{144,16},{152,24},{160,32},{168,40},{176,48},{184,... | collective-permute-start | bytes 405512 | tf_op jit(solution)/shard_map/ppermute | solution.py:275
  8.3 9.6 %collective-permute-start.4 = (s32[264,128]{1,0:T(8,128)S(1)}, s32[264,128]{1,0:T(8,128)S(1)}, u32[]{:S(2)}, u32[]{:S(2)}) collective-permute-start(s32[264,128]{1,0:T(8,128)S(1)} %project.1), channel_id=1, source_target_pairs={{8,0},{33,1},{10,2},{35,3},{12,4},{37,5},{14,6},{39,7},{16,8},{41,... | collective-permute-start | bytes 405512 | tf_op jit(solution)/shard_map/ppermute | solution.py:288
  11.0 9.2 %collective-permute-start.5 = (s32[264,128]{1,0:T(8,128)S(1)}, s32[264,128]{1,0:T(8,128)S(1)}, u32[]{:S(2)}, u32[]{:S(2)}) collective-permute-start(s32[264,128]{1,0:T(8,128)S(1)} %project.1), channel_id=1, source_target_pairs={{24,0},{225,1},{26,2},{227,3},{28,4},{229,5},{30,6},{231,7},{0,8},... | collective-permute-start | bytes 405512 | tf_op jit(solution)/shard_map/ppermute | solution.py:288
  11.0 9.2 %collective-permute-start.6 = (s32[264,128]{1,0:T(8,128)S(1)}, s32[264,128]{1,0:T(8,128)S(1)}, u32[]{:S(2)}, u32[]{:S(2)}) collective-permute-start(s32[264,128]{1,0:T(8,128)S(1)} %project.1), channel_id=1, source_target_pairs={{16,0},{65,1},{18,2},{67,3},{20,4},{69,5},{22,6},{71,7},{24,8},{73... | collective-permute-start | bytes 405512 | tf_op jit(solution)/shard_map/ppermute | solution.py:288
  15.1 8.8 %collective-permute-start.1 = (s32[264,128]{1,0:T(8,128)S(1)}, s32[264,128]{1,0:T(8,128)S(1)}, u32[]{:S(2)}, u32[]{:S(2)}) collective-permute-start(s32[264,128]{1,0:T(8,128)S(1)} %collective-permute-done), channel_id=1, source_target_pairs={{8,0},{33,1},{10,2},{35,3},{12,4},{37,5},{14,6},{39,7},{16,8},{41,... | collective-permute-start | bytes 405512 | tf_op jit(solution)/shard_map/ppermute | solution.py:288
  17.9 8.4 %collective-permute-start.2 = (s32[264,128]{1,0:T(8,128)S(1)}, s32[264,128]{1,0:T(8,128)S(1)}, u32[]{:S(2)}, u32[]{:S(2)}) collective-permute-start(s32[264,128]{1,0:T(8,128)S(1)} %collective-permute-done), channel_id=1, source_target_pairs={{24,0},{225,1},{26,2},{227,3},{28,4},{229,5},{30,6},{231,7},{0,8},... | collective-permute-start | bytes 405512 | tf_op jit(solution)/shard_map/ppermute | solution.py:288
  17.9 8.4 %collective-permute-start.3 = (s32[264,128]{1,0:T(8,128)S(1)}, s32[264,128]{1,0:T(8,128)S(1)}, u32[]{:S(2)}, u32[]{:S(2)}) collective-permute-start(s32[264,128]{1,0:T(8,128)S(1)} %collective-permute-done), channel_id=1, source_target_pairs={{16,0},{65,1},{18,2},{67,3},{20,4},{69,5},{22,6},{71,7},{24,8},{73... | collective-permute-start | bytes 405512 | tf_op jit(solution)/shard_map/ppermute | solution.py:288
  20.7 17.8 %collective-permute-start.10 = (s32[1056,128]{1,0:T(8,128)S(1)}, s32[1056,128]{1,0:T(8,128)S(1)}, u32[]{:S(2)}, u32[]{:S(2)}) collective-permute-start(s32[1056,128]{1,0:T(8,128)S(1)} %pad_add_fusion.after_ref.refs_0_), channel_id=1, source_target_pairs={{32,0},{9,1},{34,2},{11,3},{36,4},{13,5},{38,6},{15,7},{40,8},{17,... | collective-permute-start | bytes 1622024 | tf_op jit(solution)/shard_map/ppermute | solution.py:288
  20.7 21.8 %collective-permute-start.11 = (s32[1056,128]{1,0:T(8,128)S(1)}, s32[1056,128]{1,0:T(8,128)S(1)}, u32[]{:S(2)}, u32[]{:S(2)}) collective-permute-start(s32[1056,128]{1,0:T(8,128)S(1)} %pad_add_fusion.after_ref.refs_0_), channel_id=1, source_target_pairs={{224,0},{25,1},{226,2},{27,3},{228,4},{29,5},{230,6},{31,7},{232,8... | collective-permute-start | bytes 1622024 | tf_op jit(solution)/shard_map/ppermute | solution.py:288
  24.0 18.6 %collective-permute-start.12 = (s32[1056,128]{1,0:T(8,128)S(1)}, s32[1056,128]{1,0:T(8,128)S(1)}, u32[]{:S(2)}, u32[]{:S(2)}) collective-permute-start(s32[1056,128]{1,0:T(8,128)S(1)} %pad_add_fusion.after_ref.refs_0_), channel_id=1, source_target_pairs={{64,0},{17,1},{66,2},{19,3},{68,4},{21,5},{70,6},{23,7},{72,8},{25... | collective-permute-start | bytes 1622024 | tf_op jit(solution)/shard_map/ppermute | solution.py:288
  27.6 18.8 %collective-permute-start.7 = (s32[1056,128]{1,0:T(8,128)S(1)}, s32[1056,128]{1,0:T(8,128)S(1)}, u32[]{:S(2)}, u32[]{:S(2)}) collective-permute-start(s32[1056,128]{1,0:T(8,128)S(1)} %add_add_fusion.after_ref.refs_1_), channel_id=1, source_target_pairs={{32,0},{9,1},{34,2},{11,3},{36,4},{13,5},{38,6},{15,7},{40,8},{17,... | collective-permute-start | bytes 1622024 | tf_op jit(solution)/shard_map/ppermute | solution.py:288
  30.4 16.0 %collective-permute-start.8 = (s32[1056,128]{1,0:T(8,128)S(1)}, s32[1056,128]{1,0:T(8,128)S(1)}, u32[]{:S(2)}, u32[]{:S(2)}) collective-permute-start(s32[1056,128]{1,0:T(8,128)S(1)} %add_add_fusion.after_ref.refs_1_), channel_id=1, source_target_pairs={{224,0},{25,1},{226,2},{27,3},{228,4},{29,5},{230,6},{31,7},{232,8... | collective-permute-start | bytes 1622024 | tf_op jit(solution)/shard_map/ppermute | solution.py:288
  38.6 13.5 %collective-permute-start.9 = (s32[1056,128]{1,0:T(8,128)S(1)}, s32[1056,128]{1,0:T(8,128)S(1)}, u32[]{:S(2)}, u32[]{:S(2)}) collective-permute-start(s32[1056,128]{1,0:T(8,128)S(1)} %add_add_fusion.after_ref.refs_1_), channel_id=1, source_target_pairs={{64,0},{17,1},{66,2},{19,3},{68,4},{21,5},{70,6},{23,7},{72,8},{25... | collective-permute-start | bytes 1622024 | tf_op jit(solution)/shard_map/ppermute | solution.py:288
  46.4 18.5 %copy-start = (bf16[256,768]{1,0:T(8,128)(2,1)S(1)}, bf16[256,768]{1,0:T(8,128)(2,1)}, u32[]{:S(2)}) copy-start(bf16[256,768]{1,0:T(8,128)(2,1)} %x_ref.1) | copy-start | bytes 1179652
  46.4 18.5 %copy-start.1 = (f32[768,256]{1,0:T(8,128)S(1)}, f32[768,256]{1,0:T(8,128)}, u32[]{:S(2)}) copy-start(f32[768,256]{1,0:T(8,128)} %w_ref.1) | copy-start | bytes 2359300
  46.4 18.5 %copy-start.2 = (f32[256]{0:T(256)S(1)}, f32[256]{0:T(256)}, u32[]{:S(2)}) copy-start(f32[256]{0:T(256)} %param.17) | copy-start | bytes 3076
  46.4 22.4 %copy-start.3 = (s32[256]{0:T(256)S(1)}, s32[256]{0:T(256)}, u32[]{:S(2)}) copy-start(s32[256]{0:T(256)} %param.10) | copy-start | bytes 3076
  54.7 2.7 %collective-permute-start.13 = (f32[8,128,256]{2,1,0:T(8,128)S(1)}, f32[8,128,256]{2,1,0:T(8,128)S(1)}, u32[]{:S(2)}, u32[]{:S(2)}) collective-permute-start(f32[8,128,256]{2,1,0:T(8,128)S(1)} %get-tuple-element.12), channel_id=1, source_target_pairs={{1,0},{0,1},{3,2},{2,3},{5,4},{4,5},{7,6},{6,7},{9,8},{8,9},{11,10... | collective-permute-start | bytes 3145736 | tf_op jit(solution)/shard_map/ppermute | solution.py:298
  57.9 8.1 %collective-permute-start.14 = (s32[264,128]{1,0:T(8,128)S(1)}, s32[264,128]{1,0:T(8,128)S(1)}, u32[]{:S(2)}, u32[]{:S(2)}) collective-permute-start(s32[264,128]{1,0:T(8,128)S(1)} %get-tuple-element.14), channel_id=1, source_target_pairs={{4,0},{5,1},{6,2},{7,3},{0,4},{1,5},{2,6},{3,7},{12,8},{13,9},{14,... | collective-permute-start | bytes 405512 | tf_op jit(solution)/shard_map/ppermute | solution.py:292
  61.6 6.9 %collective-permute-start.15 = (s32[264,128]{1,0:T(8,128)S(1)}, s32[264,128]{1,0:T(8,128)S(1)}, u32[]{:S(2)}, u32[]{:S(2)}) collective-permute-start(s32[264,128]{1,0:T(8,128)S(1)} %get-tuple-element.15), channel_id=1, source_target_pairs={{6,0},{7,1},{0,2},{1,3},{2,4},{3,5},{4,6},{5,7},{14,8},{15,9},{8,1... | collective-permute-start | bytes 405512 | tf_op jit(solution)/shard_map/ppermute | solution.py:292
  62.3 6.5 %collective-permute-start.16 = (s32[264,128]{1,0:T(8,128)S(1)}, s32[264,128]{1,0:T(8,128)S(1)}, u32[]{:S(2)}, u32[]{:S(2)}) collective-permute-start(s32[264,128]{1,0:T(8,128)S(1)} %get-tuple-element.16), channel_id=1, source_target_pairs={{2,0},{3,1},{4,2},{5,3},{6,4},{7,5},{0,6},{1,7},{10,8},{11,9},{12,... | collective-permute-start | bytes 405512 | tf_op jit(solution)/shard_map/ppermute | solution.py:292

commit v4 on v3

--- a/solution.py
+++ b/solution.py
@@ -104,7 +104,8 @@
     )(*vmem(blocks))
 
 
-def load_kernel(pat_hbm, after_ref, out_ref, landing, sem):
+def load_kernel(pat_hbm, after_ref, out_ref, zero_ref, landing, sem):
+    zero_ref[...] = after_ref[SPAN + 2 : SPAN + 3, :1]
     chunk, depth = landing.shape[1], landing.shape[0]
     steps = pat_hbm.shape[0] // chunk
 
@@ -124,9 +125,9 @@
 def load_patterns(patterns, after):
     return pl.pallas_call(
         load_kernel,
-        out_shape=pltpu.VMEM(patterns.shape, BF),
+        out_shape=[pltpu.VMEM(patterns.shape, BF), pltpu.VMEM((1, 1), I32)],
         in_specs=[pl.BlockSpec(memory_space=pltpu.HBM), IN_VMEM],
-        out_specs=IN_VMEM,
+        out_specs=[IN_VMEM, IN_VMEM],
         scratch_shapes=[pltpu.VMEM((8, 8, TILE, TILE), I32), pltpu.SemaphoreType.DMA((8,))],
         compiler_params=pltpu.CompilerParams(vmem_limit_bytes=VMEM_LIMIT),
         name="load_patterns",
@@ -323,12 +324,12 @@
     zero = zero_after(line)
     far_line = jnp.concatenate([far] + [from_step(far, step, 0) for step in STEPS[1:]]) + zero[0, 0]
     far_across = [from_step(far_line, step, 1) for step in STEPS[1:]]
-    zero_one = load_patterns(patterns[0, 0], far_line)
+    zero_one, late_zero = load_patterns(patterns[0, 0], far_line)
 
     row_at, col_at = lax.axis_index("row"), lax.axis_index("col")
     z_at, x_at = row_at // X, row_at % X
     y_at, core_at = col_at // CORES, col_at % CORES
-    cols = tile_cols[0, 0] + far_line[-1, -1]
+    cols = tile_cols[0, 0] + late_zero[0, 0]
     source = cols // 2
     dz = (source // X - z_at) % Z
     dx = (source % X - x_at) % X

time: 69.9 us -> 70 us (level)
  Pallas kernels: 14.3 us -> 15.8 us
  other arithmetic: 5.07 us -> 3.78 us
    pallas_call x2, Pallas kernels: 6.53 us -> 7.51 us  [aggregate(): pl.pallas_call(functools.partial(aggregate_kernel, late, counts), out_sha...]
    ppermute x12, waiting for transfers between devices: 5.61 us -> 6.32 us  [from_step(): return lax.ppermute(x, ('row', 'col'), pairs)]
  transfers between devices with their start and end apart: 17 -> 17, of which waited for: 6 -> 6; matrix products, arithmetic and copies ran while one was open for 8% -> 6% of each run, Pallas kernels for 12% -> 13%
where the time goes in v4:
time: 70 us; the launch traced here: 69.7 us
  starting transfers between devices  35.6 us (51%)
  Pallas kernels  15.8 us (23%)
  waiting for transfers between devices  13.7 us (20%)
  other arithmetic  3.78 us (5%)
  between operations  0.82 us (1%)
    ppermute x12, starting transfers between devices, from_step(): return lax.ppermute(x, ('row', 'col'), pairs)  22.6 us
    pallas_call x2, Pallas kernels, aggregate(): pl.pallas_call(functools.partial(aggregate_kernel, late, counts), out_sha...  7.51 us
    ppermute x3, starting transfers between devices, from_y(): lax.ppermute(x, 'col', [((y + d) % Y * CORES + k, y * CORES + k) for y in...  6.5 us
    ppermute x1, starting transfers between devices, from_far_z(): lax.ppermute(x, 'row', [((z + Z // 2) % Z * X + k, z * X + k) for z in ra...  6.38 us
    ppermute x12, waiting for transfers between devices, from_step(): return lax.ppermute(x, ('row', 'col'), pairs)  6.32 us
    pallas_call x1, Pallas kernels, load_patterns(): pl.pallas_call(load_kernel, out_shape=[pltpu.VMEM(patterns.shape, BF), pl...  4.19 us
    ppermute x3, waiting for transfers between devices, from_y(): lax.ppermute(x, 'col', [((y + d) % Y * CORES + k, y * CORES + k) for y in...  3.54 us
    ppermute x1, waiting for transfers between devices, from_core(): return lax.ppermute(x, 'col', [(c ^ 1, c) for c in range(Y * CORES)])  2.65 us
  transfers between devices with their start and end apart: 17, of which 6 were waited for; matrix products, arithmetic and copies ran while one was open for 6% of the time, Pallas kernels for 13%

profile of v4, /device:TPU:32, one launch (start us, length us, event | category | flops | bytes accessed | tf_op | source)
XLA Modules:
  0.0 69.7 jit_solution(13042503431721373290)
XLA Ops:
  0.0 1.9 %project.1 = s32[264,128]{1,0:T(8,128)S(1)} custom-call(bf16[256,768]{1,0:T(8,128)(2,1)} %x_ref.1, f32[768,256]{1,0:T(8,128)} %w_hbm.1), custom_call_target="tpu_custom_call" | custom-call | tf_op jit(solution)/shard_map/project/pallas_call | solution.py:78
  1.9 6.4 %collective-permute-start = (s32[264,128]{1,0:T(8,128)S(1)}, s32[264,128]{1,0:T(8,128)S(1)}, u32[]{:S(2)}, u32[]{:S(2)}) collective-permute-start(s32[264,128]{1,0:T(8,128)S(1)} %project.1), channel_id=1, source_target_pairs={{128,0},{136,8},{144,16},{152,24},{160,32},{168,40},{176,48},{184,... | collective-permute-start | bytes 405512 | tf_op jit(solution)/shard_map/ppermute | solution.py:276
  8.3 2.8 %collective-permute-start.4 = (s32[264,128]{1,0:T(8,128)S(1)}, s32[264,128]{1,0:T(8,128)S(1)}, u32[]{:S(2)}, u32[]{:S(2)}) collective-permute-start(s32[264,128]{1,0:T(8,128)S(1)} %project.1), channel_id=1, source_target_pairs={{8,0},{33,1},{10,2},{35,3},{12,4},{37,5},{14,6},{39,7},{16,8},{41,... | collective-permute-start | bytes 405512 | tf_op jit(solution)/shard_map/ppermute | solution.py:289
  11.0 0.0 collective-permute-start.5
  11.0 2.3 %collective-permute-start.6 = (s32[264,128]{1,0:T(8,128)S(1)}, s32[264,128]{1,0:T(8,128)S(1)}, u32[]{:S(2)}, u32[]{:S(2)}) collective-permute-start(s32[264,128]{1,0:T(8,128)S(1)} %project.1), channel_id=1, source_target_pairs={{16,0},{65,1},{18,2},{67,3},{20,4},{69,5},{22,6},{71,7},{24,8},{73... | collective-permute-start | bytes 405512 | tf_op jit(solution)/shard_map/ppermute | solution.py:289
  14.0 1.2 %collective-permute-done = s32[264,128]{1,0:T(8,128)S(1)} collective-permute-done((s32[264,128]{1,0:T(8,128)S(1)}, s32[264,128]{1,0:T(8,128)S(1)}, u32[]{:S(2)}, u32[]{:S(2)}) %collective-permute-start) | collective-permute-done | bytes 135200 | tf_op jit(solution)/shard_map/ppermute | solution.py:276
  15.1 2.8 %collective-permute-start.1 = (s32[264,128]{1,0:T(8,128)S(1)}, s32[264,128]{1,0:T(8,128)S(1)}, u32[]{:S(2)}, u32[]{:S(2)}) collective-permute-start(s32[264,128]{1,0:T(8,128)S(1)} %collective-permute-done), channel_id=1, source_target_pairs={{8,0},{33,1},{10,2},{35,3},{12,4},{37,5},{14,6},{39,7},{16,8},{41,... | collective-permute-start | bytes 405512 | tf_op jit(solution)/shard_map/ppermute | solution.py:289
  17.9 0.0 collective-permute-start.2
  17.9 0.0 collective-permute-done.4
  17.9 2.3 %collective-permute-start.3 = (s32[264,128]{1,0:T(8,128)S(1)}, s32[264,128]{1,0:T(8,128)S(1)}, u32[]{:S(2)}, u32[]{:S(2)}) collective-permute-start(s32[264,128]{1,0:T(8,128)S(1)} %collective-permute-done), channel_id=1, source_target_pairs={{16,0},{65,1},{18,2},{67,3},{20,4},{69,5},{22,6},{71,7},{24,8},{73... | collective-permute-start | bytes 405512 | tf_op jit(solution)/shard_map/ppermute | solution.py:289
  20.2 0.0 collective-permute-done.5
  20.2 0.0 collective-permute-done.6
  20.2 0.5 zero_after.1
  20.7 0.0 collective-permute-start.10
  20.7 3.2 %collective-permute-start.11 = (s32[1056,128]{1,0:T(8,128)S(1)}, s32[1056,128]{1,0:T(8,128)S(1)}, u32[]{:S(2)}, u32[]{:S(2)}) collective-permute-start(s32[1056,128]{1,0:T(8,128)S(1)} %pad_add_fusion.after_ref.refs_0_), channel_id=1, source_target_pairs={{224,0},{25,1},{226,2},{27,3},{228,4},{29,5},{230,6},{31,7},{232,8... | collective-permute-start | bytes 1622024 | tf_op jit(solution)/shard_map/ppermute | solution.py:289
  24.0 0.0 collective-permute-done.1
  24.0 2.4 %collective-permute-start.12 = (s32[1056,128]{1,0:T(8,128)S(1)}, s32[1056,128]{1,0:T(8,128)S(1)}, u32[]{:S(2)}, u32[]{:S(2)}) collective-permute-start(s32[1056,128]{1,0:T(8,128)S(1)} %pad_add_fusion.after_ref.refs_0_), channel_id=1, source_target_pairs={{64,0},{17,1},{66,2},{19,3},{68,4},{21,5},{70,6},{23,7},{72,8},{25... | collective-permute-start | bytes 1622024 | tf_op jit(solution)/shard_map/ppermute | solution.py:289
  26.3 0.0 collective-permute-done.2
  26.3 0.0 collective-permute-done.3
  26.3 0.7 add_add_fusion.after_ref.refs_1_
  27.0 2.9 %collective-permute-start.7 = (s32[1056,128]{1,0:T(8,128)S(1)}, s32[1056,128]{1,0:T(8,128)S(1)}, u32[]{:S(2)}, u32[]{:S(2)}) collective-permute-start(s32[1056,128]{1,0:T(8,128)S(1)} %add_add_fusion.after_ref.refs_1_), channel_id=1, source_target_pairs={{32,0},{9,1},{34,2},{11,3},{36,4},{13,5},{38,6},{15,7},{40,8},{17,... | collective-permute-start | bytes 1622024 | tf_op jit(solution)/shard_map/ppermute | solution.py:289
  29.9 0.3 collective-permute-start.8
  30.2 0.0 copy-start.4
  30.2 0.0 copy-start.5
  30.2 4.2 %load_patterns.1 = (bf16[128,128,128]{2,1,0:T(8,128)(2,1)S(1)}, s32[1,1]{1,0:T(1,128)}) custom-call(s32[128,128,128]{2,1,0:T(8,128)} %bitcast.53, s32[1056,128]{1,0:T(8,128)S(1)} %add_add_fusion.after_ref.refs_1_), custom_call_target="tpu_custom_call" | custom-call | tf_op jit(solution)/shard_map/load_patterns/pallas_call | solution.py:126
  34.4 0.0 copy-done.4
  34.4 1.3 %fusion.10 = (s32[]{:T(128)}, s32[128]{0:T(128)S(1)}) fusion(pred[]{:T(512)S(6)} %eq.176, s32[]{:T(128)S(6)} %select_n.443, s32[]{:T(128)S(6)} %select_n.438, s32[1,1,128]{2,1,0:T(1,128)S(1)} %copy-done.4, s32[]{:T(128)} %bitcast.3, pred[]{:T(512)S(6)} %eq.168, s32[]{:T(128)} %bitcast.49), kind=kLoop, calls=%fused_computation.90 | loop fusion | flops 12799 | bytes 1046 | tf_op jit(solution)/shard_map/reduce_sum | solution.py:311
  35.8 0.0 copy-done.5
  35.8 0.7 fusion
  36.5 0.6 pad_add_fusion.3
  37.1 0.1 pad.1.clone
  37.2 0.2 convert_reduce_fusion
  37.4 0.0 collective-permute-done.10.refs_2_
  37.4 3.7 %collective-permute-start.9 = (s32[1056,128]{1,0:T(8,128)S(1)}, s32[1056,128]{1,0:T(8,128)S(1)}, u32[]{:S(2)}, u32[]{:S(2)}) collective-permute-start(s32[1056,128]{1,0:T(8,128)S(1)} %add_add_fusion.after_ref.refs_1_), channel_id=1, source_target_pairs={{64,0},{17,1},{66,2},{19,3},{68,4},{21,5},{70,6},{23,7},{72,8},{25... | collective-permute-start | bytes 1622024 | tf_op jit(solution)/shard_map/ppermute | solution.py:289
  41.1 0.1 select_reduce_fusion
  41.3 0.1 pad_add_fusion.1.slots_ref
  41.4 0.0 collective-permute-done.11.refs_3_
  41.4 0.0 collective-permute-done.12.refs_4_
  41.4 4.3 %aggregate_early.1.refs_3_ = f32[16,128,256]{2,1,0:T(8,128)S(1)} custom-call(s32[5,128]{1,0:T(8,128)S(1)} %pad_add_fusion.1.slots_ref, bf16[128,128,128]{2,1,0:T(8,128)(2,1)S(1)} %get-tuple-element.14.pat, s32[1056,128]{1,0:T(8,128)S(1)} %pad_add_fusion.after_ref.refs_0_, s32[1056,128]{1,0:T(8,128)S(1)} %add_add_fusion.after_ref.refs_1_, ...), custom_call_target="tpu_custom_call" | custom-call | tf_op jit(solution)/shard_map/aggregate_early/pallas_call | solution.py:194
  45.7 0.0 copy-start
  45.7 0.0 copy-start.1
  45.7 0.0 copy-start.2
  45.7 0.0 copy-start.3
  45.7 0.0 collective-permute-done.7.refs_0_
  45.7 0.0 collective-permute-done.8.refs_1_
  45.7 6.3 %collective-permute-done.9.refs_2_ = s32[1056,128]{1,0:T(8,128)S(1)} collective-permute-done((s32[1056,128]{1,0:T(8,128)S(1)}, s32[1056,128]{1,0:T(8,128)S(1)}, u32[]{:S(2)}, u32[]{:S(2)}) %collective-permute-start.9) | collective-permute-done | bytes 540704 | tf_op jit(solution)/shard_map/ppermute | solution.py:289
  52.0 3.2 %aggregate_late.1 = (f32[8,128,256]{2,1,0:T(8,128)S(1)}, f32[8,128,256]{2,1,0:T(8,128)S(1)}) custom-call(s32[5,128]{1,0:T(8,128)S(1)} %pad_add_fusion.1.slots_ref, bf16[128,128,128]{2,1,0:T(8,128)(2,1)S(1)} %get-tuple-element.14.pat, s32[1056,128]{1,0:T(8,128)S(1)} %collective-permute-done.7.refs_0_, s32[1056,128]{1,0:T(8,128)S(1)} %collective-permute-done.8.refs_1_, ...), custom_call_target="tpu_custom_call" | custom-call | tf_op jit(solution)/shard_map/aggregate_late/pallas_call | solution.py:194
  55.2 0.1 collective-permute-start.13
  55.3 2.6 %collective-permute-done.13.other_ref = f32[8,128,256]{2,1,0:T(8,128)S(1)} collective-permute-done((f32[8,128,256]{2,1,0:T(8,128)S(1)}, f32[8,128,256]{2,1,0:T(8,128)S(1)}, u32[]{:S(2)}, u32[]{:S(2)}) %collective-permute-start.13) | collective-permute-done | bytes 1048608 | tf_op jit(solution)/shard_map/ppermute | solution.py:299
  58.0 0.4 add_pair.1
  58.4 3.3 %collective-permute-start.14 = (s32[264,128]{1,0:T(8,128)S(1)}, s32[264,128]{1,0:T(8,128)S(1)}, u32[]{:S(2)}, u32[]{:S(2)}) collective-permute-start(s32[264,128]{1,0:T(8,128)S(1)} %get-tuple-element.18), channel_id=1, source_target_pairs={{4,0},{5,1},{6,2},{7,3},{0,4},{1,5},{2,6},{3,7},{12,8},{13,9},{14,... | collective-permute-start | bytes 405512 | tf_op jit(solution)/shard_map/ppermute | solution.py:293
  61.6 0.7 collective-permute-start.15
  62.3 2.6 %collective-permute-start.16 = (s32[264,128]{1,0:T(8,128)S(1)}, s32[264,128]{1,0:T(8,128)S(1)}, u32[]{:S(2)}, u32[]{:S(2)}) collective-permute-start(s32[264,128]{1,0:T(8,128)S(1)} %get-tuple-element.20), channel_id=1, source_target_pairs={{2,0},{3,1},{4,2},{5,3},{6,4},{7,5},{0,6},{1,7},{10,8},{11,9},{12,... | collective-permute-start | bytes 405512 | tf_op jit(solution)/shard_map/ppermute | solution.py:293
  64.9 0.0 copy-done
  64.9 0.0 copy-done.1
  64.9 0.0 copy-done.2
  64.9 0.4 self_part.1.self_ref
  65.2 1.1 %collective-permute-done.14.refs_0_ = s32[264,128]{1,0:T(8,128)S(1)} collective-permute-done((s32[264,128]{1,0:T(8,128)S(1)}, s32[264,128]{1,0:T(8,128)S(1)}, u32[]{:S(2)}, u32[]{:S(2)}) %collective-permute-start.14) | collective-permute-done | bytes 135200 | tf_op jit(solution)/shard_map/ppermute | solution.py:293
  66.4 2.4 %collective-permute-done.15.refs_1_ = s32[264,128]{1,0:T(8,128)S(1)} collective-permute-done((s32[264,128]{1,0:T(8,128)S(1)}, s32[264,128]{1,0:T(8,128)S(1)}, u32[]{:S(2)}, u32[]{:S(2)}) %collective-permute-start.15) | collective-permute-done | bytes 135200 | tf_op jit(solution)/shard_map/ppermute | solution.py:293
  68.7 0.1 collective-permute-done.16.refs_2_
  68.8 0.0 copy-done.3
  68.8 0.9 %finish.1 = f32[256,256]{1,0:T(8,128)} custom-call(f32[256,256]{1,0:T(8,128)S(1)} %get-tuple-element.17.own_ref, f32[256,256]{1,0:T(8,128)S(1)} %self_part.1.self_ref, s32[2,128]{1,0:T(2,128)S(1)} %bitcast.52, s32[264,128]{1,0:T(8,128)S(1)} %collective-permute-done.14.refs_0_, s32[264,128]{1,0:T(8,128)S(1)} %collective-permute-done.15.refs_1_, ...), custom_call_target="tpu_custom_call" | custom-call | tf_op jit(solution)/shard_map/finish/pallas_call | solution.py:266
  (5 shorter events, 0.1 us)
Async XLA Ops:
  1.9 13.3 %collective-permute-start = (s32[264,128]{1,0:T(8,128)S(1)}, s32[264,128]{1,0:T(8,128)S(1)}, u32[]{:S(2)}, u32[]{:S(2)}) collective-permute-start(s32[264,128]{1,0:T(8,128)S(1)} %project.1), channel_id=1, source_target_pairs={{128,0},{136,8},{144,16},{152,24},{160,32},{168,40},{176,48},{184,... | collective-permute-start | bytes 405512 | tf_op jit(solution)/shard_map/ppermute | solution.py:276
  8.3 9.6 %collective-permute-start.4 = (s32[264,128]{1,0:T(8,128)S(1)}, s32[264,128]{1,0:T(8,128)S(1)}, u32[]{:S(2)}, u32[]{:S(2)}) collective-permute-start(s32[264,128]{1,0:T(8,128)S(1)} %project.1), channel_id=1, source_target_pairs={{8,0},{33,1},{10,2},{35,3},{12,4},{37,5},{14,6},{39,7},{16,8},{41,... | collective-permute-start | bytes 405512 | tf_op jit(solution)/shard_map/ppermute | solution.py:289
  11.0 9.2 %collective-permute-start.5 = (s32[264,128]{1,0:T(8,128)S(1)}, s32[264,128]{1,0:T(8,128)S(1)}, u32[]{:S(2)}, u32[]{:S(2)}) collective-permute-start(s32[264,128]{1,0:T(8,128)S(1)} %project.1), channel_id=1, source_target_pairs={{24,0},{225,1},{26,2},{227,3},{28,4},{229,5},{30,6},{231,7},{0,8},... | collective-permute-start | bytes 405512 | tf_op jit(solution)/shard_map/ppermute | solution.py:289
  11.0 9.2 %collective-permute-start.6 = (s32[264,128]{1,0:T(8,128)S(1)}, s32[264,128]{1,0:T(8,128)S(1)}, u32[]{:S(2)}, u32[]{:S(2)}) collective-permute-start(s32[264,128]{1,0:T(8,128)S(1)} %project.1), channel_id=1, source_target_pairs={{16,0},{65,1},{18,2},{67,3},{20,4},{69,5},{22,6},{71,7},{24,8},{73... | collective-permute-start | bytes 405512 | tf_op jit(solution)/shard_map/ppermute | solution.py:289
  15.1 8.8 %collective-permute-start.1 = (s32[264,128]{1,0:T(8,128)S(1)}, s32[264,128]{1,0:T(8,128)S(1)}, u32[]{:S(2)}, u32[]{:S(2)}) collective-permute-start(s32[264,128]{1,0:T(8,128)S(1)} %collective-permute-done), channel_id=1, source_target_pairs={{8,0},{33,1},{10,2},{35,3},{12,4},{37,5},{14,6},{39,7},{16,8},{41,... | collective-permute-start | bytes 405512 | tf_op jit(solution)/shard_map/ppermute | solution.py:289
  17.9 8.4 %collective-permute-start.2 = (s32[264,128]{1,0:T(8,128)S(1)}, s32[264,128]{1,0:T(8,128)S(1)}, u32[]{:S(2)}, u32[]{:S(2)}) collective-permute-start(s32[264,128]{1,0:T(8,128)S(1)} %collective-permute-done), channel_id=1, source_target_pairs={{24,0},{225,1},{26,2},{227,3},{28,4},{229,5},{30,6},{231,7},{0,8},... | collective-permute-start | bytes 405512 | tf_op jit(solution)/shard_map/ppermute | solution.py:289
  17.9 8.4 %collective-permute-start.3 = (s32[264,128]{1,0:T(8,128)S(1)}, s32[264,128]{1,0:T(8,128)S(1)}, u32[]{:S(2)}, u32[]{:S(2)}) collective-permute-start(s32[264,128]{1,0:T(8,128)S(1)} %collective-permute-done), channel_id=1, source_target_pairs={{16,0},{65,1},{18,2},{67,3},{20,4},{69,5},{22,6},{71,7},{24,8},{73... | collective-permute-start | bytes 405512 | tf_op jit(solution)/shard_map/ppermute | solution.py:289
  20.7 16.6 %collective-permute-start.10 = (s32[1056,128]{1,0:T(8,128)S(1)}, s32[1056,128]{1,0:T(8,128)S(1)}, u32[]{:S(2)}, u32[]{:S(2)}) collective-permute-start(s32[1056,128]{1,0:T(8,128)S(1)} %pad_add_fusion.after_ref.refs_0_), channel_id=1, source_target_pairs={{32,0},{9,1},{34,2},{11,3},{36,4},{13,5},{38,6},{15,7},{40,8},{17,... | collective-permute-start | bytes 1622024 | tf_op jit(solution)/shard_map/ppermute | solution.py:289
  20.7 20.6 %collective-permute-start.11 = (s32[1056,128]{1,0:T(8,128)S(1)}, s32[1056,128]{1,0:T(8,128)S(1)}, u32[]{:S(2)}, u32[]{:S(2)}) collective-permute-start(s32[1056,128]{1,0:T(8,128)S(1)} %pad_add_fusion.after_ref.refs_0_), channel_id=1, source_target_pairs={{224,0},{25,1},{226,2},{27,3},{228,4},{29,5},{230,6},{31,7},{232,8... | collective-permute-start | bytes 1622024 | tf_op jit(solution)/shard_map/ppermute | solution.py:289
  24.0 17.4 %collective-permute-start.12 = (s32[1056,128]{1,0:T(8,128)S(1)}, s32[1056,128]{1,0:T(8,128)S(1)}, u32[]{:S(2)}, u32[]{:S(2)}) collective-permute-start(s32[1056,128]{1,0:T(8,128)S(1)} %pad_add_fusion.after_ref.refs_0_), channel_id=1, source_target_pairs={{64,0},{17,1},{66,2},{19,3},{68,4},{21,5},{70,6},{23,7},{72,8},{25... | collective-permute-start | bytes 1622024 | tf_op jit(solution)/shard_map/ppermute | solution.py:289
  27.0 18.7 %collective-permute-start.7 = (s32[1056,128]{1,0:T(8,128)S(1)}, s32[1056,128]{1,0:T(8,128)S(1)}, u32[]{:S(2)}, u32[]{:S(2)}) collective-permute-start(s32[1056,128]{1,0:T(8,128)S(1)} %add_add_fusion.after_ref.refs_1_), channel_id=1, source_target_pairs={{32,0},{9,1},{34,2},{11,3},{36,4},{13,5},{38,6},{15,7},{40,8},{17,... | collective-permute-start | bytes 1622024 | tf_op jit(solution)/shard_map/ppermute | solution.py:289
  29.9 15.8 %collective-permute-start.8 = (s32[1056,128]{1,0:T(8,128)S(1)}, s32[1056,128]{1,0:T(8,128)S(1)}, u32[]{:S(2)}, u32[]{:S(2)}) collective-permute-start(s32[1056,128]{1,0:T(8,128)S(1)} %add_add_fusion.after_ref.refs_1_), channel_id=1, source_target_pairs={{224,0},{25,1},{226,2},{27,3},{228,4},{29,5},{230,6},{31,7},{232,8... | collective-permute-start | bytes 1622024 | tf_op jit(solution)/shard_map/ppermute | solution.py:289
  30.2 4.2 %copy-start.4 = (s32[1,1,128]{2,1,0:T(1,128)S(1)}, s32[1,1,128]{2,1,0:T(1,128)}, u32[]{:S(2)}) copy-start(s32[1,1,128]{2,1,0:T(1,128)} %param.12) | copy-start | bytes 1540
  30.2 5.5 %copy-start.5 = (s32[1,1,128]{2,1,0:T(1,128)S(1)}, s32[1,1,128]{2,1,0:T(1,128)}, u32[]{:S(2)}) copy-start(s32[1,1,128]{2,1,0:T(1,128)} %param.11) | copy-start | bytes 1540
  37.4 14.7 %collective-permute-start.9 = (s32[1056,128]{1,0:T(8,128)S(1)}, s32[1056,128]{1,0:T(8,128)S(1)}, u32[]{:S(2)}, u32[]{:S(2)}) collective-permute-start(s32[1056,128]{1,0:T(8,128)S(1)} %add_add_fusion.after_ref.refs_1_), channel_id=1, source_target_pairs={{64,0},{17,1},{66,2},{19,3},{68,4},{21,5},{70,6},{23,7},{72,8},{25... | collective-permute-start | bytes 1622024 | tf_op jit(solution)/shard_map/ppermute | solution.py:289
  45.7 19.2 %copy-start = (bf16[256,768]{1,0:T(8,128)(2,1)S(1)}, bf16[256,768]{1,0:T(8,128)(2,1)}, u32[]{:S(2)}) copy-start(bf16[256,768]{1,0:T(8,128)(2,1)} %x_ref.1) | copy-start | bytes 1179652
  45.7 19.2 %copy-start.1 = (f32[768,256]{1,0:T(8,128)S(1)}, f32[768,256]{1,0:T(8,128)}, u32[]{:S(2)}) copy-start(f32[768,256]{1,0:T(8,128)} %w_ref.1) | copy-start | bytes 2359300
  45.7 19.2 %copy-start.2 = (f32[256]{0:T(256)S(1)}, f32[256]{0:T(256)}, u32[]{:S(2)}) copy-start(f32[256]{0:T(256)} %param.17) | copy-start | bytes 3076
  45.7 23.1 %copy-start.3 = (s32[256]{0:T(256)S(1)}, s32[256]{0:T(256)}, u32[]{:S(2)}) copy-start(s32[256]{0:T(256)} %param.10) | copy-start | bytes 3076
  55.2 2.7 %collective-permute-start.13 = (f32[8,128,256]{2,1,0:T(8,128)S(1)}, f32[8,128,256]{2,1,0:T(8,128)S(1)}, u32[]{:S(2)}, u32[]{:S(2)}) collective-permute-start(f32[8,128,256]{2,1,0:T(8,128)S(1)} %get-tuple-element.16), channel_id=1, source_target_pairs={{1,0},{0,1},{3,2},{2,3},{5,4},{4,5},{7,6},{6,7},{9,8},{8,9},{11,10... | collective-permute-start | bytes 3145736 | tf_op jit(solution)/shard_map/ppermute | solution.py:299
  58.4 8.0 %collective-permute-start.14 = (s32[264,128]{1,0:T(8,128)S(1)}, s32[264,128]{1,0:T(8,128)S(1)}, u32[]{:S(2)}, u32[]{:S(2)}) collective-permute-start(s32[264,128]{1,0:T(8,128)S(1)} %get-tuple-element.18), channel_id=1, source_target_pairs={{4,0},{5,1},{6,2},{7,3},{0,4},{1,5},{2,6},{3,7},{12,8},{13,9},{14,... | collective-permute-start | bytes 405512 | tf_op jit(solution)/shard_map/ppermute | solution.py:293
  61.6 7.1 %collective-permute-start.15 = (s32[264,128]{1,0:T(8,128)S(1)}, s32[264,128]{1,0:T(8,128)S(1)}, u32[]{:S(2)}, u32[]{:S(2)}) collective-permute-start(s32[264,128]{1,0:T(8,128)S(1)} %get-tuple-element.19), channel_id=1, source_target_pairs={{6,0},{7,1},{0,2},{1,3},{2,4},{3,5},{4,6},{5,7},{14,8},{15,9},{8,1... | collective-permute-start | bytes 405512 | tf_op jit(solution)/shard_map/ppermute | solution.py:293
  62.3 6.5 %collective-permute-start.16 = (s32[264,128]{1,0:T(8,128)S(1)}, s32[264,128]{1,0:T(8,128)S(1)}, u32[]{:S(2)}, u32[]{:S(2)}) collective-permute-start(s32[264,128]{1,0:T(8,128)S(1)} %get-tuple-element.20), channel_id=1, source_target_pairs={{2,0},{3,1},{4,2},{5,3},{6,4},{7,5},{0,6},{1,7},{10,8},{11,9},{12,... | collective-permute-start | bytes 405512 | tf_op jit(solution)/shard_map/ppermute | solution.py:293

commit v5 on v4

--- a/solution.py
+++ b/solution.py
@@ -164,7 +164,7 @@
                     parts[tile, TILE:, where] = low
             return carry
 
-        lax.fori_loop(0, count, decode, 0)
+        lax.fori_loop(0, count, decode, 0, unroll=True)
         at += count
 
     def add_group(g, carry):

time: 70 us -> 70.3 us (level)
  starting transfers between devices: 35.6 us -> 34.8 us
    ppermute x3, waiting for transfers between devices: 3.54 us -> 4.53 us  [from_y(): lax.ppermute(x, 'col', [((y + d) % Y * CORES + k, y * CORES + k) for y in...]
    ppermute x3, starting transfers between devices: 6.5 us -> 5.51 us  [from_y(): lax.ppermute(x, 'col', [((y + d) % Y * CORES + k, y * CORES + k) for y in...]
  transfers between devices with their start and end apart: 17 -> 17, of which waited for: 6 -> 6; matrix products, arithmetic and copies ran while one was open for 6% -> 6% of each run, Pallas kernels for 13% -> 14%
where the time goes in v5:
time: 70.3 us; the launch traced here: 70.2 us
  starting transfers between devices  34.8 us (50%)
  Pallas kernels  16.4 us (23%)
  waiting for transfers between devices  14.3 us (20%)
  other arithmetic  3.78 us (5%)
  between operations  0.82 us (1%)
    ppermute x12, starting transfers between devices, from_step(): return lax.ppermute(x, ('row', 'col'), pairs)  22.8 us
    pallas_call x2, Pallas kernels, aggregate(): pl.pallas_call(functools.partial(aggregate_kernel, late, counts), out_sha...  8.17 us
    ppermute x1, starting transfers between devices, from_far_z(): lax.ppermute(x, 'row', [((z + Z // 2) % Z * X + k, z * X + k) for z in ra...  6.38 us
    ppermute x12, waiting for transfers between devices, from_step(): return lax.ppermute(x, ('row', 'col'), pairs)  5.92 us
    ppermute x3, starting transfers between devices, from_y(): lax.ppermute(x, 'col', [((y + d) % Y * CORES + k, y * CORES + k) for y in...  5.51 us
    ppermute x3, waiting for transfers between devices, from_y(): lax.ppermute(x, 'col', [((y + d) % Y * CORES + k, y * CORES + k) for y in...  4.53 us
    pallas_call x1, Pallas kernels, load_patterns(): pl.pallas_call(load_kernel, out_shape=[pltpu.VMEM(patterns.shape, BF), pl...  4.19 us
    ppermute x1, waiting for transfers between devices, from_core(): return lax.ppermute(x, 'col', [(c ^ 1, c) for c in range(Y * CORES)])  2.65 us
  transfers between devices with their start and end apart: 17, of which 6 were waited for; matrix products, arithmetic and copies ran while one was open for 6% of the time, Pallas kernels for 14%

profile of v5, /device:TPU:32, one launch (start us, length us, event | category | flops | bytes accessed | tf_op | source)
XLA Modules:
  0.0 70.2 jit_solution(11229032059361930999)
XLA Ops:
  0.0 1.9 %project.1 = s32[264,128]{1,0:T(8,128)S(1)} custom-call(bf16[256,768]{1,0:T(8,128)(2,1)} %x_ref.1, f32[768,256]{1,0:T(8,128)} %w_hbm.1), custom_call_target="tpu_custom_call" | custom-call | tf_op jit(solution)/shard_map/project/pallas_call | solution.py:78
  1.9 6.4 %collective-permute-start = (s32[264,128]{1,0:T(8,128)S(1)}, s32[264,128]{1,0:T(8,128)S(1)}, u32[]{:S(2)}, u32[]{:S(2)}) collective-permute-start(s32[264,128]{1,0:T(8,128)S(1)} %project.1), channel_id=1, source_target_pairs={{128,0},{136,8},{144,16},{152,24},{160,32},{168,40},{176,48},{184,... | collective-permute-start | bytes 405512 | tf_op jit(solution)/shard_map/ppermute | solution.py:276
  8.3 2.8 %collective-permute-start.4 = (s32[264,128]{1,0:T(8,128)S(1)}, s32[264,128]{1,0:T(8,128)S(1)}, u32[]{:S(2)}, u32[]{:S(2)}) collective-permute-start(s32[264,128]{1,0:T(8,128)S(1)} %project.1), channel_id=1, source_target_pairs={{8,0},{33,1},{10,2},{35,3},{12,4},{37,5},{14,6},{39,7},{16,8},{41,... | collective-permute-start | bytes 405512 | tf_op jit(solution)/shard_map/ppermute | solution.py:289
  11.0 0.0 collective-permute-start.5
  11.0 2.3 %collective-permute-start.6 = (s32[264,128]{1,0:T(8,128)S(1)}, s32[264,128]{1,0:T(8,128)S(1)}, u32[]{:S(2)}, u32[]{:S(2)}) collective-permute-start(s32[264,128]{1,0:T(8,128)S(1)} %project.1), channel_id=1, source_target_pairs={{16,0},{65,1},{18,2},{67,3},{20,4},{69,5},{22,6},{71,7},{24,8},{73... | collective-permute-start | bytes 405512 | tf_op jit(solution)/shard_map/ppermute | solution.py:289
  14.0 1.2 %collective-permute-done = s32[264,128]{1,0:T(8,128)S(1)} collective-permute-done((s32[264,128]{1,0:T(8,128)S(1)}, s32[264,128]{1,0:T(8,128)S(1)}, u32[]{:S(2)}, u32[]{:S(2)}) %collective-permute-start) | collective-permute-done | bytes 135200 | tf_op jit(solution)/shard_map/ppermute | solution.py:276
  15.1 2.8 %collective-permute-start.1 = (s32[264,128]{1,0:T(8,128)S(1)}, s32[264,128]{1,0:T(8,128)S(1)}, u32[]{:S(2)}, u32[]{:S(2)}) collective-permute-start(s32[264,128]{1,0:T(8,128)S(1)} %collective-permute-done), channel_id=1, source_target_pairs={{8,0},{33,1},{10,2},{35,3},{12,4},{37,5},{14,6},{39,7},{16,8},{41,... | collective-permute-start | bytes 405512 | tf_op jit(solution)/shard_map/ppermute | solution.py:289
  17.9 0.0 collective-permute-start.2
  17.9 0.0 collective-permute-done.4
  17.9 2.3 %collective-permute-start.3 = (s32[264,128]{1,0:T(8,128)S(1)}, s32[264,128]{1,0:T(8,128)S(1)}, u32[]{:S(2)}, u32[]{:S(2)}) collective-permute-start(s32[264,128]{1,0:T(8,128)S(1)} %collective-permute-done), channel_id=1, source_target_pairs={{16,0},{65,1},{18,2},{67,3},{20,4},{69,5},{22,6},{71,7},{24,8},{73... | collective-permute-start | bytes 405512 | tf_op jit(solution)/shard_map/ppermute | solution.py:289
  20.2 0.0 collective-permute-done.5
  20.2 0.0 collective-permute-done.6
  20.2 0.5 zero_after.1
  20.7 0.0 collective-permute-start.10
  20.7 3.2 %collective-permute-start.11 = (s32[1056,128]{1,0:T(8,128)S(1)}, s32[1056,128]{1,0:T(8,128)S(1)}, u32[]{:S(2)}, u32[]{:S(2)}) collective-permute-start(s32[1056,128]{1,0:T(8,128)S(1)} %pad_add_fusion.after_ref.refs_0_), channel_id=1, source_target_pairs={{224,0},{25,1},{226,2},{27,3},{228,4},{29,5},{230,6},{31,7},{232,8... | collective-permute-start | bytes 1622024 | tf_op jit(solution)/shard_map/ppermute | solution.py:289
  24.0 0.0 collective-permute-done.1
  24.0 2.4 %collective-permute-start.12 = (s32[1056,128]{1,0:T(8,128)S(1)}, s32[1056,128]{1,0:T(8,128)S(1)}, u32[]{:S(2)}, u32[]{:S(2)}) collective-permute-start(s32[1056,128]{1,0:T(8,128)S(1)} %pad_add_fusion.after_ref.refs_0_), channel_id=1, source_target_pairs={{64,0},{17,1},{66,2},{19,3},{68,4},{21,5},{70,6},{23,7},{72,8},{25... | collective-permute-start | bytes 1622024 | tf_op jit(solution)/shard_map/ppermute | solution.py:289
  26.3 0.0 collective-permute-done.2
  26.3 0.0 collective-permute-done.3
  26.3 0.7 add_add_fusion.after_ref.refs_1_
  27.0 2.9 %collective-permute-start.7 = (s32[1056,128]{1,0:T(8,128)S(1)}, s32[1056,128]{1,0:T(8,128)S(1)}, u32[]{:S(2)}, u32[]{:S(2)}) collective-permute-start(s32[1056,128]{1,0:T(8,128)S(1)} %add_add_fusion.after_ref.refs_1_), channel_id=1, source_target_pairs={{32,0},{9,1},{34,2},{11,3},{36,4},{13,5},{38,6},{15,7},{40,8},{17,... | collective-permute-start | bytes 1622024 | tf_op jit(solution)/shard_map/ppermute | solution.py:289
  29.9 0.3 collective-permute-start.8
  30.2 0.0 copy-start.4
  30.2 0.0 copy-start.5
  30.2 4.2 %load_patterns.1 = (bf16[128,128,128]{2,1,0:T(8,128)(2,1)S(1)}, s32[1,1]{1,0:T(1,128)}) custom-call(s32[128,128,128]{2,1,0:T(8,128)} %bitcast.53, s32[1056,128]{1,0:T(8,128)S(1)} %add_add_fusion.after_ref.refs_1_), custom_call_target="tpu_custom_call" | custom-call | tf_op jit(solution)/shard_map/load_patterns/pallas_call | solution.py:126
  34.4 0.0 copy-done.4
  34.4 1.3 %fusion.10 = (s32[]{:T(128)}, s32[128]{0:T(128)S(1)}) fusion(pred[]{:T(512)S(6)} %eq.176, s32[]{:T(128)S(6)} %select_n.443, s32[]{:T(128)S(6)} %select_n.438, s32[1,1,128]{2,1,0:T(1,128)S(1)} %copy-done.4, s32[]{:T(128)} %bitcast.3, pred[]{:T(512)S(6)} %eq.168, s32[]{:T(128)} %bitcast.49), kind=kLoop, calls=%fused_computation.90 | loop fusion | flops 12799 | bytes 1046 | tf_op jit(solution)/shard_map/reduce_sum | solution.py:311
  35.8 0.0 copy-done.5
  35.8 0.7 fusion
  36.5 0.6 pad_add_fusion.3
  37.1 0.1 pad.1.clone
  37.2 0.2 convert_reduce_fusion
  37.4 0.0 collective-permute-done.10.refs_2_
  37.4 3.9 %collective-permute-start.9 = (s32[1056,128]{1,0:T(8,128)S(1)}, s32[1056,128]{1,0:T(8,128)S(1)}, u32[]{:S(2)}, u32[]{:S(2)}) collective-permute-start(s32[1056,128]{1,0:T(8,128)S(1)} %add_add_fusion.after_ref.refs_1_), channel_id=1, source_target_pairs={{64,0},{17,1},{66,2},{19,3},{68,4},{21,5},{70,6},{23,7},{72,8},{25... | collective-permute-start | bytes 1622024 | tf_op jit(solution)/shard_map/ppermute | solution.py:289
  41.3 0.1 select_reduce_fusion
  41.5 0.1 pad_add_fusion.1.slots_ref
  41.5 0.0 collective-permute-done.11.refs_3_
  41.5 0.0 collective-permute-done.12.refs_4_
  41.5 4.5 %aggregate_early.1.refs_3_ = f32[16,128,256]{2,1,0:T(8,128)S(1)} custom-call(s32[5,128]{1,0:T(8,128)S(1)} %pad_add_fusion.1.slots_ref, bf16[128,128,128]{2,1,0:T(8,128)(2,1)S(1)} %get-tuple-element.14.pat, s32[1056,128]{1,0:T(8,128)S(1)} %pad_add_fusion.after_ref.refs_0_, s32[1056,128]{1,0:T(8,128)S(1)} %add_add_fusion.after_ref.refs_1_, ...), custom_call_target="tpu_custom_call" | custom-call | tf_op jit(solution)/shard_map/aggregate_early/pallas_call | solution.py:194
  46.1 0.0 copy-start
  46.1 0.0 copy-start.1
  46.1 0.0 copy-start.2
  46.1 0.0 copy-start.3
  46.1 0.0 collective-permute-done.7.refs_0_
  46.1 0.0 collective-permute-done.8.refs_1_
  46.1 5.9 %collective-permute-done.9.refs_2_ = s32[1056,128]{1,0:T(8,128)S(1)} collective-permute-done((s32[1056,128]{1,0:T(8,128)S(1)}, s32[1056,128]{1,0:T(8,128)S(1)}, u32[]{:S(2)}, u32[]{:S(2)}) %collective-permute-start.9) | collective-permute-done | bytes 540704 | tf_op jit(solution)/shard_map/ppermute | solution.py:289
  52.0 3.6 %aggregate_late.1 = (f32[8,128,256]{2,1,0:T(8,128)S(1)}, f32[8,128,256]{2,1,0:T(8,128)S(1)}) custom-call(s32[5,128]{1,0:T(8,128)S(1)} %pad_add_fusion.1.slots_ref, bf16[128,128,128]{2,1,0:T(8,128)(2,1)S(1)} %get-tuple-element.14.pat, s32[1056,128]{1,0:T(8,128)S(1)} %collective-permute-done.7.refs_0_, s32[1056,128]{1,0:T(8,128)S(1)} %collective-permute-done.8.refs_1_, ...), custom_call_target="tpu_custom_call" | custom-call | tf_op jit(solution)/shard_map/aggregate_late/pallas_call | solution.py:194
  55.7 0.1 collective-permute-start.13
  55.8 2.6 %collective-permute-done.13.other_ref = f32[8,128,256]{2,1,0:T(8,128)S(1)} collective-permute-done((f32[8,128,256]{2,1,0:T(8,128)S(1)}, f32[8,128,256]{2,1,0:T(8,128)S(1)}, u32[]{:S(2)}, u32[]{:S(2)}) %collective-permute-start.13) | collective-permute-done | bytes 1048608 | tf_op jit(solution)/shard_map/ppermute | solution.py:299
  58.4 0.4 add_pair.1
  58.8 2.3 %collective-permute-start.14 = (s32[264,128]{1,0:T(8,128)S(1)}, s32[264,128]{1,0:T(8,128)S(1)}, u32[]{:S(2)}, u32[]{:S(2)}) collective-permute-start(s32[264,128]{1,0:T(8,128)S(1)} %get-tuple-element.18), channel_id=1, source_target_pairs={{4,0},{5,1},{6,2},{7,3},{0,4},{1,5},{2,6},{3,7},{12,8},{13,9},{14,... | collective-permute-start | bytes 405512 | tf_op jit(solution)/shard_map/ppermute | solution.py:293
  61.1 1.7 %collective-permute-start.15 = (s32[264,128]{1,0:T(8,128)S(1)}, s32[264,128]{1,0:T(8,128)S(1)}, u32[]{:S(2)}, u32[]{:S(2)}) collective-permute-start(s32[264,128]{1,0:T(8,128)S(1)} %get-tuple-element.19), channel_id=1, source_target_pairs={{6,0},{7,1},{0,2},{1,3},{2,4},{3,5},{4,6},{5,7},{14,8},{15,9},{8,1... | collective-permute-start | bytes 405512 | tf_op jit(solution)/shard_map/ppermute | solution.py:293
  62.7 1.6 %collective-permute-start.16 = (s32[264,128]{1,0:T(8,128)S(1)}, s32[264,128]{1,0:T(8,128)S(1)}, u32[]{:S(2)}, u32[]{:S(2)}) collective-permute-start(s32[264,128]{1,0:T(8,128)S(1)} %get-tuple-element.20), channel_id=1, source_target_pairs={{2,0},{3,1},{4,2},{5,3},{6,4},{7,5},{0,6},{1,7},{10,8},{11,9},{12,... | collective-permute-start | bytes 405512 | tf_op jit(solution)/shard_map/ppermute | solution.py:293
  64.3 0.0 copy-done
  64.3 0.0 copy-done.1
  64.3 0.0 copy-done.2
  64.3 0.4 self_part.1.self_ref
  64.7 2.1 %collective-permute-done.14.refs_0_ = s32[264,128]{1,0:T(8,128)S(1)} collective-permute-done((s32[264,128]{1,0:T(8,128)S(1)}, s32[264,128]{1,0:T(8,128)S(1)}, u32[]{:S(2)}, u32[]{:S(2)}) %collective-permute-start.14) | collective-permute-done | bytes 135200 | tf_op jit(solution)/shard_map/ppermute | solution.py:293
  66.8 2.1 %collective-permute-done.15.refs_1_ = s32[264,128]{1,0:T(8,128)S(1)} collective-permute-done((s32[264,128]{1,0:T(8,128)S(1)}, s32[264,128]{1,0:T(8,128)S(1)}, u32[]{:S(2)}, u32[]{:S(2)}) %collective-permute-start.15) | collective-permute-done | bytes 135200 | tf_op jit(solution)/shard_map/ppermute | solution.py:293
  68.9 0.3 collective-permute-done.16.refs_2_
  69.2 0.0 copy-done.3
  69.2 0.9 %finish.1 = f32[256,256]{1,0:T(8,128)} custom-call(f32[256,256]{1,0:T(8,128)S(1)} %get-tuple-element.17.own_ref, f32[256,256]{1,0:T(8,128)S(1)} %self_part.1.self_ref, s32[2,128]{1,0:T(2,128)S(1)} %bitcast.52, s32[264,128]{1,0:T(8,128)S(1)} %collective-permute-done.14.refs_0_, s32[264,128]{1,0:T(8,128)S(1)} %collective-permute-done.15.refs_1_, ...), custom_call_target="tpu_custom_call" | custom-call | tf_op jit(solution)/shard_map/finish/pallas_call | solution.py:266
  (5 shorter events, 0.1 us)
Async XLA Ops:
  1.9 13.3 %collective-permute-start = (s32[264,128]{1,0:T(8,128)S(1)}, s32[264,128]{1,0:T(8,128)S(1)}, u32[]{:S(2)}, u32[]{:S(2)}) collective-permute-start(s32[264,128]{1,0:T(8,128)S(1)} %project.1), channel_id=1, source_target_pairs={{128,0},{136,8},{144,16},{152,24},{160,32},{168,40},{176,48},{184,... | collective-permute-start | bytes 405512 | tf_op jit(solution)/shard_map/ppermute | solution.py:276
  8.3 9.6 %collective-permute-start.4 = (s32[264,128]{1,0:T(8,128)S(1)}, s32[264,128]{1,0:T(8,128)S(1)}, u32[]{:S(2)}, u32[]{:S(2)}) collective-permute-start(s32[264,128]{1,0:T(8,128)S(1)} %project.1), channel_id=1, source_target_pairs={{8,0},{33,1},{10,2},{35,3},{12,4},{37,5},{14,6},{39,7},{16,8},{41,... | collective-permute-start | bytes 405512 | tf_op jit(solution)/shard_map/ppermute | solution.py:289
  11.0 9.2 %collective-permute-start.5 = (s32[264,128]{1,0:T(8,128)S(1)}, s32[264,128]{1,0:T(8,128)S(1)}, u32[]{:S(2)}, u32[]{:S(2)}) collective-permute-start(s32[264,128]{1,0:T(8,128)S(1)} %project.1), channel_id=1, source_target_pairs={{24,0},{225,1},{26,2},{227,3},{28,4},{229,5},{30,6},{231,7},{0,8},... | collective-permute-start | bytes 405512 | tf_op jit(solution)/shard_map/ppermute | solution.py:289
  11.0 9.2 %collective-permute-start.6 = (s32[264,128]{1,0:T(8,128)S(1)}, s32[264,128]{1,0:T(8,128)S(1)}, u32[]{:S(2)}, u32[]{:S(2)}) collective-permute-start(s32[264,128]{1,0:T(8,128)S(1)} %project.1), channel_id=1, source_target_pairs={{16,0},{65,1},{18,2},{67,3},{20,4},{69,5},{22,6},{71,7},{24,8},{73... | collective-permute-start | bytes 405512 | tf_op jit(solution)/shard_map/ppermute | solution.py:289
  15.1 8.8 %collective-permute-start.1 = (s32[264,128]{1,0:T(8,128)S(1)}, s32[264,128]{1,0:T(8,128)S(1)}, u32[]{:S(2)}, u32[]{:S(2)}) collective-permute-start(s32[264,128]{1,0:T(8,128)S(1)} %collective-permute-done), channel_id=1, source_target_pairs={{8,0},{33,1},{10,2},{35,3},{12,4},{37,5},{14,6},{39,7},{16,8},{41,... | collective-permute-start | bytes 405512 | tf_op jit(solution)/shard_map/ppermute | solution.py:289
  17.9 8.4 %collective-permute-start.2 = (s32[264,128]{1,0:T(8,128)S(1)}, s32[264,128]{1,0:T(8,128)S(1)}, u32[]{:S(2)}, u32[]{:S(2)}) collective-permute-start(s32[264,128]{1,0:T(8,128)S(1)} %collective-permute-done), channel_id=1, source_target_pairs={{24,0},{225,1},{26,2},{227,3},{28,4},{229,5},{30,6},{231,7},{0,8},... | collective-permute-start | bytes 405512 | tf_op jit(solution)/shard_map/ppermute | solution.py:289
  17.9 8.4 %collective-permute-start.3 = (s32[264,128]{1,0:T(8,128)S(1)}, s32[264,128]{1,0:T(8,128)S(1)}, u32[]{:S(2)}, u32[]{:S(2)}) collective-permute-start(s32[264,128]{1,0:T(8,128)S(1)} %collective-permute-done), channel_id=1, source_target_pairs={{16,0},{65,1},{18,2},{67,3},{20,4},{69,5},{22,6},{71,7},{24,8},{73... | collective-permute-start | bytes 405512 | tf_op jit(solution)/shard_map/ppermute | solution.py:289
  20.7 16.6 %collective-permute-start.10 = (s32[1056,128]{1,0:T(8,128)S(1)}, s32[1056,128]{1,0:T(8,128)S(1)}, u32[]{:S(2)}, u32[]{:S(2)}) collective-permute-start(s32[1056,128]{1,0:T(8,128)S(1)} %pad_add_fusion.after_ref.refs_0_), channel_id=1, source_target_pairs={{32,0},{9,1},{34,2},{11,3},{36,4},{13,5},{38,6},{15,7},{40,8},{17,... | collective-permute-start | bytes 1622024 | tf_op jit(solution)/shard_map/ppermute | solution.py:289
  20.7 20.8 %collective-permute-start.11 = (s32[1056,128]{1,0:T(8,128)S(1)}, s32[1056,128]{1,0:T(8,128)S(1)}, u32[]{:S(2)}, u32[]{:S(2)}) collective-permute-start(s32[1056,128]{1,0:T(8,128)S(1)} %pad_add_fusion.after_ref.refs_0_), channel_id=1, source_target_pairs={{224,0},{25,1},{226,2},{27,3},{228,4},{29,5},{230,6},{31,7},{232,8... | collective-permute-start | bytes 1622024 | tf_op jit(solution)/shard_map/ppermute | solution.py:289
  24.0 17.6 %collective-permute-start.12 = (s32[1056,128]{1,0:T(8,128)S(1)}, s32[1056,128]{1,0:T(8,128)S(1)}, u32[]{:S(2)}, u32[]{:S(2)}) collective-permute-start(s32[1056,128]{1,0:T(8,128)S(1)} %pad_add_fusion.after_ref.refs_0_), channel_id=1, source_target_pairs={{64,0},{17,1},{66,2},{19,3},{68,4},{21,5},{70,6},{23,7},{72,8},{25... | collective-permute-start | bytes 1622024 | tf_op jit(solution)/shard_map/ppermute | solution.py:289
  27.0 19.1 %collective-permute-start.7 = (s32[1056,128]{1,0:T(8,128)S(1)}, s32[1056,128]{1,0:T(8,128)S(1)}, u32[]{:S(2)}, u32[]{:S(2)}) collective-permute-start(s32[1056,128]{1,0:T(8,128)S(1)} %add_add_fusion.after_ref.refs_1_), channel_id=1, source_target_pairs={{32,0},{9,1},{34,2},{11,3},{36,4},{13,5},{38,6},{15,7},{40,8},{17,... | collective-permute-start | bytes 1622024 | tf_op jit(solution)/shard_map/ppermute | solution.py:289
  29.9 16.2 %collective-permute-start.8 = (s32[1056,128]{1,0:T(8,128)S(1)}, s32[1056,128]{1,0:T(8,128)S(1)}, u32[]{:S(2)}, u32[]{:S(2)}) collective-permute-start(s32[1056,128]{1,0:T(8,128)S(1)} %add_add_fusion.after_ref.refs_1_), channel_id=1, source_target_pairs={{224,0},{25,1},{226,2},{27,3},{228,4},{29,5},{230,6},{31,7},{232,8... | collective-permute-start | bytes 1622024 | tf_op jit(solution)/shard_map/ppermute | solution.py:289
  30.2 4.2 %copy-start.4 = (s32[1,1,128]{2,1,0:T(1,128)S(1)}, s32[1,1,128]{2,1,0:T(1,128)}, u32[]{:S(2)}) copy-start(s32[1,1,128]{2,1,0:T(1,128)} %param.12) | copy-start | bytes 1540
  30.2 5.5 %copy-start.5 = (s32[1,1,128]{2,1,0:T(1,128)S(1)}, s32[1,1,128]{2,1,0:T(1,128)}, u32[]{:S(2)}) copy-start(s32[1,1,128]{2,1,0:T(1,128)} %param.11) | copy-start | bytes 1540
  37.4 14.7 %collective-permute-start.9 = (s32[1056,128]{1,0:T(8,128)S(1)}, s32[1056,128]{1,0:T(8,128)S(1)}, u32[]{:S(2)}, u32[]{:S(2)}) collective-permute-start(s32[1056,128]{1,0:T(8,128)S(1)} %add_add_fusion.after_ref.refs_1_), channel_id=1, source_target_pairs={{64,0},{17,1},{66,2},{19,3},{68,4},{21,5},{70,6},{23,7},{72,8},{25... | collective-permute-start | bytes 1622024 | tf_op jit(solution)/shard_map/ppermute | solution.py:289
  46.1 18.2 %copy-start = (bf16[256,768]{1,0:T(8,128)(2,1)S(1)}, bf16[256,768]{1,0:T(8,128)(2,1)}, u32[]{:S(2)}) copy-start(bf16[256,768]{1,0:T(8,128)(2,1)} %x_ref.1) | copy-start | bytes 1179652
  46.1 18.2 %copy-start.1 = (f32[768,256]{1,0:T(8,128)S(1)}, f32[768,256]{1,0:T(8,128)}, u32[]{:S(2)}) copy-start(f32[768,256]{1,0:T(8,128)} %w_ref.1) | copy-start | bytes 2359300
  46.1 18.2 %copy-start.2 = (f32[256]{0:T(256)S(1)}, f32[256]{0:T(256)}, u32[]{:S(2)}) copy-start(f32[256]{0:T(256)} %param.17) | copy-start | bytes 3076
  46.1 23.1 %copy-start.3 = (s32[256]{0:T(256)S(1)}, s32[256]{0:T(256)}, u32[]{:S(2)}) copy-start(s32[256]{0:T(256)} %param.10) | copy-start | bytes 3076
  55.7 2.7 %collective-permute-start.13 = (f32[8,128,256]{2,1,0:T(8,128)S(1)}, f32[8,128,256]{2,1,0:T(8,128)S(1)}, u32[]{:S(2)}, u32[]{:S(2)}) collective-permute-start(f32[8,128,256]{2,1,0:T(8,128)S(1)} %get-tuple-element.16), channel_id=1, source_target_pairs={{1,0},{0,1},{3,2},{2,3},{5,4},{4,5},{7,6},{6,7},{9,8},{8,9},{11,10... | collective-permute-start | bytes 3145736 | tf_op jit(solution)/shard_map/ppermute | solution.py:299
  58.8 8.0 %collective-permute-start.14 = (s32[264,128]{1,0:T(8,128)S(1)}, s32[264,128]{1,0:T(8,128)S(1)}, u32[]{:S(2)}, u32[]{:S(2)}) collective-permute-start(s32[264,128]{1,0:T(8,128)S(1)} %get-tuple-element.18), channel_id=1, source_target_pairs={{4,0},{5,1},{6,2},{7,3},{0,4},{1,5},{2,6},{3,7},{12,8},{13,9},{14,... | collective-permute-start | bytes 405512 | tf_op jit(solution)/shard_map/ppermute | solution.py:293
  61.1 7.8 %collective-permute-start.15 = (s32[264,128]{1,0:T(8,128)S(1)}, s32[264,128]{1,0:T(8,128)S(1)}, u32[]{:S(2)}, u32[]{:S(2)}) collective-permute-start(s32[264,128]{1,0:T(8,128)S(1)} %get-tuple-element.19), channel_id=1, source_target_pairs={{6,0},{7,1},{0,2},{1,3},{2,4},{3,5},{4,6},{5,7},{14,8},{15,9},{8,1... | collective-permute-start | bytes 405512 | tf_op jit(solution)/shard_map/ppermute | solution.py:293
  62.7 6.5 %collective-permute-start.16 = (s32[264,128]{1,0:T(8,128)S(1)}, s32[264,128]{1,0:T(8,128)S(1)}, u32[]{:S(2)}, u32[]{:S(2)}) collective-permute-start(s32[264,128]{1,0:T(8,128)S(1)} %get-tuple-element.20), channel_id=1, source_target_pairs={{2,0},{3,1},{4,2},{5,3},{6,4},{7,5},{0,6},{1,7},{10,8},{11,9},{12,... | collective-permute-start | bytes 405512 | tf_op jit(solution)/shard_map/ppermute | solution.py:293
